TPU v7x, 32 devices: a whole 2x2x4 slice. The times are simulated.
32 devices in a mesh: tm: 4 (over z), row: 2 (over x), obs: 4 (over y, core).
Axes of the slice: x: 2, y: 2, z: 4, core: 2. Of those that a mesh axis runs over, the one named last changes fastest.
Arguments:
- dyn_pattern: int32 [8, 8, 3], P('tm'), may hold values from 0 to 7
- dyn_values: float32 [8, 1024, 384], P('tm', ('row', 'obs')), may hold values from -0.3125 to 0.3125
- offsets: float32 [8, 1024], P('tm', ('row', 'obs')), may hold values from -6 to 6
- covariance: float32 [8, 1024, 1024], P('tm', ('row', 'obs')), may hold values from -1 to 14, as said below
- obs_block: int32 [8, 128], P('tm'), may hold values from 0 to 7
- obs_matrix: float32 [8, 128, 256], P('tm', 'obs'), may hold values from -0.375 to 0.375
- obs_data: float32 [8, 128], P('tm', 'obs'), may hold values from -6 to 6
Outputs:
- scan_dynamics: float32 [4, 1024, 1024], P('tm', ('row', 'obs'))
- scan_offset: float32 [4, 1024], P('tm', ('row', 'obs'))
- scan_covariance: float32 [4, 1024, 1024], P('tm', ('row', 'obs'))
- scan_factor: float32 [4, 1024, 512], P('tm', ('row', 'obs'))
- scan_information: float32 [4, 1024], P('tm', ('row', 'obs'))
Inputs may be any that keep to these rules, and one draw needn't show every extreme that they name: `dyn_pattern`: each entry names a block column. `obs_block`: each entry names a state block. Each covariance is symmetric and positive definite.
All inputs are finite; a program needn't handle non-finite values.
Results may differ from a plain program's by a relative error of at most 0.00019.
Values sent between devices are 32-bit elements; how exact they have to be, the bound alone decides.
No kernel may reach another device: no remote copies, remote signals or barrier semaphores. Data moves between devices by JAX's collectives and lax.ppermute only.
A program may use at most 128 MiB of HBM per device.

v0:
```python
import jax
import jax.numpy as jnp
from jax import lax
from jax.sharding import PartitionSpec as P

largest_value = lax.Precision.HIGHEST


def shifted(block, axis, distance):
    devices = range(lax.axis_size(axis))
    route = [(i - distance, i) for i in devices if i - distance in devices]
    return lax.ppermute(block, axis, route)


def product(left, right):
    return jnp.dot(left, right, precision=largest_value, preferred_element_type=jnp.float32)


def lower_solve(lower, rhs):
    return lax.linalg.triangular_solve(lower, rhs, left_side=True, lower=True)


def assemble_dynamics(pattern, values):
    number_of_blocks = pattern.shape[0]
    per_row = pattern.shape[1]
    states = values.shape[0]
    block_extent = states // number_of_blocks
    indicator_matrix = (
        pattern[:, :, None] == jnp.arange(number_of_blocks, dtype=jnp.int32)[None, None, :]
    ).astype(jnp.float32)
    blocks = values.reshape(number_of_blocks, block_extent, per_row, block_extent)
    return jnp.einsum("ckd,cikj->cidj", indicator_matrix, blocks, precision=largest_value).reshape(
        states, states
    )


def assemble_factor(indices, matrix, number_of_blocks):
    item_count = matrix.shape[0]
    block_extent = matrix.shape[1] // 2
    reach = (indices[:, None] + jnp.arange(2, dtype=jnp.int32)[None, :]) % number_of_blocks
    indicator_matrix = (
        reach[:, :, None] == jnp.arange(number_of_blocks, dtype=jnp.int32)[None, None, :]
    ).astype(jnp.float32)
    piece_list = matrix.reshape(item_count, 2, block_extent)
    return jnp.einsum(
        "onr,onz->rzo", indicator_matrix, piece_list, precision=largest_value
    ).reshape(number_of_blocks * block_extent, item_count)


def combine(
    prior_dyn,
    prior_offsets,
    prior_cov,
    prior_factor,
    prior_zeta,
    own_dyn,
    own_offsets,
    own_cov,
    own_factor,
    own_zeta,
    row_start,
):
    panel_rows = prior_cov.shape[0]
    rank_width = own_factor.shape[1]
    own_pan = lax.dynamic_slice_in_dim(own_dyn, row_start, panel_rows, 0)
    gain_pan = product(prior_cov, own_factor)
    gain_rows = lax.all_gather(gain_pan, ("row", "obs"), axis=0, tiled=True)
    identity = jnp.eye(rank_width, dtype=jnp.float32)
    factor_pan = lax.dynamic_slice_in_dim(own_factor, row_start, panel_rows, 0)
    system = identity + lax.psum(product(factor_pan.T, gain_pan), ("row", "obs"))
    lower = jnp.linalg.cholesky(system)
    carried = product(own_dyn, gain_rows)
    observed = product(prior_dyn.T, own_factor)
    upper_part = lower_solve(lower, observed.T)
    weights = lower_solve(lower, carried.T).T
    weight_pan = lax.dynamic_slice_in_dim(weights, row_start, panel_rows, 0)
    spread_pan = product(prior_cov, own_dyn.T)
    moved = product(own_pan, lax.all_gather(spread_pan, ("row", "obs"), axis=0, tiled=True))
    new_dyn = product(own_pan, prior_dyn) - product(weight_pan, upper_part)
    new_cov = moved - product(weight_pan, weights.T) + own_cov
    residual = own_zeta - product(own_factor.T, prior_offsets)
    solved = lower_solve(lower, residual[:, None])[:, 0]
    new_offsets = product(own_pan, prior_offsets) + product(weight_pan, solved) + own_offsets
    upper_pan = lax.dynamic_slice_in_dim(upper_part, row_start, panel_rows, 1).T
    new_factor = jnp.concatenate([upper_pan, prior_factor], axis=1)
    new_zeta = jnp.concatenate([solved, prior_zeta])
    return (new_dyn, new_offsets, new_cov, new_factor, new_zeta)


def per_device(dyn_pattern, dyn_values, offsets, covariance, obs_block, obs_matrix, obs_data):
    panel_rows = covariance.shape[1]
    row_start = lax.axis_index(("row", "obs")) * panel_rows
    number_of_blocks = dyn_pattern.shape[1]
    obs_rows, obs_values = (
        lax.all_gather(obs_matrix, "obs", axis=1, tiled=True),
        lax.all_gather(obs_data, "obs", axis=1, tiled=True),
    )
    row_values, row_offsets = (
        lax.all_gather(dyn_values, ("row", "obs"), axis=1, tiled=True),
        lax.all_gather(offsets, ("row", "obs"), axis=1, tiled=True),
    )
    first_dyn = assemble_dynamics(dyn_pattern[0], row_values[0])
    second_dyn = assemble_dynamics(dyn_pattern[1], row_values[1])
    first_factor = assemble_factor(obs_block[0], obs_rows[0], number_of_blocks)
    second_factor = assemble_factor(obs_block[1], obs_rows[1], number_of_blocks)
    first_pan = lax.dynamic_slice_in_dim(first_factor, row_start, panel_rows, 0)
    dyn_pan, off_pan, cov_pan, fac_pan, zeta_full = combine(
        first_dyn,
        row_offsets[0],
        covariance[0],
        first_pan,
        obs_values[0],
        second_dyn,
        offsets[1],
        covariance[1],
        second_factor,
        obs_values[1],
        row_start,
    )
    later_pan, later_cov, later_off, later_fac, later_zeta = shifted(
        (dyn_pan, cov_pan, off_pan, fac_pan, zeta_full), "tm", -1
    )
    prior_full, later_full, later_factor, prior_offsets = (
        lax.all_gather(dyn_pan, ("row", "obs"), axis=0, tiled=True),
        lax.all_gather(later_pan, ("row", "obs"), axis=0, tiled=True),
        lax.all_gather(later_fac, ("row", "obs"), axis=0, tiled=True),
        lax.all_gather(off_pan, ("row", "obs"), axis=0, tiled=True),
    )
    top_dyn, top_off, top_cov, top_fac, top_zeta = combine(
        prior_full,
        prior_offsets,
        cov_pan,
        fac_pan,
        zeta_full,
        later_full,
        later_off,
        later_cov,
        later_factor,
        later_zeta,
        row_start,
    )
    even_turn = lax.axis_index("tm") % 2 == 0
    padded_fac = jnp.concatenate([fac_pan, jnp.zeros_like(fac_pan)], axis=1)
    padded_zeta = jnp.concatenate([zeta_full, jnp.zeros_like(zeta_full)])
    out_dyn = jnp.where(even_turn, top_dyn, dyn_pan)
    out_off = jnp.where(even_turn, top_off, off_pan)
    out_cov = jnp.where(even_turn, top_cov, cov_pan)
    out_fac = jnp.where(even_turn, top_fac, padded_fac)
    out_zeta = jnp.where(even_turn, top_zeta, padded_zeta)
    output_information = product(out_fac, out_zeta)
    return (out_dyn[None], out_off[None], out_cov[None], out_fac[None], output_information[None])


def solution(mesh):
    placed = (
        P("tm", None, None),
        P("tm", ("row", "obs"), None),
        P("tm", ("row", "obs")),
        P("tm", ("row", "obs"), None),
        P("tm", None),
        P("tm", "obs", None),
        P("tm", "obs"),
    )
    return jax.shard_map(
        per_device,
        mesh=mesh,
        in_specs=placed,
        out_specs=(
            P("tm", ("row", "obs"), None),
            P("tm", ("row", "obs")),
            P("tm", ("row", "obs"), None),
            P("tm", ("row", "obs"), None),
            P("tm", ("row", "obs")),
        ),
        check_vma=False,
    )
```

profile of v0, /device:TPU:0, one launch (start us, length us, event | category | flops | bytes accessed | tf_op | source)
XLA Modules:
  0.0 423.1 jit_solution(2578465447513517123)
XLA Ops:
  8.0 7.4 %all_gather.37 = f32[2,128,256]{2,1,0:T(8,128)S(1)} all-gather(f32[2,32,256]{2,1,0:T(8,128)} %param.16), channel_id=1, replica_groups=mesh['tm'=4,'row'=2,'obs'=4] {'obs'}, dimensions={1}, use_global_device_ids=true | all-gather | bytes 327680 | tf_op jit(solution)/shard_map/all_gather | solution.py:95
  20.2 24.8 %all-gather.10.cloned.1.call-done = f32[2,1024,384]{2,1,0:T(8,128)} async-done(((f32[2,128,384]{2,1,0:T(8,128)}), f32[2,1024,384]{2,1,0:T(8,128)}) %all-gather.10.cloned.1.call-update) | async-done | bytes 3145744 | tf_op jit(solution)/shard_map/all_gather | solution.py:99
  65.0 36.0 %all-reduce.4.cloned.1.call-done = f32[128,128]{1,0:T(8,128)} async-done(((f32[128,128]{1,0:T(8,128)}), f32[128,128]{1,0:T(8,128)}) %all-reduce.4.cloned.1.call-update) | async-done | bytes 65552 | tf_op jit(solution)/shard_map/psum | solution.py:70
  102.9 11.7 %cholesky.60 = f32[128,128]{1,0:T(8,128)S(1)} custom-call(f32[128,128]{1,0:T(8,128)S(1)} %fusion.81), custom_call_target="Cholesky" | custom-call | tf_op jit(solution)/shard_map/jit(cholesky)/cholesky | solution.py:71
  115.9 9.8 %custom-call.31 = f32[1,128,128]{1,2,0:T(8,128)S(1)} custom-call(f32[1,128,128]{2,1,0:T(8,128)S(1)} %fusion.68), custom_call_target="InvertDiagBlocksLowerTriangular" | custom-call | tf_op jit(solution)/shard_map/triangular_solve/custom-call.4 | solution.py:20
  139.5 5.6 %collective-permute-done.1 = f32[128,256]{0,1:T(8,128)S(1)} collective-permute-done((f32[128,256]{0,1:T(8,128)S(1)}, f32[128,256]{0,1:T(8,128)S(1)}, u32[]{:S(2)}, u32[]{:S(2)}) %collective-permute-start.1) | collective-permute-done | bytes 131104 | tf_op jit(solution)/shard_map/ppermute | solution.py:12
  145.8 11.9 %all_gather.38 = f32[1024,128]{0,1:T(8,128)S(1)} all-gather(f32[128,128]{0,1:T(8,128)S(1)} %bitcast.275), channel_id=1, replica_groups=mesh['tm'=4,'row'=2,'obs'=4] {'row','obs'}, dimensions={0}, use_global_device_ids=true | all-gather | bytes 589824 | tf_op jit(solution)/shard_map/all_gather | solution.py:67
  161.2 4.7 %fusion.136 = f32[128,1024]{1,0:T(8,128)S(1)} fusion(f32[1024,128]{0,1:T(8,128)S(1)} %all_gather.38, f32[128,8,8,128]{3,2,1,0:T(8,128)S(1)} %bitcast.262), kind=kOutput, calls=%fused_computation.200 | convolution fusion | flops 1610612736 | bytes 5242880 | tf_op jit(solution)/shard_map/dot_general | solution.py:16
  171.4 14.8 %collective-permute-done = f32[128,1024]{1,0:T(8,128)S(1)} collective-permute-done((f32[128,1024]{1,0:T(8,128)S(1)}, f32[128,1024]{1,0:T(8,128)S(1)}, u32[]{:S(2)}, u32[]{:S(2)}) %collective-permute-start) | collective-permute-done | bytes 524320 | tf_op jit(solution)/shard_map/ppermute | solution.py:12
  188.8 6.7 %fusion.11 = f32[128,1024]{1,0:T(8,128)S(1)} fusion(f32[128,1024]{1,0:T(8,128)S(1)} %fusion.100, f32[1024,1024]{0,1:T(8,128)} %all-gather.18.cloned.1.call-done, f32[2,128,1024]{2,1,0:T(8,128)S(1)} %copy-done.10, f32[1024,1024]{1,0:T(8,128)} %bitcast.270, s32[]{:T(128)S(6)} %select_n.93), kind=kOutput, calls=%fused_computation.21 | convolution fusion | flops 1610874880 | bytes 6291460 | tf_op jit(solution)/shard_map/dot_general | solution.py:16
  201.0 5.1 %all-gather = f32[4,32,2]{1,2,0:T(2,128)S(1)} all-gather(f32[1,32,2]{1,2,0:T(2,128)S(1)} %bitcast.286), channel_id=1, replica_groups=mesh['tm'=4,'row'=2,'obs'=4] {'obs'}, dimensions={0}, use_global_device_ids=true | all-gather | bytes 1280 | tf_op jit(solution)/shard_map/all_gather | solution.py:96
  206.1 8.4 %all_gather.44 = f32[2,1024]{1,0:T(2,128)S(1)} all-gather(f32[2,128]{1,0:T(2,128)S(1)} %copy-done.19), channel_id=1, replica_groups=mesh['tm'=4,'row'=2,'obs'=4] {'row','obs'}, dimensions={1}, use_global_device_ids=true | all-gather | bytes 9216 | tf_op jit(solution)/shard_map/all_gather | solution.py:100
  222.2 8.3 %all-gather.1 = f32[8,1,128]{2,1,0:T(1,128)S(1)} all-gather(f32[1,1,128]{2,1,0:T(1,128)} %bitcast.48), channel_id=1, replica_groups=mesh['tm'=4,'row'=2,'obs'=4] {'row','obs'}, dimensions={0}, use_global_device_ids=true | all-gather | bytes 4608 | tf_op jit(solution)/shard_map/all_gather | solution.py:127
  230.5 7.5 %fusion.144 = f32[128,1024]{1,0:T(8,128)} fusion(f32[128,1024]{1,0:T(8,128)S(1)} %fusion.11, f32[1024,1024]{1,0:T(8,128)} %all-gather.12.cloned.1.call-done), kind=kOutput, calls=%fused_computation.208 | convolution fusion | flops 1610612736 | bytes 5242880 | tf_op jit(solution)/shard_map/dot_general | solution.py:16
  240.4 21.8 %all-gather.14.cloned.1.call-done = f32[1024,1024]{1,0:T(8,128)} async-done(((f32[128,1024]{1,0:T(8,128)}), f32[1024,1024]{1,0:T(8,128)}) %all-gather.14.cloned.1.call-update) | async-done | bytes 4194320 | tf_op jit(solution)/shard_map/all_gather | solution.py:124
  262.2 5.7 %fusion.143 = f32[256,1024]{1,0:T(8,128)S(1)} fusion(f32[1024,256]{0,1:T(8,128)S(1)} %copy-done.5, f32[1024,1024]{1,0:T(8,128)} %all-gather.14.cloned.1.call-done), kind=kOutput, calls=%fused_computation.207 | convolution fusion | flops 3221225472 | bytes 6291456 | tf_op jit(solution)/shard_map/dot_general | solution.py:16
  268.0 51.8 %all-reduce.6.cloned.1.call-done = f32[256,256]{0,1:T(8,128)} async-done(((f32[256,256]{0,1:T(8,128)}), f32[256,256]{0,1:T(8,128)}) %all-reduce.6.cloned.1.call-update) | async-done | bytes 262160 | tf_op jit(solution)/shard_map/psum | solution.py:70
  321.8 11.7 %cholesky.115 = f32[128,128]{1,0:T(8,128)S(1)} custom-call(f32[128,128]{1,0:T(8,128)S(1)} %cholesky.141), custom_call_target="Cholesky" | custom-call | tf_op jit(solution)/shard_map/jit(cholesky)/cholesky | solution.py:71
  333.6 9.8 %custom-call.26 = f32[1,128,128]{1,2,0:T(8,128)S(1)} custom-call(f32[1,128,128]{2,1,0:T(8,128)S(1)} %get-tuple-element.67), custom_call_target="InvertDiagBlocksLowerTriangular" | custom-call | tf_op jit(solution)/shard_map/jit(cholesky)/cholesky | solution.py:71
  343.9 11.7 %cholesky.128 = f32[128,128]{1,0:T(8,128)S(1)} custom-call(f32[128,128]{1,0:T(8,128)S(1)} %convolution_subtract_fusion.3), custom_call_target="Cholesky" | custom-call | tf_op jit(solution)/shard_map/jit(cholesky)/cholesky | solution.py:71
  363.7 20.7 %custom-call.33 = f32[2,128,128]{1,2,0:T(8,128)S(1)} custom-call(f32[2,128,128]{2,1,0:T(8,128)} %copy-done.25), custom_call_target="InvertDiagBlocksLowerTriangular" | custom-call | tf_op jit(solution)/shard_map/triangular_solve/custom-call.5 | solution.py:20
  391.2 9.2 %fusion.142 = f32[256,1024]{1,0:T(8,128)S(1)} fusion(f32[1024,256]{1,0:T(8,128)} %all-gather.20.cloned.1.call-done, f32[1024,1024]{1,0:T(8,128)} %all-gather.12.cloned.1.call-done), kind=kOutput, calls=%fused_computation.206 | convolution fusion | flops 3221225472 | bytes 6291456 | tf_op jit(solution)/shard_map/dot_general | solution.py:16
  406.1 4.3 %fusion.10 = f32[1,128,1024]{2,1,0:T(8,128)} fusion(f32[128,1024]{1,0:T(8,128)S(1)} %copy-done.8, f32[128,1024]{1,0:T(8,128)S(1)} %fusion.23, f32[1024,1024]{1,0:T(8,128)S(1)} %copy-done.4, f32[1024,1024]{1,0:T(8,128)} %all-gather.12.cloned.1.call-done, s32[]{:T(128)S(6)} %select_n.93, pred[]{:T(512)S(6)} %eq.68), kind=kOutput, calls=%fused_computation.20 | convolution fusion | flops 1610874880 | bytes 6291461 | tf_op jit(solution)/shard_map/dot_general | solution.py:16
  410.4 5.7 %fusion.14 = f32[1,128,1024]{2,1,0:T(8,128)} fusion(f32[128,1024]{1,0:T(8,128)S(1)} %fusion.11, f32[128,1024]{1,0:T(8,128)} %collective-permute-done.4, f32[128,1024]{1,0:T(8,128)S(1)} %fusion.24, f32[1024,1024]{1,0:T(8,128)} %all-gather.22.cloned.1.call-done, f32[1024,1024]{1,0:T(8,128)} %all-gather.12.cloned.1.call-done, s32[]{:T(128)S(6)} %select_n.93, ...), kind=kOutput, calls=%fused_computation.24 | convolution fusion | flops 1611005952 | bytes 6815749 | tf_op jit(solution)/shard_map/dot_general | solution.py:16
  (175 shorter events, 95.6 us)
Async XLA Ops:
  7.2 12.9 %copy-start.20 = (s32[2,8,3]{1,0,2:T(2,128)S(1)}, s32[2,8,3]{1,0,2:T(2,128)}, u32[]{:S(2)}) copy-start(s32[2,8,3]{1,0,2:T(2,128)} %param.11) | copy-start | bytes 580
  7.2 37.8 %all-gather.10.cloned.1.call-start = ((), (), s32[]{:S(2)}) async-start(), calls=%async_computation | async-start | bytes 3538944 | tf_op jit(solution)/shard_map/all_gather | solution.py:99
  7.9 93.2 %all-reduce.4.cloned.1.call-start = ((), (), s32[]{:S(2)}) async-start(), calls=%async_computation.1 | async-start | bytes 131072 | tf_op jit(solution)/shard_map/psum | solution.py:70
  20.0 168.8 %all-gather.18.cloned.1.call-start = ((), (), s32[]{:S(2)}) async-start(), calls=%async_computation.5 | async-start | bytes 4718592 | tf_op jit(solution)/shard_map/all_gather | solution.py:78
  62.4 133.1 %all-gather.16.cloned.1.call-start = ((), (), s32[]{:S(2)}) async-start(), calls=%async_computation.4 | async-start | bytes 1179648 | tf_op jit(solution)/shard_map/all_gather | solution.py:126
  65.0 73.2 %copy-start.15 = (f32[128,128]{0,1:T(8,128)}, f32[128,128]{0,1:T(8,128)S(1)}, u32[]{:S(2)}) copy-start(f32[128,128]{0,1:T(8,128)S(1)} %constant_dynamic-slice_fusion.1) | copy-start | bytes 196612
  138.2 22.9 %copy-start.14 = (f32[128,128]{0,1:T(8,128)}, f32[128,128]{0,1:T(8,128)S(1)}, u32[]{:S(2)}) copy-start(f32[128,128]{0,1:T(8,128)S(1)} %get-tuple-element.61) | copy-start | bytes 196612
  138.2 6.9 %collective-permute-start.1 = (f32[128,256]{0,1:T(8,128)S(1)}, f32[128,256]{0,1:T(8,128)S(1)}, u32[]{:S(2)}, u32[]{:S(2)}) collective-permute-start(f32[128,256]{0,1:T(8,128)S(1)} %pad_maximum_fusion.4), channel_id=1, source_target_pairs={{8,0},{16,8},{24,16},{9,1},{17,9},{25,17},{10,2},{18,10},{26,18},{... | collective-permute-start | bytes 393224 | tf_op jit(solution)/shard_map/ppermute | solution.py:12
  145.7 84.7 %all-gather.12.cloned.1.call-start = ((), (), s32[]{:S(2)}) async-start(), calls=%async_computation.2 | async-start | bytes 4718592 | tf_op jit(solution)/shard_map/all_gather | solution.py:125
  167.1 21.7 %copy-start.10 = (f32[2,128,1024]{2,1,0:T(8,128)S(1)}, f32[2,128,1024]{2,1,0:T(8,128)}, u32[]{:S(2)}) copy-start(f32[2,128,1024]{2,1,0:T(8,128)} %param.14) | copy-start | bytes 3145732
  170.1 17.0 %copy-start.7 = (f32[128,1024]{1,0:T(8,128)}, f32[128,1024]{1,0:T(8,128)S(1)}, u32[]{:S(2)}) copy-start(f32[128,1024]{1,0:T(8,128)S(1)} %fusion.6) | copy-start | bytes 1572868
  170.1 16.1 %collective-permute-start = (f32[128,1024]{1,0:T(8,128)S(1)}, f32[128,1024]{1,0:T(8,128)S(1)}, u32[]{:S(2)}, u32[]{:S(2)}) collective-permute-start(f32[128,1024]{1,0:T(8,128)S(1)} %fusion.6), channel_id=1, source_target_pairs={{8,0},{16,8},{24,16},{9,1},{17,9},{25,17},{10,2},{18,10},{26,18},{... | collective-permute-start | bytes 1572872 | tf_op jit(solution)/shard_map/ppermute | solution.py:12
  187.0 75.2 %all-gather.14.cloned.1.call-start = ((), (), s32[]{:S(2)}) async-start(), calls=%async_computation.3 | async-start | bytes 4718592 | tf_op jit(solution)/shard_map/all_gather | solution.py:124
  187.6 132.1 %all-reduce.6.cloned.1.call-start = ((), (), s32[]{:S(2)}) async-start(), calls=%async_computation.6 | async-start | bytes 524288 | tf_op jit(solution)/shard_map/psum | solution.py:70
  188.7 12.3 %copy-start.24 = (f32[2,32]{1,0:T(2,128)S(1)}, f32[2,32]{1,0:T(2,128)}, u32[]{:S(2)}) copy-start(f32[2,32]{1,0:T(2,128)} %param.17) | copy-start | bytes 772
  188.7 17.4 %copy-start.19 = (f32[2,128]{1,0:T(2,128)S(1)}, f32[2,128]{1,0:T(2,128)}, u32[]{:S(2)}) copy-start(f32[2,128]{1,0:T(2,128)} %param.13) | copy-start | bytes 3076
  198.0 40.0 %copy-start.5 = (f32[1024,256]{0,1:T(8,128)S(1)}, f32[1024,256]{0,1:T(8,128)}, u32[]{:S(2)}) copy-start(f32[1024,256]{0,1:T(8,128)} %all-gather.16.cloned.1.call-done) | copy-start | bytes 3145732
  200.1 191.0 %all-gather.20.cloned.1.call-start = ((), (), s32[]{:S(2)}) async-start(), calls=%async_computation.7 | async-start | bytes 1179648 | tf_op jit(solution)/shard_map/all_gather | solution.py:67
  200.9 209.5 %all-gather.22.cloned.1.call-start = ((), (), s32[]{:S(2)}) async-start(), calls=%async_computation.8 | async-start | bytes 4718592 | tf_op jit(solution)/shard_map/all_gather | solution.py:78
  217.2 50.8 %copy-start.22 = (f32[128]{0:T(128)}, f32[128]{0:T(128)S(1)}, u32[]{:S(2)}) copy-start(f32[128]{0:T(128)S(1)} %slice_bitcast_fusion.11) | copy-start | bytes 1540
  217.4 21.6 %collective-permute-start.2 = (f32[256]{0:T(256)S(1)}, f32[256]{0:T(256)S(1)}, u32[]{:S(2)}, u32[]{:S(2)}) collective-permute-start(f32[256]{0:T(256)S(1)} %pad_maximum_fusion.5), channel_id=1, source_target_pairs={{8,0},{16,8},{24,16},{9,1},{17,9},{25,17},{10,2},{18,10},{26,18},{... | collective-permute-start | bytes 3080 | tf_op jit(solution)/shard_map/ppermute | solution.py:12
  220.9 181.6 %collective-permute-start.3 = (f32[128]{0:T(128)}, f32[128]{0:T(128)}, u32[]{:S(2)}, u32[]{:S(2)}) collective-permute-start(f32[128]{0:T(128)} %fusion.16), channel_id=1, source_target_pairs={{8,0},{16,8},{24,16},{9,1},{17,9},{25,17},{10,2},{18,10},{26,18},{... | collective-permute-start | bytes 1544 | tf_op jit(solution)/shard_map/ppermute | solution.py:12
  239.0 171.4 %collective-permute-start.4 = (f32[128,1024]{1,0:T(8,128)S(1)}, f32[128,1024]{1,0:T(8,128)}, u32[]{:S(2)}, u32[]{:S(2)}) collective-permute-start(f32[128,1024]{1,0:T(8,128)S(1)} %fusion.11), channel_id=1, source_target_pairs={{8,0},{16,8},{24,16},{9,1},{17,9},{25,17},{10,2},{18,10},{26,18},{... | collective-permute-start | bytes 1572872 | tf_op jit(solution)/shard_map/ppermute | solution.py:12
  319.7 65.2 %copy-start.23 = (f32[128]{0:T(128)S(1)}, f32[128]{0:T(128)}, u32[]{:S(2)}) copy-start(f32[128]{0:T(128)} %copy-done.22) | copy-start | bytes 1540
  (16 other events, 60.9 us)
Sparse Core Ops, SparseCore 0:
  9.9 35.0 all-gather.9
  48.6 52.4 all-reduce.3
  103.7 37.0 all-gather.17
  145.9 22.1 all-gather.15
  187.2 35.8 all-gather.11
  225.5 36.6 all-gather.13
  266.1 53.5 all-reduce.5
  322.2 23.3 all-gather.19
  347.5 36.9 all-gather.21
where the time goes:
time: 431 us; the launch traced here: 423 us
  waiting for transfers between devices  157 us (36%)
  matrix products  88.1 us (20%)
  other arithmetic  84.3 us (20%)
  blocking collectives  41.1 us (10%)
  local copies, waits for them, and re-layouts  28.5 us (7%)
  between operations  16.3 us (4%)
  starting transfers between devices  7.91 us (2%)
    psum x2, waiting for transfers between devices, combine(): lax.psum(product(factor_pan.T, gain_pan), ('row', 'obs'))  87.8 us
    dot_general x25, matrix products, product(): jnp.dot(left, right, precision=largest_value, preferred_element_type=jnp....  71.6 us
    another operation x10, other arithmetic, combine(): lower = jnp.linalg.cholesky(system)  47 us
    another operation x8, other arithmetic, lower_solve(): return lax.linalg.triangular_solve(lower, rhs, left_side=True, lower=True)  31.8 us
    all_gather x1, waiting for transfers between devices, per_device(): lax.all_gather(dyn_values, ('row', 'obs'), axis=1, tiled=True)  24.8 us
    all_gather x1, waiting for transfers between devices, per_device(): lax.all_gather(dyn_pan, ('row', 'obs'), axis=0, tiled=True)  21.8 us
    ppermute x5, waiting for transfers between devices, shifted(): return lax.ppermute(block, axis, route)  20.3 us
    all_gather x1, blocking collectives, combine(): gain_rows = lax.all_gather(gain_pan, ('row', 'obs'), axis=0, tiled=True)  11.9 us
  transfers between devices with their start and end apart: 14, of which 6 were waited for; matrix products, arithmetic and copies ran while one was open for 44% of the time, Pallas kernels for 0%

commit v1 on v0

v1 whole, which is shorter than its diff:
```python
import jax
import jax.numpy as jnp
from jax import lax
from jax.experimental import pallas as pl
from jax.experimental.pallas import tpu as pltpu
from jax.sharding import PartitionSpec as P

F32 = jnp.float32
BF16 = jnp.bfloat16
NN = (((1,), (0,)), ((), ()))
NT = (((1,), (1,)), ((), ()))
PLANE = ("row", "obs")
SMALL = 8


def split(x):
    high = x.astype(BF16)
    return high, (x - high.astype(F32)).astype(BF16)


def dot3(left, right, dims):
    def one(a, b):
        return lax.dot_general(a, b, dims, preferred_element_type=F32)

    return one(left[0], right[0]) + (one(left[0], right[1]) + one(left[1], right[0]))


def mm(left, right, dims=NN):
    return dot3(split(left), split(right), dims)


def reciprocal(x):
    y = pl.reciprocal(x, approx=True)
    return y * (2.0 - x * y)


def inverse_root(x):
    y = lax.rsqrt(x)
    return y * (1.5 - (0.5 * x) * (y * y))


def inverse_factor(matrix):
    size = matrix.shape[0]
    tiles = size // 8
    sub = lax.broadcasted_iota(jnp.int32, (8, size), 0)
    lane = lax.broadcasted_iota(jnp.int32, (8, size), 1)

    def wide(x):
        return jnp.broadcast_to(x, (8, size))

    rows = [matrix[8 * t : 8 * t + 8, :] for t in range(tiles)]
    inverse = [jnp.where(lane == sub + 8 * t, 1.0, 0.0).astype(F32) for t in range(tiles)]
    for p in range(tiles):
        column = {
            (t, c): wide(rows[t][:, 8 * p + c : 8 * p + c + 1])
            for t in range(p, tiles)
            for c in range(8)
        }
        scale = None
        for r in range(8):
            pivot = wide(column[p, r][r : r + 1, :])
            over = reciprocal(pivot)
            root = inverse_root(pivot)
            scale = root if r == 0 else jnp.where(sub == r, root, scale)
            factor = {t: column[t, r] * over for t in range(p, tiles)}
            for c in range(r + 1, 8):
                other = wide(column[p, r][c : c + 1, :])
                for t in range(p, tiles):
                    column[t, c] = column[t, c] - factor[t] * other
            factor[p] = jnp.where(sub > r, factor[p], 0.0)
            row_here = wide(rows[p][r : r + 1, :])
            inverse_here = wide(inverse[p][r : r + 1, :])
            for t in range(p, tiles):
                rows[t] = rows[t] - factor[t] * row_here
                inverse[t] = inverse[t] - factor[t] * inverse_here
        inverse[p] = inverse[p] * scale
    return jnp.concatenate(inverse, axis=0)


def identity(size):
    sub = lax.broadcasted_iota(jnp.int32, (size, size), 0)
    lane = lax.broadcasted_iota(jnp.int32, (size, size), 1)
    return jnp.where(sub == lane, 1.0, 0.0).astype(F32)


def dense_factor(matrix, blocks, number):
    items, width = matrix.shape[0], matrix.shape[1] // 2
    at = jnp.transpose(jnp.broadcast_to(blocks.astype(F32), (width, items)))
    pieces = []
    for r in range(number):
        first = jnp.where(at == float(r), matrix[:, :width], 0.0)
        second = jnp.where(at == float((r - 1) % number), matrix[:, width:], 0.0)
        pieces.append(first + second)
    return jnp.concatenate(pieces, axis=1)


def call(body, name, out_shapes, args, specs, scratch=(), flops=0, out_specs=None):
    whole = pl.BlockSpec(memory_space=pltpu.VMEM)
    return pl.pallas_call(
        body,
        name=name,
        grid=(1,),
        in_specs=specs,
        out_specs=out_specs or [whole] * len(out_shapes),
        out_shape=[jax.ShapeDtypeStruct(s, F32) for s in out_shapes],
        scratch_shapes=list(scratch),
        compiler_params=pltpu.CompilerParams(vmem_limit_bytes=56 * 2**20),
        cost_estimate=pl.CostEstimate(flops=flops, bytes_accessed=2**20, transcendentals=0),
    )(*args)


VM = pl.BlockSpec(memory_space=pltpu.VMEM)
SM = pl.BlockSpec(memory_space=pltpu.SMEM)


def element(shape, which):
    return pl.BlockSpec((1,) + tuple(shape[1:]), lambda i: (which,) + (0,) * (len(shape) - 1))


class Plan:
    def __init__(self, mesh, pattern, values, obs_block, obs_matrix):
        self.row, self.obs = mesh.shape["row"], mesh.shape["obs"]
        self.tm = mesh.shape["tm"]
        self.n = self.row * self.obs
        self.number, self.per_row = pattern.shape[1:]
        self.panel = values.shape[1]
        self.states = self.panel * self.n
        self.width = self.states // self.number
        self.items = obs_block.shape[1]
        self.share = obs_matrix.shape[1]
        self.swapped = self.n == 8 and self.panel % 128 == 0

    def source(self, info, k):
        return lax.bitwise_xor(info[0], k) if self.swapped else k

    def rows_of(self, info, k):
        start = self.source(info, k) * self.panel
        return pl.ds(pl.multiple_of(start, self.panel) if self.swapped else start, self.panel)


def exchange(x, axes, mask, size):
    return lax.ppermute(x, axes, [(a, a ^ mask) for a in range(size)])


def gather(plan, x):
    if plan.swapped:
        even = jnp.stack([x] + [exchange(x, PLANE, k, plan.n) for k in (2, 4, 6)])
        return even, exchange(even, PLANE, 1, plan.n)
    everything = lax.all_gather(x, PLANE, axis=0)
    return everything[0::2], everything[1::2]


def swap_blocks(plan, x):
    return lax.all_to_all(x, PLANE, 0, 0, tiled=True)


def earlier(plan, x):
    return lax.ppermute(x, "tm", [(i, i - 1) for i in range(1, plan.tm)])


def gain_step(plan, info, ints, pieces, covariance, offsets, data):
    share, panel, items = plan.share, plan.panel, plan.items

    def body(info, ints, *refs):
        parts = refs[: plan.obs]
        cov, off, dat, message, obs = refs[plan.obs :]
        for k, part in enumerate(parts):
            start = pl.multiple_of(lax.bitwise_xor(info[1], k) * share, share)
            obs[:, pl.ds(start, share), :] = part[...]
        factor = dense_factor(obs[1], ints[1:2, :items], plan.number)
        message[:panel, :] = mm(cov[0], factor, NT)
        message[panel:, :] = jnp.zeros((SMALL, items), F32)
        message[panel : panel + 2, :panel] = off[...]
        spread = jnp.concatenate([dat[...], jnp.zeros((2, items - share), F32)], axis=1)
        spread = jnp.concatenate([spread, jnp.zeros((6, items), F32)], axis=0)
        message[panel + 2 : panel + 4, :] = pltpu.roll(spread, info[1] * share, 1)[:2]

    return call(
        body,
        "gain",
        [(panel + SMALL, items), (2, items, 2 * plan.width)],
        (info, ints, *pieces, covariance, offsets, data),
        [SM, VM] + [VM] * plan.obs + [element(covariance.shape, 0), VM, VM],
        flops=2**27,
    )


def system_step(plan, info, ints, even, odd, obs):
    states, items, panel = plan.states, plan.items, plan.panel

    def body(info, ints, even, odd, obs, pack):
        tail = states + items
        zeta = jnp.zeros((2, items), F32)
        pack[tail:, :] = jnp.zeros((SMALL * plan.number, items), F32)
        for k in range(plan.n):
            piece = (even, odd)[k % 2]
            pack[plan.rows_of(info, k), :] = piece[k // 2, :panel, :]
            start = plan.source(info, k) * panel
            if plan.swapped:
                block = start // plan.width
                at = pl.multiple_of(tail + block * SMALL, SMALL)
                pack[pl.ds(at, 2), :] = piece[k // 2, panel : panel + 2, :]
            else:
                at = tail + start // plan.width * SMALL
                lane = start % plan.width
                pack[at : at + 2, lane : lane + panel] = piece[k // 2, panel : panel + 2, :panel]
            if k < plan.obs:
                zeta = zeta + piece[k // 2, panel + 2 : panel + 4, :]
        pack[tail + 2 : tail + 4, :] = zeta
        factor = dense_factor(obs[0], ints[1:2, :items], plan.number)
        system = identity(items) + mm(factor, pack[:states, :])
        pack[states:tail, :] = inverse_factor(system)

    return call(
        body,
        "system",
        [(states + items + SMALL * plan.number, items)],
        (info, ints, even, odd, obs),
        [SM, VM, VM, VM, element(obs.shape, 1)],
        flops=2**30,
    )[0]


def spread_step(plan, info, ints, even, odd, covariance):
    states, panel, width = plan.states, plan.panel, plan.width
    wide = plan.per_row * width

    def body(info, ints, even, odd, cov, out, values):
        for k in range(plan.n):
            values[:, plan.rows_of(info, k), :] = (even, odd)[k % 2][k // 2]
        for c in range(plan.number):
            taken = [
                cov[0, :, pl.ds(pl.multiple_of(ints[1, plan.items + c * plan.per_row + k] * width, width), width)]
                for k in range(plan.per_row)
            ]
            out[c * width : (c + 1) * width, :] = mm(
                values[1, c * width : (c + 1) * width, :], jnp.concatenate(taken, axis=1), NT
            )

    return call(
        body,
        "spread",
        [(states, panel), (2, states, wide)],
        (info, ints, even, odd, covariance),
        [SM, SM, VM, VM, element(covariance.shape, 0)],
        flops=2**28,
    )


def assemble_step(plan, info, even, odd):
    states = plan.states
    wide = plan.per_row * plan.width

    def body(info, even, odd, values):
        for k in range(plan.n):
            values[:, plan.rows_of(info, k), :] = (even, odd)[k % 2][k // 2]

    return call(body, "assemble", [(2, states, wide)], (info, even, odd), [SM, VM, VM])[0]


def level_step(plan, ints, values, pack, obs):
    states, items, width, number, per_row = (
        plan.states,
        plan.items,
        plan.width,
        plan.number,
        plan.per_row,
    )
    tail = states + items

    def body(ints, ints_v, values, pack, obs, dyn, weights, upper, small, dense, high, low, up_h, up_l):
        def block(e, c, k):
            return pl.multiple_of(ints[e, items + c * per_row + k] * width, width)

        def rows(c):
            return pl.ds(pl.multiple_of(c * width, width), width)

        def build(c, carry):
            dense[...] = jnp.zeros_like(dense)
            for k in range(per_row):
                at = pl.ds(block(0, c, k), width)
                dense[:, at] = dense[:, at] + values[0, rows(c), k * width : (k + 1) * width]
            high[rows(c), :], low[rows(c), :] = split(dense[...])
            return carry

        lax.fori_loop(0, number, build, 0)
        inverse = pack[states:tail, :]
        factor = dense_factor(obs[1], ints_v[1:2, :items], number)
        factor_pair = split(factor)
        inverse_pair = split(inverse)
        tile = min(256, states)

        def raise_tile(j, carry):
            at = pl.ds(pl.multiple_of(j * tile, tile), tile)
            seen = dot3(factor_pair, (high[:, at], low[:, at]), NN)
            part = dot3(inverse_pair, split(seen), NN)
            upper[:, at] = part
            up_h[:, at], up_l[:, at] = split(part)
            return carry

        lax.fori_loop(0, states // tile, raise_tile, 0)
        vector = jnp.concatenate(
            [pack[tail + c * SMALL : tail + (c + 1) * SMALL, :] for c in range(number)], axis=1
        )
        zeta = pack[tail : tail + SMALL, :]
        residual = zeta[3:4, :] - mm(vector, factor, NT)[0:1, :]
        solved = mm(jnp.broadcast_to(residual, (SMALL, items)), inverse, NT)
        solved_pair = split(solved)
        small[...] = jnp.zeros_like(small)
        small[1:2, :items] = solved[0:1, :]
        small[2:3, :items] = zeta[2:3, :]

        def combine(c, carry):
            own = values[1, rows(c), :]
            own_pair = split(own)
            starts = [block(1, c, k) for k in range(per_row)]
            gains = jnp.concatenate([pack[pl.ds(s, width), :] for s in starts], axis=0)
            carried = dot3(own_pair, split(gains), NN)
            weight = dot3(split(carried), inverse_pair, NT)
            weights[rows(c), :] = weight
            weight_pair = split(weight)
            left = tuple(jnp.concatenate([a, -b], axis=1) for a, b in zip(own_pair, weight_pair))
            right = tuple(
                jnp.concatenate([a[pl.ds(s, width), :] for s in starts] + [b[...]], axis=0)
                for a, b in ((high, up_h), (low, up_l))
            )
            dyn[rows(c), :] = dot3(left, right, NN)
            taken = jnp.concatenate(
                [
                    pack[pl.ds(pl.multiple_of(tail + ints[1, items + c * per_row + k] * SMALL, SMALL), SMALL), :]
                    for k in range(per_row)
                ],
                axis=1,
            )
            moved = dot3(split(taken), own_pair, NT) + dot3(solved_pair, weight_pair, NT)
            own_offset = pack[pl.ds(pl.multiple_of(tail + c * SMALL, SMALL), SMALL), :]
            small[0:1, pl.ds(pl.multiple_of(c * width, width), width)] = moved[0:1, :] + own_offset[1:2, :]
            return carry

        lax.fori_loop(0, number, combine, 0)

    return call(
        body,
        "level",
        [(states, states), (states, items), (items, states), (SMALL, states)],
        (ints, ints, values, pack, obs),
        [SM, VM, VM, VM, VM],
        scratch=[
            pltpu.VMEM((width, states), F32),
            pltpu.VMEM((states, states), BF16),
            pltpu.VMEM((states, states), BF16),
            pltpu.VMEM((items, states), BF16),
            pltpu.VMEM((items, states), BF16),
        ],
        flops=2**32,
    )


def covariance_step(plan, info, ints, moved, values, weights, covariance):
    states, panel, width, items = plan.states, plan.panel, plan.width, plan.items

    def body(info, ints, moved, values, weights, cov, out, held):
        for a in range(plan.n):
            held[:, a * panel : (a + 1) * panel] = moved[a]
        own = weights[pl.ds(pl.multiple_of(info[0] * panel, panel), panel), :]
        for c in range(plan.number):
            taken = [
                held[:, pl.ds(pl.multiple_of(ints[1, items + c * plan.per_row + k] * width, width), width)]
                for k in range(plan.per_row)
            ]
            at = slice(c * width, (c + 1) * width)
            left = jnp.concatenate(taken + [-own], axis=1)
            right = jnp.concatenate([values[0, at, :], weights[at, :]], axis=1)
            out[:, at] = mm(left, right, NT) + cov[0, :, at]

    return call(
        body,
        "covariance",
        [(panel, states)],
        (info, ints, moved, values, weights, covariance),
        [SM, SM, VM, element(values.shape, 1), VM, element(covariance.shape, 1)],
        scratch=[pltpu.VMEM((panel, states), F32)],
        flops=2**28,
    )[0]


def later_gain_step(plan, ints, cov, upper, obs):
    items = plan.items

    def body(ints, cov, upper, obs, out):
        factor = jnp.concatenate([upper[...], dense_factor(obs[0], ints[0:1, :items], plan.number)], axis=0)
        out[...] = mm(cov[...], factor, NT)

    return call(
        body,
        "later_gain",
        [(plan.panel, 2 * items)],
        (ints, cov, upper, obs),
        [VM, VM, VM, element(obs.shape, 0)],
        flops=2**28,
    )[0]


def later_spread_step(plan, dyn, cov):
    def body(dyn, cov, out):
        pair = split(cov[...])
        tile = plan.width

        def one(c, carry):
            at = pl.ds(pl.multiple_of(c * tile, tile), tile)
            out[at, :] = dot3(split(dyn[at, :]), pair, NT)
            return carry

        lax.fori_loop(0, plan.states // tile, one, 0)

    return call(
        body, "later_spread", [(plan.states, plan.panel)], (dyn, cov), [VM, VM], flops=2**29
    )[0]


def later_system_step(plan, info, ints, even, odd, upper, obs):
    states, items, panel = plan.states, plan.items, plan.panel

    def body(info, ints, even, odd, upper, obs, gains, inverse):
        for k in range(plan.n):
            gains[plan.rows_of(info, k), :] = (even, odd)[k % 2][k // 2]
        pair = split(gains[...])
        first = dot3(split(upper[...]), pair, NN)
        other = dense_factor(obs[0], ints[0:1, :items], plan.number)
        second = dot3(split(other), pair, NN)
        top = inverse_factor(identity(items) + first[:, :items])
        lower = mm(second[:, :items], top, NT)
        rest = identity(items) + second[:, items:] - mm(lower, lower, NT)
        bottom = inverse_factor(rest)
        inverse[:items, :items] = top
        inverse[:items, items:] = jnp.zeros((items, items), F32)
        inverse[items:, :items] = -mm(bottom, mm(lower, top))
        inverse[items:, items:] = bottom

    return call(
        body,
        "later_system",
        [(states, 2 * items), (2 * items, 2 * items)],
        (info, ints, even, odd, upper, obs),
        [SM, VM, VM, VM, VM, element(obs.shape, 0)],
        flops=2**31,
    )


def final_step(plan, info, ints, later_ints, own, later, own_cov, later_cov, gains, inverse, moved, own_obs, later_obs):
    states, items, panel, width, number = plan.states, plan.items, plan.panel, plan.width, plan.number
    own_dyn, own_upper, own_small = own
    later_dyn, later_upper, later_small = later

    def body(
        info, ints, later_ints, own_dyn, own_upper, own_small, later_dyn, later_upper, later_small,
        own_cov, later_cov, gains, inverse, moved, own_obs, later_obs,
        out_dyn, out_off, out_cov, out_fac, out_info, weights, upper, held, fac,
    ):
        me = info[0]
        mine = pl.ds(pl.multiple_of(me * panel, panel), panel)
        tile = min(256, states)

        def columns(ref):
            if panel % 128 == 0:
                return jnp.transpose(ref[:, mine])
            return jnp.transpose(pltpu.roll(ref[...], states - me * panel, 1)[:, :panel])

        def own_row(ref):
            if panel % 128 == 0:
                return ref[:, mine]
            return pltpu.roll(ref[...], states - me * panel, 1)[:, :panel]

        fac[...] = dense_factor(own_obs[0], ints[0:1, :items], number)

        @pl.when(info[2] == 0)
        def _():
            out_dyn[0] = own_dyn[mine, :]
            out_off[0] = own_row(own_small)[0:1, :]
            out_cov[0] = own_cov[...]
            out_fac[0, :, :items] = columns(own_upper)
            out_fac[0, :, items : 2 * items] = columns(fac)
            out_fac[0, :, 2 * items :] = jnp.zeros((panel, 2 * items), F32)
            zeta = jnp.concatenate([own_small[1:2, :items], own_small[2:3, :items]], axis=1)
            zeta = jnp.broadcast_to(zeta, (SMALL, 2 * items))
            out_info[0] = mm(zeta, out_fac[0, :, : 2 * items], NT)[0:1, :]

        @pl.when(info[2] == 1)
        def _():
            inverse_pair = split(inverse[...])
            gains_pair = split(gains[...])
            factor = jnp.concatenate(
                [later_upper[...], dense_factor(later_obs[0], later_ints[0:1, :items], number)], axis=0
            )
            factor_pair = split(factor)

            def weigh(c, carry):
                at = pl.ds(pl.multiple_of(c * tile, tile), tile)
                weights[at, :] = dot3(split(dot3(split(later_dyn[at, :]), gains_pair, NN)), inverse_pair, NT)
                return carry

            lax.fori_loop(0, states // tile, weigh, 0)
            for a in range(plan.n):
                held[:, a * panel : (a + 1) * panel] = moved[a]
            own_weight = weights[mine, :]
            weight_pair = split(-own_weight)
            held_pair = split(held[...])
            cov_left = tuple(jnp.concatenate([a, b], axis=1) for a, b in zip(held_pair, weight_pair))
            dyn_pair = split(later_dyn[mine, :])
            left = tuple(jnp.concatenate([a, b], axis=1) for a, b in zip(dyn_pair, weight_pair))

            def finish(c, carry):
                at = pl.ds(pl.multiple_of(c * tile, tile), tile)
                own_pair = split(own_dyn[:, at])
                up = dot3(inverse_pair, split(dot3(factor_pair, own_pair, NN)), NN)
                upper[:, at] = up
                right = tuple(jnp.concatenate([a, b], axis=0) for a, b in zip(own_pair, split(up)))
                out_dyn[0, :, at] = dot3(left, right, NN)
                right = split(jnp.concatenate([later_dyn[at, :], weights[at, :]], axis=1))
                out_cov[0, :, at] = dot3(cov_left, right, NT) + later_cov[:, at]
                return carry

            lax.fori_loop(0, states // tile, finish, 0)
            residual = jnp.concatenate([later_small[1:2, :items], later_small[2:3, :items]], axis=1)
            offset = jnp.broadcast_to(own_small[0:1, :], (SMALL, states))
            residual = jnp.broadcast_to(residual, (SMALL, 2 * items)) - mm(offset, factor, NT)
            solved = mm(residual, inverse[...], NT)
            gone = mm(offset, later_dyn[mine, :], NT) + mm(solved, own_weight, NT)
            out_off[0] = gone[0:1, :] + own_row(later_small)[0:1, :]
            out_fac[0, :, : 2 * items] = columns(upper)
            out_fac[0, :, 2 * items : 3 * items] = columns(own_upper)
            out_fac[0, :, 3 * items :] = columns(fac)
            zeta = jnp.concatenate([solved[0:1, :], own_small[1:2, :items], own_small[2:3, :items]], axis=1)
            zeta = jnp.broadcast_to(zeta, (SMALL, 4 * items))
            out_info[0] = mm(zeta, out_fac[0], NT)[0:1, :]

    return call(
        body,
        "final",
        [
            (1, panel, states),
            (1, 1, panel),
            (1, panel, states),
            (1, panel, 4 * items),
            (1, 1, panel),
        ],
        (
            info, ints, later_ints, own_dyn, own_upper, own_small, later_dyn, later_upper, later_small,
            own_cov, later_cov, gains, inverse, moved, own_obs, later_obs,
        ),
        [SM] + [VM] * 13 + [element(own_obs.shape, 0), element(later_obs.shape, 0)],
        scratch=[
            pltpu.VMEM((states, 2 * items), F32),
            pltpu.VMEM((2 * items, states), F32),
            pltpu.VMEM((panel, states), F32),
            pltpu.VMEM((items, states), F32),
        ],
        flops=2**32,
    )


def per_device(mesh, dyn_pattern, dyn_values, offsets, covariance, obs_block, obs_matrix, obs_data):
    plan = Plan(mesh, dyn_pattern, dyn_values, obs_block, obs_matrix)
    here = lax.axis_index(PLANE)
    even_turn = 1 - lax.axis_index("tm") % 2
    info = jnp.stack([here, lax.axis_index("obs"), even_turn]).astype(jnp.int32)
    ints = jnp.concatenate([obs_block, dyn_pattern.reshape(2, -1)], axis=1)

    pieces = [obs_matrix] + [exchange(obs_matrix, "obs", k, plan.obs) for k in range(1, plan.obs)]
    message, obs = gain_step(plan, info, ints, pieces, covariance, offsets, obs_data)
    later_values = earlier(plan, dyn_values)
    own_even, own_odd = gather(plan, dyn_values)
    later_even, later_odd = gather(plan, later_values)
    gain_even, gain_odd = gather(plan, message)
    pack = system_step(plan, info, ints, gain_even, gain_odd, obs)
    later_ints = earlier(plan, ints)
    later_obs = earlier(plan, obs)
    later_pack = earlier(plan, pack)

    spread, values = spread_step(plan, info, ints, own_even, own_odd, covariance)
    moved = swap_blocks(plan, spread.reshape(plan.n, plan.panel, plan.panel))
    own_dyn, own_weights, own_upper, own_small = level_step(plan, ints, values, pack, obs)
    own_cov = covariance_step(plan, info, ints, moved, values, own_weights, covariance)
    later_cov = earlier(plan, own_cov)

    later_full = assemble_step(plan, info, later_even, later_odd)
    later_dyn, _, later_upper, later_small = level_step(plan, later_ints, later_full, later_pack, later_obs)
    gain = later_gain_step(plan, later_ints, own_cov, later_upper, later_obs)
    gain_even, gain_odd = gather(plan, gain)
    spread = later_spread_step(plan, later_dyn, own_cov)
    moved = swap_blocks(plan, spread.reshape(plan.n, plan.panel, plan.panel))
    gains, inverse = later_system_step(plan, info, later_ints, gain_even, gain_odd, later_upper, later_obs)
    dyn, off, cov, fac, information = final_step(
        plan, info, ints, later_ints,
        (own_dyn, own_upper, own_small), (later_dyn, later_upper, later_small),
        own_cov, later_cov, gains, inverse, moved, obs, later_obs,
    )
    return dyn, off[:, 0], cov, fac, information[:, 0]


def solution(mesh):
    placed = (
        P("tm", None, None),
        P("tm", PLANE, None),
        P("tm", PLANE),
        P("tm", PLANE, None),
        P("tm", None),
        P("tm", "obs", None),
        P("tm", "obs"),
    )

    def run(*arrays):
        return per_device(mesh, *arrays)

    return jax.shard_map(
        run,
        mesh=mesh,
        in_specs=placed,
        out_specs=(
            P("tm", PLANE, None),
            P("tm", PLANE),
            P("tm", PLANE, None),
            P("tm", PLANE, None),
            P("tm", PLANE),
        ),
        check_vma=False,
    )
```

time: 431 us -> 190 us (0.44)
  waiting for transfers between devices: 157 us -> 44.2 us
  Pallas kernels: 0 us -> 100 us
  matrix products: 88.1 us -> 0 us
  other arithmetic: 84.3 us -> 3.71 us
  blocking collectives: 41.1 us -> 0 us
  starting transfers between devices: 7.91 us -> 31.3 us
  local copies, waits for them, and re-layouts: 28.5 us -> 5.4 us
  between operations: 16.3 us -> 0.91 us
    pallas_call x0 -> x11, Pallas kernels: none -> 100 us  [call(): pl.pallas_call(body, name=name, grid=(1,), in_specs=specs, out_specs=out_...]
    psum x2 -> x0, waiting for transfers between devices: 87.8 us -> none  [combine(): lax.psum(product(factor_pan.T, gain_pan), ('row', 'obs'))]
    dot_general x29 -> x0, matrix products: 82 us -> none  [the longest x25 71.6 us: product(): jnp.dot(left, right, precision=largest_value, preferred_element_type=jnp....]
    another operation x18 -> x5, other arithmetic: 78.8 us -> 3.71 us  [the longest x4 3.05 us: gather(): even = jnp.stack([x] + [exchange(x, PLANE, k, plan.n) for k in (2, 4, 6)])]
    all_gather x7 -> x0, waiting for transfers between devices: 46.6 us -> none  [the longest x1 24.8 us: per_device(): lax.all_gather(dyn_values, ('row', 'obs'), axis=1, tiled=True)]
    all_gather x5 -> x0, blocking collectives: 41.1 us -> none  [the longest x1 11.9 us: combine(): gain_rows = lax.all_gather(gain_pan, ('row', 'obs'), axis=0, tiled=True)]
    ppermute x5 -> x24, waiting for transfers between devices: 20.3 us -> 44.2 us  [the longest x19 35.8 us: exchange(): return lax.ppermute(x, axes, [(a, a ^ mask) for a in range(size)])]
    ppermute x5 -> x24, starting transfers between devices: 6.62 us -> 23.9 us  [the longest x19 17.5 us: exchange(): return lax.ppermute(x, axes, [(a, a ^ mask) for a in range(size)])]
  transfers between devices with their start and end apart: 14 -> 26, of which waited for: 6 -> 12; matrix products, arithmetic and copies ran while one was open for 44% -> 2% of each run, Pallas kernels for 0% -> 38%
where the time goes in v1:
time: 190 us; the launch traced here: 186 us
  Pallas kernels  100 us (53%)
  waiting for transfers between devices  44.2 us (23%)
  starting transfers between devices  31.3 us (16%)
  local copies, waits for them, and re-layouts  5.4 us (3%)
  other arithmetic  3.71 us (2%)
    pallas_call x11, Pallas kernels, call(): pl.pallas_call(body, name=name, grid=(1,), in_specs=specs, out_specs=out_...  100 us
    ppermute x19, waiting for transfers between devices, exchange(): return lax.ppermute(x, axes, [(a, a ^ mask) for a in range(size)])  35.8 us
    ppermute x19, starting transfers between devices, exchange(): return lax.ppermute(x, axes, [(a, a ^ mask) for a in range(size)])  17.5 us
    ppermute x5, waiting for transfers between devices, earlier(): return lax.ppermute(x, 'tm', [(i, i - 1) for i in range(1, plan.tm)])  8.41 us
    all_to_all x2, starting transfers between devices, swap_blocks(): return lax.all_to_all(x, PLANE, 0, 0, tiled=True)  7.42 us
    ppermute x5, starting transfers between devices, earlier(): return lax.ppermute(x, 'tm', [(i, i - 1) for i in range(1, plan.tm)])  6.45 us
    unnamed x42, local copies, waits for them, and re-layouts  5.31 us
  transfers between devices with their start and end apart: 26, of which 12 were waited for; matrix products, arithmetic and copies ran while one was open for 2% of the time, Pallas kernels for 38%

profile of v1, /device:TPU:0, one launch (start us, length us, event | category | flops | bytes accessed | tf_op | source)
XLA Modules:
  0.0 186.0 jit_solution(18223452184947551453)
XLA Ops:
  1.9 3.0 %collective-permute-start.2 = (f32[2,128,384]{2,1,0:T(8,128)}, f32[2,128,384]{2,1,0:T(8,128)S(1)}, u32[]{:S(2)}, u32[]{:S(2)}) collective-permute-start(f32[2,128,384]{2,1,0:T(8,128)} %param.8), channel_id=1, source_target_pairs={{0,4},{1,5},{2,6},{3,7},{4,0},{5,1},{6,2},{7,3},{8,12},{9,13},{10,... | collective-permute-start | bytes 1179656 | tf_op jit(solution)/shard_map/ppermute | solution.py:142
  6.5 8.4 %collective-permute-done.12 = f32[2,128,384]{2,1,0:T(8,128)S(1)} collective-permute-done((f32[2,128,384]{2,1,0:T(8,128)}, f32[2,128,384]{2,1,0:T(8,128)S(1)}, u32[]{:S(2)}, u32[]{:S(2)}) %collective-permute-start.12) | collective-permute-done | bytes 393248 | tf_op jit(solution)/shard_map/ppermute | solution.py:158
  14.9 2.6 %collective-permute-start.15 = (f32[2,128,384]{2,1,0:T(8,128)S(1)}, f32[2,128,384]{2,1,0:T(8,128)S(1)}, u32[]{:S(2)}, u32[]{:S(2)}) collective-permute-start(f32[2,128,384]{2,1,0:T(8,128)S(1)} %collective-permute-done.12), channel_id=1, source_target_pairs={{0,6},{1,7},{2,4},{3,5},{4,2},{5,3},{6,0},{7,1},{8,14},{9,15},{10,... | collective-permute-start | bytes 1179656 | tf_op jit(solution)/shard_map/ppermute | solution.py:142
  18.4 14.7 %collective-permute-done.1 = f32[2,128,384]{2,1,0:T(8,128)S(1)} collective-permute-done((f32[2,128,384]{2,1,0:T(8,128)}, f32[2,128,384]{2,1,0:T(8,128)S(1)}, u32[]{:S(2)}, u32[]{:S(2)}) %collective-permute-start.1) | collective-permute-done | bytes 393248 | tf_op jit(solution)/shard_map/ppermute | solution.py:142
  34.3 5.3 %collective-permute-done.14 = f32[2,128,384]{2,1,0:T(8,128)S(1)} collective-permute-done((f32[2,128,384]{2,1,0:T(8,128)S(1)}, f32[2,128,384]{2,1,0:T(8,128)S(1)}, u32[]{:S(2)}, u32[]{:S(2)}) %collective-permute-start.14) | collective-permute-done | bytes 393248 | tf_op jit(solution)/shard_map/ppermute | solution.py:142
  47.7 2.2 %gain.1 = (f32[136,128]{1,0:T(8,128)}, f32[2,128,256]{2,1,0:T(8,128)}) custom-call(s32[3]{0:T(128)} %pad_add_fusion.info, s32[2,152]{1,0:T(2,128)} %copy-done.12, f32[2,32,256]{2,1,0:T(8,128)} %refs_0_.1, f32[2,32,256]{2,1,0:T(8,128)} %copy-done.10, f32[2,32,256]{2,1,0:T(8,128)} %copy-done.9, f32[2,32,256]{2,1,0:T(8,128)} %copy-done.11, ...), custom_call_target="tpu_custom_call" | custom-call | flops 134217728 | bytes 1048576 | tf_op jit(solution)/shard_map/gain/pallas_call | solution.py:99
  51.3 1.9 %collective-permute-start.9 = (f32[136,128]{1,0:T(8,128)}, f32[136,128]{1,0:T(8,128)S(1)}, u32[]{:S(2)}, u32[]{:S(2)}) collective-permute-start(f32[136,128]{1,0:T(8,128)} %get-tuple-element.24), channel_id=1, source_target_pairs={{0,4},{1,5},{2,6},{3,7},{4,0},{5,1},{6,2},{7,3},{8,12},{9,13},{10,... | collective-permute-start | bytes 208904 | tf_op jit(solution)/shard_map/ppermute | solution.py:142
  53.5 2.6 %collective-permute-done.10 = f32[136,128]{1,0:T(8,128)S(1)} collective-permute-done((f32[136,128]{1,0:T(8,128)}, f32[136,128]{1,0:T(8,128)S(1)}, u32[]{:S(2)}, u32[]{:S(2)}) %collective-permute-start.10) | collective-permute-done | bytes 69664 | tf_op jit(solution)/shard_map/ppermute | solution.py:142
  58.8 1.5 collective-permute-done.11.odd
  61.0 6.8 %system.1.pack = f32[1216,128]{1,0:T(8,128)} custom-call(s32[3]{0:T(128)} %pad_add_fusion.info, s32[2,152]{1,0:T(2,128)} %copy-done.12, f32[4,136,128]{2,1,0:T(8,128)} %copy-done.6, f32[4,136,128]{2,1,0:T(8,128)} %copy-done.19, f32[2,128,256]{2,1,0:T(8,128)} %get-tuple-element.25.obs.own_obs), custom_call_target="tpu_custom_call" | custom-call | flops 1073741824 | bytes 1048576 | tf_op jit(solution)/shard_map/system/pallas_call | solution.py:99
  71.7 4.3 %spread.1 = (f32[1024,128]{1,0:T(8,128)}, f32[2,1024,384]{2,1,0:T(8,128)}) custom-call(s32[3]{0:T(128)} %pad_add_fusion.info, s32[2,152]{1,0:T(2,128)} %copy-done.12, f32[4,2,128,384]{3,2,1,0:T(8,128)} %copy-done, f32[4,2,128,384]{3,2,1,0:T(8,128)} %collective-permute-done.4.odd, f32[2,128,1024]{2,1,0:T(8,128)} %cov.3), custom_call_target="tpu_custom_call" | custom-call | flops 268435456 | bytes 1048576 | tf_op jit(solution)/shard_map/spread/pallas_call | solution.py:99
  76.0 3.7 %all-to-all-start = ((f32[8,128,128]{2,1,0:T(8,128)}), f32[8,128,128]{2,1,0:T(8,128)S(1)}, u32[]{:S(2)}, u32[]{:S(2)}) async-start(f32[8,128,128]{2,1,0:T(8,128)} %bitcast.24), calls=%async_computation | async-start | bytes 1048576 | tf_op jit(solution)/shard_map/all_to_all | solution.py:154
  79.7 17.9 %level.2 = (f32[1024,1024]{1,0:T(8,128)}, f32[1024,128]{1,0:T(8,128)}, f32[128,1024]{1,0:T(8,128)}, f32[8,1024]{1,0:T(8,128)}) custom-call(s32[2,152]{1,0:T(2,128)} %copy-done.12, s32[2,152]{1,0:T(2,128)} %copy-done.12, f32[2,1024,384]{2,1,0:T(8,128)} %get-tuple-element.23.values, f32[1216,128]{1,0:T(8,128)} %system.1.pack, ...), custom_call_target="tpu_custom_call" | custom-call | flops 4294967296 | bytes 1048576 | tf_op jit(solution)/shard_map/level/pallas_call | solution.py:99
  97.6 3.8 %assemble.1.values = f32[2,1024,384]{2,1,0:T(8,128)} custom-call(s32[3]{0:T(128)} %pad_add_fusion.info, f32[4,2,128,384]{3,2,1,0:T(8,128)} %copy-done.1, f32[4,2,128,384]{3,2,1,0:T(8,128)} %collective-permute-done.16.odd), custom_call_target="tpu_custom_call" | custom-call | bytes 1048576 | tf_op jit(solution)/shard_map/assemble/pallas_call | solution.py:99
  102.1 18.0 %level.3 = (f32[1024,1024]{1,0:T(8,128)}, f32[1024,128]{1,0:T(8,128)}, f32[128,1024]{1,0:T(8,128)}, f32[8,1024]{1,0:T(8,128)}) custom-call(s32[2,152]{1,0:T(2,128)} %copy-done.15, s32[2,152]{1,0:T(2,128)} %copy-done.15, f32[2,1024,384]{2,1,0:T(8,128)} %assemble.1.values, f32[1216,128]{1,0:T(8,128)} %collective-permute-done.17.pack, f32[2,128,256]{2,1,0:T(8,128)} %copy-done.7), custom_call_target="tpu_custom_call" | custom-call | flops 4294967296 | bytes 1048576 | tf_op jit(solution)/shard_map/level/pallas_call | solution.py:99
  120.9 3.9 %covariance.1.cov.own_cov = f32[128,1024]{1,0:T(8,128)} custom-call(s32[3]{0:T(128)} %pad_add_fusion.info, s32[2,152]{1,0:T(2,128)} %copy-done.12, f32[8,128,128]{2,1,0:T(8,128)} %copy-done.3, f32[2,1024,384]{2,1,0:T(8,128)} %get-tuple-element.23.values, f32[1024,128]{1,0:T(8,128)} %get-tuple-element.33.weights, f32[2,128,1024]{2,1,0:T(8,128)} %cov.3), custom_call_target="tpu_custom_call" | custom-call | flops 268435456 | bytes 1048576 | tf_op jit(solution)/shard_map/covariance/pallas_call | solution.py:99
  124.7 2.6 %later_gain.1 = f32[128,256]{1,0:T(8,128)} custom-call(s32[2,152]{1,0:T(2,128)} %copy-done.15, f32[128,1024]{1,0:T(8,128)} %covariance.1.cov.own_cov, f32[128,1024]{1,0:T(8,128)} %get-tuple-element.30.upper.later_upper, f32[2,128,256]{2,1,0:T(8,128)} %copy-done.7), custom_call_target="tpu_custom_call" | custom-call | flops 268435456 | bytes 1048576 | tf_op jit(solution)/shard_map/later_gain/pallas_call | solution.py:99
  127.4 2.7 %collective-permute-start.22 = (f32[128,256]{1,0:T(8,128)}, f32[128,256]{1,0:T(8,128)S(1)}, u32[]{:S(2)}, u32[]{:S(2)}) collective-permute-start(f32[128,256]{1,0:T(8,128)} %later_gain.1), channel_id=1, source_target_pairs={{0,6},{1,7},{2,4},{3,5},{4,2},{5,3},{6,0},{7,1},{8,14},{9,15},{10,... | collective-permute-start | bytes 393224 | tf_op jit(solution)/shard_map/ppermute | solution.py:142
  130.9 4.0 %collective-permute-done.22 = f32[128,256]{1,0:T(8,128)S(1)} collective-permute-done((f32[128,256]{1,0:T(8,128)}, f32[128,256]{1,0:T(8,128)S(1)}, u32[]{:S(2)}, u32[]{:S(2)}) %collective-permute-start.22) | collective-permute-done | bytes 131104 | tf_op jit(solution)/shard_map/ppermute | solution.py:142
  134.8 2.3 %collective-permute-done.21 = f32[128,256]{1,0:T(8,128)S(1)} collective-permute-done((f32[128,256]{1,0:T(8,128)}, f32[128,256]{1,0:T(8,128)S(1)}, u32[]{:S(2)}, u32[]{:S(2)}) %collective-permute-start.21) | collective-permute-done | bytes 131104 | tf_op jit(solution)/shard_map/ppermute | solution.py:142
  139.5 6.2 %later_spread.1 = f32[1024,128]{1,0:T(8,128)} custom-call(f32[1024,1024]{1,0:T(8,128)} %get-tuple-element.29.dyn.later_dyn, f32[128,1024]{1,0:T(8,128)} %covariance.1.cov.own_cov), custom_call_target="tpu_custom_call" | custom-call | flops 536870912 | bytes 1048576 | tf_op jit(solution)/shard_map/later_spread/pallas_call | solution.py:99
  145.7 3.7 %all-to-all-start.1 = ((f32[8,128,128]{2,1,0:T(8,128)}), f32[8,128,128]{2,1,0:T(8,128)S(1)}, u32[]{:S(2)}, u32[]{:S(2)}) async-start(f32[8,128,128]{2,1,0:T(8,128)} %bitcast.23), calls=%async_computation.1 | async-start | bytes 1048576 | tf_op jit(solution)/shard_map/all_to_all | solution.py:154
  150.2 11.8 %later_system.1 = (f32[1024,256]{1,0:T(8,128)}, f32[256,256]{1,0:T(8,128)}) custom-call(s32[3]{0:T(128)} %pad_add_fusion.info, s32[2,152]{1,0:T(2,128)} %copy-done.15, f32[4,128,256]{2,1,0:T(8,128)} %copy-done.5, f32[4,128,256]{2,1,0:T(8,128)} %copy-done.18, f32[128,1024]{1,0:T(8,128)} %get-tuple-element.30.upper.later_upper, f32[2,128,256]{2,1,0:T(8,128)} %copy-done.7), custom_call_target="tpu_custom_call" | custom-call | flops 2147483648 | bytes 1048576 | tf_op jit(solution)/shard_map/later_system/pallas_call | solution.py:99
  163.0 23.0 %final.1 = (f32[1,128,1024]{2,1,0:T(8,128)}, f32[1,1,128]{2,1,0:T(1,128)}, f32[1,128,1024]{2,1,0:T(8,128)}, f32[1,128,512]{2,1,0:T(8,128)}, f32[1,1,128]{2,1,0:T(1,128)}) custom-call(s32[3]{0:T(128)} %pad_add_fusion.info, s32[2,152]{1,0:T(2,128)} %copy-done.12, s32[2,152]{1,0:T(2,128)} %copy-done.15, f32[1024,1024]{1,0:T(8,128)} %get-tuple-element.26.own_dyn, ...), custom_call_target="tpu_custom_call" | custom-call | flops 4294967296 | bytes 1048576 | tf_op jit(solution)/shard_map/final/pallas_call | solution.py:99
  (88 shorter events, 28.2 us)
Async XLA Ops:
  0.6 14.2 %collective-permute-start.12 = (f32[2,128,384]{2,1,0:T(8,128)}, f32[2,128,384]{2,1,0:T(8,128)S(1)}, u32[]{:S(2)}, u32[]{:S(2)}) collective-permute-start(f32[2,128,384]{2,1,0:T(8,128)} %param.8), channel_id=1, source_target_pairs={{8,0},{16,8},{24,16},{9,1},{17,9},{25,17},{10,2},{18,10},{26,18},{... | collective-permute-start | bytes 1179656 | tf_op jit(solution)/shard_map/ppermute | solution.py:158
  1.9 16.1 %collective-permute-start.2 = (f32[2,128,384]{2,1,0:T(8,128)}, f32[2,128,384]{2,1,0:T(8,128)S(1)}, u32[]{:S(2)}, u32[]{:S(2)}) collective-permute-start(f32[2,128,384]{2,1,0:T(8,128)} %param.8), channel_id=1, source_target_pairs={{0,4},{1,5},{2,6},{3,7},{4,0},{5,1},{6,2},{7,3},{8,12},{9,13},{10,... | collective-permute-start | bytes 1179656 | tf_op jit(solution)/shard_map/ppermute | solution.py:142
  4.9 28.1 %collective-permute-start.1 = (f32[2,128,384]{2,1,0:T(8,128)}, f32[2,128,384]{2,1,0:T(8,128)S(1)}, u32[]{:S(2)}, u32[]{:S(2)}) collective-permute-start(f32[2,128,384]{2,1,0:T(8,128)} %param.8), channel_id=1, source_target_pairs={{0,2},{1,3},{2,0},{3,1},{4,6},{5,7},{6,4},{7,5},{8,10},{9,11},{10,... | collective-permute-start | bytes 1179656 | tf_op jit(solution)/shard_map/ppermute | solution.py:142
  6.5 26.6 %collective-permute-start.3 = (f32[2,128,384]{2,1,0:T(8,128)}, f32[2,128,384]{2,1,0:T(8,128)S(1)}, u32[]{:S(2)}, u32[]{:S(2)}) collective-permute-start(f32[2,128,384]{2,1,0:T(8,128)} %param.8), channel_id=1, source_target_pairs={{0,6},{1,7},{2,4},{3,5},{4,2},{5,3},{6,0},{7,1},{8,14},{9,15},{10,... | collective-permute-start | bytes 1179656 | tf_op jit(solution)/shard_map/ppermute | solution.py:142
  14.9 19.4 %collective-permute-start.15 = (f32[2,128,384]{2,1,0:T(8,128)S(1)}, f32[2,128,384]{2,1,0:T(8,128)S(1)}, u32[]{:S(2)}, u32[]{:S(2)}) collective-permute-start(f32[2,128,384]{2,1,0:T(8,128)S(1)} %collective-permute-done.12), channel_id=1, source_target_pairs={{0,6},{1,7},{2,4},{3,5},{4,2},{5,3},{6,0},{7,1},{8,14},{9,15},{10,... | collective-permute-start | bytes 1179656 | tf_op jit(solution)/shard_map/ppermute | solution.py:142
  17.5 22.1 %collective-permute-start.14 = (f32[2,128,384]{2,1,0:T(8,128)S(1)}, f32[2,128,384]{2,1,0:T(8,128)S(1)}, u32[]{:S(2)}, u32[]{:S(2)}) collective-permute-start(f32[2,128,384]{2,1,0:T(8,128)S(1)} %collective-permute-done.12), channel_id=1, source_target_pairs={{0,4},{1,5},{2,6},{3,7},{4,0},{5,1},{6,2},{7,3},{8,12},{9,13},{10,... | collective-permute-start | bytes 1179656 | tf_op jit(solution)/shard_map/ppermute | solution.py:142
  18.0 23.0 %collective-permute-start.13 = (f32[2,128,384]{2,1,0:T(8,128)S(1)}, f32[2,128,384]{2,1,0:T(8,128)S(1)}, u32[]{:S(2)}, u32[]{:S(2)}) collective-permute-start(f32[2,128,384]{2,1,0:T(8,128)S(1)} %collective-permute-done.12), channel_id=1, source_target_pairs={{0,2},{1,3},{2,0},{3,1},{4,6},{5,7},{6,4},{7,5},{8,10},{9,11},{10,... | collective-permute-start | bytes 1179656 | tf_op jit(solution)/shard_map/ppermute | solution.py:142
  34.2 37.5 %collective-permute-start.4 = (f32[4,2,128,384]{3,2,1,0:T(8,128)S(1)}, f32[4,2,128,384]{3,2,1,0:T(8,128)}, u32[]{:S(2)}, u32[]{:S(2)}) collective-permute-start(f32[4,2,128,384]{3,2,1,0:T(8,128)S(1)} %pad_maximum_fusion.even), channel_id=1, source_target_pairs={{0,1},{1,0},{2,3},{3,2},{4,5},{5,4},{6,7},{7,6},{8,9},{9,8},{10,11... | collective-permute-start | bytes 4718600 | tf_op jit(solution)/shard_map/ppermute | solution.py:142
  41.1 56.5 %collective-permute-start.16 = (f32[4,2,128,384]{3,2,1,0:T(8,128)S(1)}, f32[4,2,128,384]{3,2,1,0:T(8,128)}, u32[]{:S(2)}, u32[]{:S(2)}) collective-permute-start(f32[4,2,128,384]{3,2,1,0:T(8,128)S(1)} %pad_maximum_fusion.1.even), channel_id=1, source_target_pairs={{0,1},{1,0},{2,3},{3,2},{4,5},{5,4},{6,7},{7,6},{8,9},{9,8},{10,11... | collective-permute-start | bytes 4718600 | tf_op jit(solution)/shard_map/ppermute | solution.py:142
  41.8 4.3 %collective-permute-start.6 = (f32[2,32,256]{2,1,0:T(8,128)S(1)}, f32[2,32,256]{2,1,0:T(8,128)S(1)}, u32[]{:S(2)}, u32[]{:S(2)}) collective-permute-start(f32[2,32,256]{2,1,0:T(8,128)S(1)} %copy-done.8), channel_id=1, source_target_pairs={{0,2},{1,3},{2,0},{3,1},{4,6},{5,7},{6,4},{7,5},{8,10},{9,11},{10,... | collective-permute-start | bytes 196616 | tf_op jit(solution)/shard_map/ppermute | solution.py:142
  43.4 3.7 %collective-permute-start.7 = (f32[2,32,256]{2,1,0:T(8,128)S(1)}, f32[2,32,256]{2,1,0:T(8,128)S(1)}, u32[]{:S(2)}, u32[]{:S(2)}) collective-permute-start(f32[2,32,256]{2,1,0:T(8,128)S(1)} %copy-done.8), channel_id=1, source_target_pairs={{0,3},{1,2},{2,1},{3,0},{4,7},{5,6},{6,5},{7,4},{8,11},{9,10},{10,... | collective-permute-start | bytes 196616 | tf_op jit(solution)/shard_map/ppermute | solution.py:142
  50.0 6.1 %collective-permute-start.10 = (f32[136,128]{1,0:T(8,128)}, f32[136,128]{1,0:T(8,128)S(1)}, u32[]{:S(2)}, u32[]{:S(2)}) collective-permute-start(f32[136,128]{1,0:T(8,128)} %get-tuple-element.24), channel_id=1, source_target_pairs={{0,6},{1,7},{2,4},{3,5},{4,2},{5,3},{6,0},{7,1},{8,14},{9,15},{10,... | collective-permute-start | bytes 208904 | tf_op jit(solution)/shard_map/ppermute | solution.py:142
  51.3 5.6 %collective-permute-start.9 = (f32[136,128]{1,0:T(8,128)}, f32[136,128]{1,0:T(8,128)S(1)}, u32[]{:S(2)}, u32[]{:S(2)}) collective-permute-start(f32[136,128]{1,0:T(8,128)} %get-tuple-element.24), channel_id=1, source_target_pairs={{0,4},{1,5},{2,6},{3,7},{4,0},{5,1},{6,2},{7,3},{8,12},{9,13},{10,... | collective-permute-start | bytes 208904 | tf_op jit(solution)/shard_map/ppermute | solution.py:142
  53.2 4.5 %collective-permute-start.8 = (f32[136,128]{1,0:T(8,128)}, f32[136,128]{1,0:T(8,128)S(1)}, u32[]{:S(2)}, u32[]{:S(2)}) collective-permute-start(f32[136,128]{1,0:T(8,128)} %get-tuple-element.24), channel_id=1, source_target_pairs={{0,2},{1,3},{2,0},{3,1},{4,6},{5,7},{6,4},{7,5},{8,10},{9,11},{10,... | collective-permute-start | bytes 208904 | tf_op jit(solution)/shard_map/ppermute | solution.py:142
  67.8 33.6 %collective-permute-start.17 = (f32[1216,128]{1,0:T(8,128)}, f32[1216,128]{1,0:T(8,128)}, u32[]{:S(2)}, u32[]{:S(2)}) collective-permute-start(f32[1216,128]{1,0:T(8,128)} %system.1.pack), channel_id=1, source_target_pairs={{8,0},{16,8},{24,16},{9,1},{17,9},{25,17},{10,2},{18,10},{26,18},{... | collective-permute-start | bytes 1867784 | tf_op jit(solution)/shard_map/ppermute | solution.py:158
  69.1 32.3 %collective-permute-start = (s32[2,152]{1,0:T(2,128)S(1)}, s32[2,152]{1,0:T(2,128)S(1)}, u32[]{:S(2)}, u32[]{:S(2)}) collective-permute-start(s32[2,152]{1,0:T(2,128)S(1)} %copy-done.13), channel_id=1, source_target_pairs={{8,0},{16,8},{24,16},{9,1},{17,9},{25,17},{10,2},{18,10},{26,18},{... | collective-permute-start | bytes 3656 | tf_op jit(solution)/shard_map/ppermute | solution.py:158
  70.4 31.0 %collective-permute-start.18 = (f32[2,128,256]{2,1,0:T(8,128)}, f32[2,128,256]{2,1,0:T(8,128)S(1)}, u32[]{:S(2)}, u32[]{:S(2)}) collective-permute-start(f32[2,128,256]{2,1,0:T(8,128)} %get-tuple-element.25.obs.own_obs), channel_id=1, source_target_pairs={{8,0},{16,8},{24,16},{9,1},{17,9},{25,17},{10,2},{18,10},{26,18},{... | collective-permute-start | bytes 786440 | tf_op jit(solution)/shard_map/ppermute | solution.py:158
  76.0 44.1 %all-to-all-start = ((f32[8,128,128]{2,1,0:T(8,128)}), f32[8,128,128]{2,1,0:T(8,128)S(1)}, u32[]{:S(2)}, u32[]{:S(2)}) async-start(f32[8,128,128]{2,1,0:T(8,128)} %bitcast.24), calls=%async_computation | async-start | bytes 1048576 | tf_op jit(solution)/shard_map/all_to_all | solution.py:154
  127.4 7.4 %collective-permute-start.22 = (f32[128,256]{1,0:T(8,128)}, f32[128,256]{1,0:T(8,128)S(1)}, u32[]{:S(2)}, u32[]{:S(2)}) collective-permute-start(f32[128,256]{1,0:T(8,128)} %later_gain.1), channel_id=1, source_target_pairs={{0,6},{1,7},{2,4},{3,5},{4,2},{5,3},{6,0},{7,1},{8,14},{9,15},{10,... | collective-permute-start | bytes 393224 | tf_op jit(solution)/shard_map/ppermute | solution.py:142
  130.0 7.1 %collective-permute-start.21 = (f32[128,256]{1,0:T(8,128)}, f32[128,256]{1,0:T(8,128)S(1)}, u32[]{:S(2)}, u32[]{:S(2)}) collective-permute-start(f32[128,256]{1,0:T(8,128)} %later_gain.1), channel_id=1, source_target_pairs={{0,4},{1,5},{2,6},{3,7},{4,0},{5,1},{6,2},{7,3},{8,12},{9,13},{10,... | collective-permute-start | bytes 393224 | tf_op jit(solution)/shard_map/ppermute | solution.py:142
  130.6 6.6 %collective-permute-start.20 = (f32[128,256]{1,0:T(8,128)}, f32[128,256]{1,0:T(8,128)S(1)}, u32[]{:S(2)}, u32[]{:S(2)}) collective-permute-start(f32[128,256]{1,0:T(8,128)} %later_gain.1), channel_id=1, source_target_pairs={{0,2},{1,3},{2,0},{3,1},{4,6},{5,7},{6,4},{7,5},{8,10},{9,11},{10,... | collective-permute-start | bytes 393224 | tf_op jit(solution)/shard_map/ppermute | solution.py:142
  138.1 11.3 %collective-permute-start.23 = (f32[4,128,256]{2,1,0:T(8,128)S(1)}, f32[4,128,256]{2,1,0:T(8,128)S(1)}, u32[]{:S(2)}, u32[]{:S(2)}) collective-permute-start(f32[4,128,256]{2,1,0:T(8,128)S(1)} %pad_maximum_fusion.2.even), channel_id=1, source_target_pairs={{0,1},{1,0},{2,3},{3,2},{4,5},{5,4},{6,7},{7,6},{8,9},{9,8},{10,11... | collective-permute-start | bytes 1572872 | tf_op jit(solution)/shard_map/ppermute | solution.py:142
  138.2 23.9 %collective-permute-start.19 = (f32[128,1024]{1,0:T(8,128)S(1)}, f32[128,1024]{1,0:T(8,128)S(1)}, u32[]{:S(2)}, u32[]{:S(2)}) collective-permute-start(f32[128,1024]{1,0:T(8,128)S(1)} %copy-done.2), channel_id=1, source_target_pairs={{8,0},{16,8},{24,16},{9,1},{17,9},{25,17},{10,2},{18,10},{26,18},{... | collective-permute-start | bytes 1572872 | tf_op jit(solution)/shard_map/ppermute | solution.py:158
  145.7 16.4 %all-to-all-start.1 = ((f32[8,128,128]{2,1,0:T(8,128)}), f32[8,128,128]{2,1,0:T(8,128)S(1)}, u32[]{:S(2)}, u32[]{:S(2)}) async-start(f32[8,128,128]{2,1,0:T(8,128)} %bitcast.23), calls=%async_computation.1 | async-start | bytes 1048576 | tf_op jit(solution)/shard_map/all_to_all | solution.py:154
  (22 other events, 86.6 us)

commit v2 on v1

v2 whole, which is shorter than its diff:
```python
import jax
import jax.numpy as jnp
from jax import lax
from jax.experimental import pallas as pl
from jax.experimental.pallas import tpu as pltpu
from jax.sharding import PartitionSpec as P

F32 = jnp.float32
BF16 = jnp.bfloat16
NN = (((1,), (0,)), ((), ()))
NT = (((1,), (1,)), ((), ()))
PLANE = ("row", "obs")
SMALL = 8


def split(x):
    high = x.astype(BF16)
    return high, (x - high.astype(F32)).astype(BF16)


def dot3(left, right, dims):
    (a, b), (c, d) = left, right
    return lax.dot_general(
        jnp.concatenate([a, a, b], axis=1),
        jnp.concatenate([c, d, c], axis=dims[0][1][0]),
        dims,
        preferred_element_type=F32,
    )


def mm(left, right, dims=NN):
    return dot3(split(left), split(right), dims)


def reciprocal(x):
    y = pl.reciprocal(x, approx=True)
    return y * (2.0 - x * y)


def inverse_root(x):
    y = lax.rsqrt(x)
    return y * (1.5 - (0.5 * x) * (y * y))


def inverse_factor(matrix):
    size = matrix.shape[0]
    tiles = size // 8
    sub = lax.broadcasted_iota(jnp.int32, (8, size), 0)
    lane = lax.broadcasted_iota(jnp.int32, (8, size), 1)

    def wide(x):
        return jnp.broadcast_to(x, (8, size))

    rows = [matrix[8 * t : 8 * t + 8, :] for t in range(tiles)]
    inverse = [jnp.where(lane == sub + 8 * t, 1.0, 0.0).astype(F32) for t in range(tiles)]
    for p in range(tiles):
        column = {
            (t, c): wide(rows[t][:, 8 * p + c : 8 * p + c + 1])
            for t in range(p, tiles)
            for c in range(8)
        }
        scale = None
        for r in range(8):
            pivot = wide(column[p, r][r : r + 1, :])
            over = reciprocal(pivot)
            root = inverse_root(pivot)
            scale = root if r == 0 else jnp.where(sub == r, root, scale)
            factor = {t: column[t, r] * over for t in range(p, tiles)}
            for c in range(r + 1, 8):
                other = wide(column[p, r][c : c + 1, :])
                for t in range(p, tiles):
                    column[t, c] = column[t, c] - factor[t] * other
            factor[p] = jnp.where(sub > r, factor[p], 0.0)
            row_here = wide(rows[p][r : r + 1, :])
            inverse_here = wide(inverse[p][r : r + 1, :])
            for t in range(p, tiles):
                rows[t] = rows[t] - factor[t] * row_here
                inverse[t] = inverse[t] - factor[t] * inverse_here
        inverse[p] = inverse[p] * scale
    return jnp.concatenate(inverse, axis=0)


def identity(size):
    sub = lax.broadcasted_iota(jnp.int32, (size, size), 0)
    lane = lax.broadcasted_iota(jnp.int32, (size, size), 1)
    return jnp.where(sub == lane, 1.0, 0.0).astype(F32)


def dense_factor(matrix, blocks, number):
    items, width = matrix.shape[0], matrix.shape[1] // 2
    at = jnp.transpose(jnp.broadcast_to(blocks.astype(F32), (width, items)))
    pieces = []
    for r in range(number):
        first = jnp.where(at == float(r), matrix[:, :width], 0.0)
        second = jnp.where(at == float((r - 1) % number), matrix[:, width:], 0.0)
        pieces.append(first + second)
    return jnp.concatenate(pieces, axis=1)


def call(body, name, out_shapes, args, specs, scratch=(), micros=1, grant=24):
    return pl.pallas_call(
        body,
        name=name,
        grid=(1,),
        in_specs=specs,
        out_specs=[VM] * len(out_shapes),
        out_shape=[s if isinstance(s, jax.ShapeDtypeStruct) else jax.ShapeDtypeStruct(s, F32) for s in out_shapes],
        scratch_shapes=list(scratch),
        compiler_params=pltpu.CompilerParams(vmem_limit_bytes=grant * 2**20),
        cost_estimate=pl.CostEstimate(flops=micros * 10**9, bytes_accessed=2**20, transcendentals=0),
    )(*args)


VM = pl.BlockSpec(memory_space=pltpu.VMEM)
SM = pl.BlockSpec(memory_space=pltpu.SMEM)


def element(shape, which):
    return pl.BlockSpec((1,) + tuple(shape[1:]), lambda i: (which,) + (0,) * (len(shape) - 1))


def part(shape, which):
    if len(shape) == 3:
        return VM
    return pl.BlockSpec((shape[0], None) + tuple(shape[2:]), lambda i: (0, which, 0, 0))


class Plan:
    def __init__(self, mesh, pattern, values, obs_block, obs_matrix):
        self.row, self.obs = mesh.shape["row"], mesh.shape["obs"]
        self.tm = mesh.shape["tm"]
        self.n = self.row * self.obs
        self.number, self.per_row = pattern.shape[1:]
        self.panel = values.shape[1]
        self.states = self.panel * self.n
        self.width = self.states // self.number
        self.items = obs_block.shape[1]
        self.share = obs_matrix.shape[1]
        self.swapped = self.n == 8 and self.panel % 128 == 0

    def source(self, info, k):
        return lax.bitwise_xor(info[0], k) if self.swapped else k

    def rows_of(self, info, k):
        start = self.source(info, k) * self.panel
        return pl.ds(pl.multiple_of(start, self.panel) if self.swapped else start, self.panel)


def exchange(x, axes, mask, size):
    return lax.ppermute(x, axes, [(a, a ^ mask) for a in range(size)])


def first_leg(plan, x):
    if plan.swapped:
        return [x] + [exchange(x, PLANE, k, plan.n) for k in (2, 4, 6)]
    return [lax.all_gather(x, PLANE, axis=0)]


def second_leg(plan, pieces):
    if plan.swapped:
        even = jnp.stack(pieces)
        return even, exchange(even, PLANE, 1, plan.n)
    return pieces[0][0::2], pieces[0][1::2]


def other_core(plan, even, odd):
    if plan.swapped:
        return exchange(even, PLANE, 1, plan.n)
    return earlier(plan, odd)


def gather(plan, x):
    return second_leg(plan, first_leg(plan, x))


def tie(*trees):
    return lax.optimization_barrier(trees)


def swap_blocks(plan, x):
    return lax.all_to_all(x, PLANE, 0, 0, tiled=True)


def earlier(plan, x):
    return lax.ppermute(x, "tm", [(i, i - 1) for i in range(1, plan.tm)])


def gain_step(plan, info, blocks, pieces, covariance, offsets, data):
    share, panel, items = plan.share, plan.panel, plan.items

    def body(info, blocks, *refs):
        parts = refs[: plan.obs]
        cov, off, dat, message, obs = refs[plan.obs :]
        for k, part in enumerate(parts):
            start = pl.multiple_of(lax.bitwise_xor(info[1], k) * share, share)
            obs[:, pl.ds(start, share), :] = part[...]
        factor = dense_factor(obs[1], blocks[1:2, :], plan.number)
        message[:panel, :] = mm(cov[0], factor, NT)
        message[panel:, :] = jnp.zeros((SMALL, items), F32)
        message[panel : panel + 2, :panel] = off[...]
        spread = jnp.concatenate([dat[...], jnp.zeros((2, items - share), F32)], axis=1)
        spread = jnp.concatenate([spread, jnp.zeros((6, items), F32)], axis=0)
        message[panel + 2 : panel + 4, :] = pltpu.roll(spread, info[1] * share, 1)[:2]

    return call(
        body,
        "gain",
        [(panel + SMALL, items), (2, items, 2 * plan.width)],
        (info, blocks, *pieces, covariance, offsets, data),
        [SM, VM] + [VM] * plan.obs + [element(covariance.shape, 0), VM, VM],
        grant=56,
        micros=1,
    )


def system_step(plan, info, ints, even, odd, obs):
    states, items, panel = plan.states, plan.items, plan.panel

    def body(info, ints, even, odd, obs, gains, pack):
        tail = items
        zeta = jnp.zeros((2, items), F32)
        end = tail + SMALL * plan.number
        pack[tail:end, :] = jnp.zeros((SMALL * plan.number, items), F32)
        for e in range(2):
            for h in range(2):
                at = end + (2 * e + h) * items
                pack[at : at + items, :] = obs[e, :, h * plan.width : (h + 1) * plan.width]
        for k in range(plan.n):
            piece = (even, odd)[k % 2]
            gains[plan.rows_of(info, k), :] = piece[k // 2, :panel, :]
            start = plan.source(info, k) * panel
            if plan.swapped:
                block = start // plan.width
                at = pl.multiple_of(tail + block * SMALL, SMALL)
                pack[pl.ds(at, 2), :] = piece[k // 2, panel : panel + 2, :]
            else:
                at = tail + start // plan.width * SMALL
                lane = start % plan.width
                pack[at : at + 2, lane : lane + panel] = piece[k // 2, panel : panel + 2, :panel]
            if k < plan.obs:
                zeta = zeta + piece[k // 2, panel + 2 : panel + 4, :]
        pack[tail + 2 : tail + 4, :] = zeta
        factor = dense_factor(obs[1], ints[1:2, :items], plan.number)
        system = identity(items) + mm(factor, gains[...])
        pack[:tail, :] = inverse_factor(system)

    return call(
        body,
        "system",
        [(states, items), (5 * items + SMALL * plan.number, items)],
        (info, ints, even, odd, obs),
        [SM, VM, VM, VM, VM],
        micros=20,
    )


def fill(plan, info, even, odd, out):
    for k in range(plan.n):
        out[plan.rows_of(info, k), :] = (even, odd)[k % 2][k // 2, : plan.panel]


def starts(plan, ints, which, c):
    return [
        pl.multiple_of(ints[which, plan.items + c * plan.per_row + k] * plan.width, plan.width)
        for k in range(plan.per_row)
    ]


def spread_step(plan, info, ints, even, odd, covariance):
    states, panel, width = plan.states, plan.panel, plan.width
    wide = plan.per_row * width

    def body(info, ints, even, odd, cov, out, values, high, low):
        fill(plan, info, even, odd, values)
        high[...], low[...] = split(cov[0])
        for c in range(plan.number):
            taken = tuple(
                jnp.concatenate([r[:, pl.ds(s, width)] for s in starts(plan, ints, 1, c)], axis=1)
                for r in (high, low)
            )
            at = slice(c * width, (c + 1) * width)
            out[at, :] = dot3(split(values[at, :]), taken, NT)

    return call(
        body,
        "spread",
        [(states, panel), (states, wide)],
        (info, ints, even, odd, covariance),
        [SM, SM, VM, VM, element(covariance.shape, 0)],
        scratch=[pltpu.VMEM((panel, states), BF16)] * 2,
        micros=1,
    )


def packed_factor(plan, ints, which, pack):
    at = plan.items + SMALL * plan.number + 2 * which * plan.items
    matrix = jnp.concatenate([pack[at + h * plan.items : at + (h + 1) * plan.items, :] for h in range(2)], axis=1)
    return dense_factor(matrix, ints[which : which + 1, : plan.items], plan.number)


def gathered(plan, ints, which, c, refs):
    begins = starts(plan, ints, which, c)
    return tuple(jnp.concatenate([r[pl.ds(s, plan.width), :] for s in begins], axis=0) for r in refs)


def gathered_columns(plan, ints, which, c, refs):
    begins = starts(plan, ints, which, c)
    return tuple(jnp.concatenate([r[:, pl.ds(s, plan.width)] for s in begins], axis=1) for r in refs)


def block(plan, c):
    return slice(c * plan.width, (c + 1) * plan.width)


def beside(first, second, axis):
    return tuple(jnp.concatenate([x, y], axis=axis) for x, y in zip(first, second))


def negative(pair):
    return tuple(-x for x in pair)


def across(plan, ints, which, left, values, out, rows=None):
    if rows is None:
        rows = range(plan.number)
    width = plan.width
    out[...] = jnp.zeros_like(out)
    for i, c in enumerate(rows):
        product = dot3(left(i, c), split(values(c)), NN)
        for k, s in enumerate(starts(plan, ints, which, c)):
            at = pl.ds(s, width)
            out[:, at] = out[:, at] + product[:, k * width : (k + 1) * width]


def columns_of(pair, at):
    return tuple(x[:, at] for x in pair)


def upper_part(plan, ints, factor, inverse, values, upper, seen):
    pair = split(factor)
    across(plan, ints, 0, lambda i, c: columns_of(pair, block(plan, c)), lambda c: values[block(plan, c), :], seen)
    upper[...] = dot3(inverse, split(seen[...]), NN)


def weigh(plan, ints, values, gains, pack, gain_h, gain_l, weights):
    items = plan.items
    inverse = split(pack[:items, :])
    gain_h[...], gain_l[...] = split(dot3(split(gains), inverse, NT))
    for c in range(plan.number):
        weights[block(plan, c), :] = dot3(
            split(values[block(plan, c), :]), gathered(plan, ints, 1, c, (gain_h, gain_l)), NN
        )


def solve_vectors(plan, pack, factor, small):
    items, number = plan.items, plan.number
    tail = items
    vector = jnp.concatenate(
        [pack[tail + c * SMALL : tail + (c + 1) * SMALL, :] for c in range(number)], axis=1
    )
    zeta = pack[tail : tail + SMALL, :]
    residual = zeta[3:4, :] - mm(vector, factor, NT)[0:1, :]
    solved = mm(jnp.broadcast_to(residual, (SMALL, items)), pack[:tail, :], NT)
    small[0:1, :] = solved[0:1, :]
    small[1:2, :] = zeta[2:3, :]
    small[2:, :] = jnp.zeros((SMALL - 2, items), F32)
    return solved


def earlier_offsets(plan, ints, c, pack):
    tail = plan.items
    begins = [
        pl.multiple_of(tail + ints[1, plan.items + c * plan.per_row + k] * SMALL, SMALL)
        for k in range(plan.per_row)
    ]
    return [pack[pl.ds(s, SMALL), :] for s in begins]


def own_block(plan, info):
    start = info[0] * plan.panel
    return start // plan.width, pl.ds(pl.multiple_of(start, plan.panel), plan.panel)


def panel_dynamics(plan, info, ints, first, second, weights, upper_pair, out):
    width = plan.width
    c, mine = own_block(plan, info)
    left = split(second[mine, :])
    middle = [ints[1, plan.items + c * plan.per_row + k] for k in range(plan.per_row)]
    across(
        plan,
        ints,
        0,
        lambda i, c: columns_of(left, slice(i * width, (i + 1) * width)),
        lambda c: first[pl.ds(pl.multiple_of(c * width, width), width), :],
        out,
        middle,
    )
    out[...] = out[...] - dot3(split(weights[mine, :]), upper_pair, NN)


def level_step(plan, info, ints, even, odd, values, gains, pack):
    states, items = plan.states, plan.items

    def body(info, ints, ints_v, even, odd, values, gains, pack, first, weights, upper, small, *scratch):
        seen, gain_h, gain_l = scratch
        fill(plan, info, even, odd, first)
        factor = packed_factor(plan, ints_v, 1, pack)
        inverse = split(pack[:items, :])
        upper_part(plan, ints, factor, inverse, first, upper, seen)
        weigh(plan, ints, values, gains[...], pack, gain_h, gain_l, weights)
        solve_vectors(plan, pack, factor, small)

    return call(
        body,
        "level",
        [(states, plan.per_row * plan.width), (states, items), (items, states), (SMALL, items)],
        (info, ints, ints, even, odd, values, gains, pack),
        [SM, SM, VM, VM, VM, VM, VM, VM],
        scratch=[pltpu.VMEM((items, states), F32)] + [pltpu.VMEM((states, items), BF16)] * 2,
        micros=1,
    )


def later_upper_step(plan, info, ints, even, odd, pack):
    states, items = plan.states, plan.items

    def body(info, ints, ints_v, even, odd, pack, first, upper, seen):
        fill(plan, info, even, odd, first)
        factor = packed_factor(plan, ints_v, 1, pack)
        inverse = split(pack[:items, :])
        upper_part(plan, ints, factor, inverse, first, upper, seen)

    return call(
        body,
        "later_upper",
        [(states, plan.per_row * plan.width), (items, states)],
        (info, ints, ints, even, odd, pack),
        [SM, SM, VM, part(even.shape, 0), part(odd.shape, 0), VM],
        scratch=[pltpu.VMEM((items, states), F32)],
        micros=1,
    )


def later_level_step(plan, info, ints, even, odd, gain_even, gain_odd, first, upper, pack, cov):
    states, items, panel = plan.states, plan.items, plan.panel

    def body(info, ints, ints_v, even, odd, gain_even, gain_odd, first, upper, pack, cov, second, weights, small, out, dyn, offset, *scratch):
        gains, gain_h, gain_l, cov_h, cov_l, part_h, part_l = scratch
        fill(plan, info, even, odd, second)
        fill(plan, info, gain_even, gain_odd, gains)
        weigh(plan, ints, second, gains[...], pack, gain_h, gain_l, weights)
        cov_h[...], cov_l[...] = split(cov[...])
        upper_pair = split(upper[...])
        rest = split(dot3(upper_pair, (cov_h[...], cov_l[...]), NT))
        for c in range(plan.number):
            at = block(plan, c)
            taken = gathered_columns(plan, ints, 0, c, (cov_h, cov_l))
            part_h[at, :], part_l[at, :] = split(dot3(split(first[at, :]), taken, NT))
        for c in range(plan.number):
            at = block(plan, c)
            left = beside(split(second[at, :]), negative(split(weights[at, :])), 1)
            out[at, :] = dot3(left, beside(gathered(plan, ints, 1, c, (part_h, part_l)), rest, 0), NN)
        panel_dynamics(plan, info, ints, first, second, weights, upper_pair, dyn)
        factor = packed_factor(plan, ints_v, 1, pack)
        solved = solve_vectors(plan, pack, factor, small)
        c, mine = own_block(plan, info)
        left = jnp.concatenate(earlier_offsets(plan, ints, c, pack) + [solved], axis=1)
        right = jnp.concatenate([second[mine, :], weights[mine, :]], axis=1)
        own = pack[pl.ds(pl.multiple_of(items + c * SMALL, SMALL), SMALL), :]
        if panel % plan.width:
            own = pltpu.roll(own, plan.width - lax.rem(info[0] * panel, plan.width), 1)[:, :panel]
        offset[...] = mm(left, right, NT) + jnp.broadcast_to(own[1:2, :], (SMALL, panel))

    return call(
        body,
        "later_level",
        [
            (states, plan.per_row * plan.width),
            (states, items),
            (SMALL, items),
            (states, panel),
            (panel, states),
            (SMALL, panel),
        ],
        (info, ints, ints, even, odd, gain_even, gain_odd, first, upper, pack, cov),
        [SM, SM, VM, part(even.shape, 1), part(odd.shape, 1), VM, VM, VM, VM, VM, VM],
        scratch=[pltpu.VMEM((states, items), F32)]
        + [pltpu.VMEM((states, items), BF16)] * 2
        + [pltpu.VMEM((panel, states), BF16)] * 2
        + [pltpu.VMEM((states, panel), BF16)] * 2,
        micros=1,
    )


def ahead_step(plan, info, ints, later_ints, first, second, weights, upper, later_upper, later_pack):
    states, items, panel, width = plan.states, plan.items, plan.panel, plan.width

    def body(info, ints, ints_v, first, second, weights, upper, later_upper, pack, out, column, high, low):
        c, _ = own_block(plan, info)
        for r in range(plan.number):
            total = jnp.zeros((width, width), F32)
            for k in range(plan.per_row):
                here = ints[0, items + r * plan.per_row + k] == c
                total = total + jnp.where(here, first[block(plan, r), k * width : (k + 1) * width], 0.0)
            if panel % width:
                total = pltpu.roll(total, width - lax.rem(info[0] * panel, width), 1)
            column[block(plan, r), :] = total[:, :panel]
        high[...], low[...] = split(column[...])
        if panel % width:
            shift = states - info[0] * panel
            rest = split(pltpu.roll(upper[...], shift, 1)[:, :panel])
        else:
            rest = split(upper[:, own_block(plan, info)[1]])
        for r in range(plan.number):
            at = block(plan, r)
            left = beside(split(second[at, :]), negative(split(weights[at, :])), 1)
            column[at, :] = dot3(left, beside(gathered(plan, ints, 1, r, (high, low)), rest, 0), NN)
        factor = jnp.concatenate(
            [later_upper[...], packed_factor(plan, ints_v, 0, pack)], axis=0
        )
        out[...] = mm(factor, column[...], NN)

    return call(
        body,
        "ahead",
        [(2 * items, panel)],
        (info, ints, later_ints, first, second, weights, upper, later_upper, later_pack),
        [SM, SM, VM, VM, VM, VM, VM, VM, VM],
        scratch=[pltpu.VMEM((states, panel), F32)] + [pltpu.VMEM((states, panel), BF16)] * 2,
        micros=1,
    )[0]


def covariance_step(plan, info, ints, moved, values, weights, covariance, pack, small):
    states, panel, items = plan.states, plan.panel, plan.items
    tail = items

    def body(info, ints, moved, values, weights, cov, pack, small, out, offset, held_h, held_l):
        for a in range(plan.n):
            at = slice(a * panel, (a + 1) * panel)
            held_h[:, at], held_l[:, at] = split(moved[a])
        mine = own_block(plan, info)[1]
        solved = jnp.broadcast_to(small[0:1, :], (SMALL, items))
        last = split(jnp.concatenate([-weights[mine, :], solved], axis=0))
        for c in range(plan.number):
            at = block(plan, c)
            top = gathered_columns(plan, ints, 1, c, (held_h, held_l))
            low = split(jnp.concatenate(earlier_offsets(plan, ints, c, pack), axis=1))
            left = beside(beside(top, low, 0), last, 1)
            right = beside(split(values[at, :]), split(weights[at, :]), 1)
            result = dot3(left, right, NT)
            out[:, at] = result[:panel, :] + cov[0, :, at]
            own = pack[tail + c * SMALL : tail + (c + 1) * SMALL, :]
            offset[:, at] = result[panel:, :] + jnp.broadcast_to(own[1:2, :], (SMALL, items))

    return call(
        body,
        "covariance",
        [(panel, states), (SMALL, states)],
        (info, ints, moved, values, weights, covariance, pack, small),
        [SM, SM, VM, VM, VM, element(covariance.shape, 1), VM, VM],
        scratch=[pltpu.VMEM((panel, states), BF16)] * 2,
        grant=56,
        micros=1,
    )


def later_gain_step(plan, ints, cov, upper, pack):
    items = plan.items

    def body(ints, cov, upper, pack, out):
        factor = jnp.concatenate([upper[...], packed_factor(plan, ints, 0, pack)], axis=0)
        out[...] = mm(cov[...], factor, NT)

    return call(
        body,
        "later_gain",
        [(plan.panel, 2 * items)],
        (ints, cov, upper, pack),
        [VM, VM, VM, VM],
        micros=1,
    )[0]


def later_system_step(plan, info, ints, even, odd, upper, pack, first, second, weights):
    states, items = plan.states, plan.items
    rank = 2 * items

    def body(info, ints, ints_v, even, odd, upper, pack, first, second, weights, carried, inverse, *scratch):
        gain_h, gain_l, part_h, part_l = scratch
        for k in range(plan.n):
            at = plan.rows_of(info, k)
            gain_h[at, :], gain_l[at, :] = split((even, odd)[k % 2][k // 2])
        pair = (gain_h[...], gain_l[...])
        above = dot3(split(upper[...]), pair, NN)
        other = packed_factor(plan, ints_v, 0, pack)
        below = dot3(split(other), pair, NN)
        for c in range(plan.number):
            at = block(plan, c)
            taken = gathered(plan, ints, 0, c, (gain_h, gain_l))
            part_h[at, :], part_l[at, :] = split(dot3(split(first[at, :]), taken, NN))
        rest = split(above)
        for c in range(plan.number):
            at = block(plan, c)
            left = beside(split(second[at, :]), negative(split(weights[at, :])), 1)
            carried[at, :] = dot3(left, beside(gathered(plan, ints, 1, c, (part_h, part_l)), rest, 0), NN)
        top = inverse_factor(identity(items) + above[:, :items])
        lower = mm(below[:, :items], top, NT)
        bottom = inverse_factor(identity(items) + below[:, items:] - mm(lower, lower, NT))
        inverse[:items, :items] = top
        inverse[:items, items:] = jnp.zeros((items, items), F32)
        inverse[items:, :items] = -mm(bottom, mm(lower, top))
        inverse[items:, items:] = bottom

    return call(
        body,
        "later_system",
        [(states, rank), (rank, rank)],
        (info, ints, ints, even, odd, upper, pack, first, second, weights),
        [SM, SM, VM, VM, VM, VM, VM, VM, VM, VM],
        scratch=[pltpu.VMEM((states, rank), BF16)] * 4,
        grant=56,
        micros=15,
    )


def final_step(plan, info, ints, later_ints, own, later, covs, carried, inverse, moved, seen, pack, later_pack):
    states, items, panel, width, number = plan.states, plan.items, plan.panel, plan.width, plan.number
    rank = 2 * items

    def body(
        info, ints, later_ints, ints_v, later_ints_v,
        first, second, own_weights, own_upper, own_small, own_offset,
        later_first, later_second, later_weights, later_upper, later_small, later_dyn, later_offset,
        own_cov, later_cov, carried, inverse, moved, seen, pack, later_pack,
        out_dyn, out_off, out_cov, out_fac, out_info,
        weights, fac, held_h, held_l, part_h, part_l, dyn, half,
    ):
        mine = own_block(plan, info)[1]

        def own_columns(ref):
            if panel % 128 == 0:
                return ref[:, mine]
            return pltpu.roll(ref[...], states - info[0] * panel, 1)[:, :panel]

        fac[...] = packed_factor(plan, ints_v, 0, pack)
        last = [jnp.transpose(own_columns(own_upper)), jnp.transpose(own_columns(fac))]

        @pl.when(info[2] == 0)
        def _():
            panel_dynamics(plan, info, ints, first, second, own_weights, split(own_upper[...]), dyn)
            out_dyn[0] = dyn[...]
            out_off[0] = own_columns(own_offset)[0:1, :]
            out_cov[0] = own_cov[...]
            out_fac[0, :, :items] = last[0]
            out_fac[0, :, items:rank] = last[1]
            out_fac[0, :, rank:] = jnp.zeros((panel, rank), F32)
            zeta = jnp.concatenate([own_small[0:1, :], own_small[1:2, :]], axis=1)
            zeta = jnp.broadcast_to(zeta, (SMALL, rank))
            out_info[0] = mm(zeta, out_fac[0, :, :rank], NT)[0:1, :]

        @pl.when(info[2] == 1)
        def _():
            inverse_pair = split(inverse[...])
            weights[...] = dot3(split(carried[...]), inverse_pair, NT)
            own_weight = weights[mine, :]
            weight_pair = split(-own_weight)
            factor = jnp.concatenate(
                [later_upper[...], packed_factor(plan, later_ints_v, 0, later_pack)], axis=0
            )
            factor_pair = split(factor)
            left = later_dyn[...] + dot3(split(dot3(weight_pair, inverse_pair, NN)), factor_pair, NN)
            left_pair = split(left)
            across(
                plan, ints, 1, lambda i, c: columns_of(left_pair, block(plan, c)),
                lambda c: second[block(plan, c), :], half,
            )
            for a in range(plan.n):
                at = slice(a * panel, (a + 1) * panel)
                held_h[:, at], held_l[:, at] = split(moved[a])
            rest = negative(split(dot3((held_h[...], held_l[...]), split(later_upper[...]), NT)))
            for c in range(number):
                at = block(plan, c)
                taken = gathered_columns(plan, later_ints, 0, c, (held_h, held_l))
                part_h[:, at], part_l[:, at] = split(dot3(taken, split(later_first[at, :]), NT))
            rest = beside(rest, weight_pair, 1)
            middle = split(half[...])
            across(
                plan, ints, 0, lambda i, c: columns_of(middle, block(plan, c)),
                lambda c: first[block(plan, c), :], dyn,
            )
            for c in range(number):
                at = block(plan, c)
                taken = beside(gathered_columns(plan, later_ints, 1, c, (part_h, part_l)), rest, 1)
                right = jnp.concatenate([later_second[at, :], later_weights[at, :], weights[at, :]], axis=1)
                out_cov[0, :, at] = dot3(taken, split(right), NT) + later_cov[:, at]
            through = split(dot3(left_pair, split(own_weights[...]), NN))
            out_dyn[0] = dyn[...] - dot3(through, split(own_upper[...]), NN)
            residual = jnp.concatenate([later_small[0:1, :], later_small[1:2, :]], axis=1)
            offset = own_offset[...]
            residual = jnp.broadcast_to(residual, (SMALL, rank)) - dot3(split(offset), factor_pair, NT)
            solved = dot3(split(residual), inverse_pair, NT)
            gone = mm(offset, later_dyn[...], NT) + mm(solved, own_weight, NT)
            out_off[0] = gone[0:1, :] + later_offset[0:1, :]
            out_fac[0, :, :rank] = jnp.transpose(dot3(inverse_pair, split(seen[...]), NN))
            out_fac[0, :, rank : rank + items] = last[0]
            out_fac[0, :, rank + items :] = last[1]
            zeta = jnp.concatenate([solved[0:1, :], own_small[0:1, :], own_small[1:2, :]], axis=1)
            zeta = jnp.broadcast_to(zeta, (SMALL, 2 * rank))
            out_info[0] = mm(zeta, out_fac[0], NT)[0:1, :]

    return call(
        body,
        "final",
        [
            (1, panel, states),
            (1, 1, panel),
            (1, panel, states),
            (1, panel, 2 * rank),
            (1, 1, panel),
        ],
        (
            info, ints, later_ints, ints, later_ints, *own, *later, *covs,
            carried, inverse, moved, seen, pack, later_pack,
        ),
        [SM] * 3 + [VM] * 21 + [VM, VM],
        scratch=[
            pltpu.VMEM((states, rank), F32),
            pltpu.VMEM((items, states), F32),
        ]
        + [pltpu.VMEM((panel, states), BF16)] * 4
        + [pltpu.VMEM((panel, states), F32)] * 2,
        grant=56,
        micros=1,
    )


def per_device(mesh, dyn_pattern, dyn_values, offsets, covariance, obs_block, obs_matrix, obs_data):
    plan = Plan(mesh, dyn_pattern, dyn_values, obs_block, obs_matrix)
    here = lax.axis_index(PLANE)
    even_turn = 1 - lax.axis_index("tm") % 2
    info = jnp.stack([here, lax.axis_index("obs"), even_turn]).astype(jnp.int32)
    ints = jnp.concatenate([obs_block, dyn_pattern.reshape(2, -1)], axis=1)

    pieces = [obs_matrix] + [exchange(obs_matrix, "obs", k, plan.obs) for k in range(1, plan.obs)]
    later_ints = earlier(plan, ints)
    own_first, own_second = dyn_values[0], dyn_values[1]
    pieces, own_first, own_second = tie(pieces, own_first, own_second)
    later_values = earlier(plan, own_first)
    message, obs = gain_step(plan, info, obs_block, pieces, covariance, offsets, obs_data)
    gain_leg_one = first_leg(plan, message)
    gain_leg_one, own_second, own_first, later_ints = tie(gain_leg_one, own_second, own_first, later_ints)
    gain_even, gain_odd = second_leg(plan, gain_leg_one)
    later_gain_even = earlier(plan, gain_even)
    second_leg_one = first_leg(plan, own_second)
    gains, pack = system_step(plan, info, ints, gain_even, gain_odd, obs)
    pack, second_leg_one, own_first, later_values, later_gain_even = tie(
        pack, second_leg_one, own_first, later_values, later_gain_even
    )
    later_pack = earlier(plan, pack)
    second_even, second_odd = second_leg(plan, second_leg_one)
    later_second_even = earlier(plan, second_even)
    first_leg_one = first_leg(plan, own_first)

    spread, second = spread_step(plan, info, ints, second_even, second_odd, covariance)
    first_leg_one, second, later_values, later_pack, later_gain_even = tie(
        first_leg_one, second, later_values, later_pack, later_gain_even
    )
    moved = swap_blocks(plan, spread.reshape(plan.n, plan.panel, plan.panel))
    first_even, first_odd = second_leg(plan, first_leg_one)
    later_leg_one = first_leg(plan, later_values)
    later_gain_odd = other_core(plan, later_gain_even, gain_odd)
    first, weights, upper, small = level_step(plan, info, ints, first_even, first_odd, second, gains, pack)
    moved, weights, later_leg_one, later_second_even = tie(moved, weights, later_leg_one, later_second_even)
    later_even, later_odd = second_leg(plan, later_leg_one)
    later_second_odd = other_core(plan, later_second_even, second_odd)
    cov, offset = covariance_step(plan, info, ints, moved, second, weights, covariance, pack, small)
    own = (first, second, weights, upper, small, offset)

    later_first, later_upper = later_upper_step(plan, info, later_ints, later_even, later_odd, later_pack)
    gain = later_gain_step(plan, later_ints, cov, later_upper, later_pack)
    gain_leg_one = first_leg(plan, gain)
    later_second, later_weights, later_small, spread, later_dyn, later_offset = later_level_step(
        plan, info, later_ints, later_second_even, later_second_odd, later_gain_even, later_gain_odd,
        later_first, later_upper, later_pack, cov,
    )
    gain_leg_one, spread, cov = tie(gain_leg_one, spread, cov)
    later_cov = earlier(plan, cov)
    later = (later_first, later_second, later_weights, later_upper, later_small, later_dyn, later_offset)
    gain_even, gain_odd = second_leg(plan, gain_leg_one)
    moved = swap_blocks(plan, spread.reshape(plan.n, plan.panel, plan.panel))
    seen = ahead_step(plan, info, ints, later_ints, first, second, weights, upper, later_upper, later_pack)
    carried, inverse = later_system_step(
        plan, info, later_ints, gain_even, gain_odd, later_upper, later_pack,
        later_first, later_second, later_weights,
    )
    moved, later_cov, inverse = tie(moved, later_cov, inverse)
    dyn, off, cov, fac, information = final_step(
        plan, info, ints, later_ints, own, later, (cov, later_cov), carried, inverse, moved, seen, pack, later_pack
    )
    return dyn, off[:, 0], cov, fac, information[:, 0]


def solution(mesh):
    placed = (
        P("tm", None, None),
        P("tm", PLANE, None),
        P("tm", PLANE),
        P("tm", PLANE, None),
        P("tm", None),
        P("tm", "obs", None),
        P("tm", "obs"),
    )

    def run(*arrays):
        return per_device(mesh, *arrays)

    return jax.shard_map(
        run,
        mesh=mesh,
        in_specs=placed,
        out_specs=(
            P("tm", PLANE, None),
            P("tm", PLANE),
            P("tm", PLANE, None),
            P("tm", PLANE, None),
            P("tm", PLANE),
        ),
        check_vma=False,
    )
```

time: 190 us -> 136 us (0.72); the launches traced: 186 us -> 135 us
  Pallas kernels: 100 us -> 57 us
  waiting for transfers between devices: 44.2 us -> 20.5 us
  local copies, waits for them, and re-layouts: 5.4 us -> 13.3 us
  starting transfers between devices: 31.3 us -> 37.8 us
    pallas_call x11, Pallas kernels: 100 us -> 57 us  [call(): pl.pallas_call(body, name=name, grid=(1,), in_specs=specs, out_specs=[VM]...]
    ppermute x19 -> x25, waiting for transfers between devices: 35.8 us -> 8.19 us  [exchange(): return lax.ppermute(x, axes, [(a, a ^ mask) for a in range(size)])]
    unnamed x42 -> x80, local copies, waits for them, and re-layouts: 5.31 us -> 11.4 us
    ppermute x19 -> x25, starting transfers between devices: 17.5 us -> 21.8 us  [exchange(): return lax.ppermute(x, axes, [(a, a ^ mask) for a in range(size)])]
    ppermute x5 -> x6, waiting for transfers between devices: 8.41 us -> 12.3 us  [earlier(): return lax.ppermute(x, 'tm', [(i, i - 1) for i in range(1, plan.tm)])]
    ppermute x5 -> x6, starting transfers between devices: 6.45 us -> 7.91 us  [earlier(): return lax.ppermute(x, 'tm', [(i, i - 1) for i in range(1, plan.tm)])]
    another operation x4 -> x5, other arithmetic: 3.05 us -> 4.28 us  [second_leg(): even = jnp.stack(pieces)]
  transfers between devices with their start and end apart: 26 -> 33, of which waited for: 12 -> 7; matrix products, arithmetic and copies ran while one was open for 2% -> 3% of each run, Pallas kernels for 38% -> 30%
where the time goes in v2:
time: 136 us; the launch traced here: 135 us
  Pallas kernels  57 us (42%)
  starting transfers between devices  37.8 us (28%)
  waiting for transfers between devices  20.5 us (15%)
  local copies, waits for them, and re-layouts  13.3 us (10%)
  other arithmetic  4.83 us (4%)
  between operations  1.42 us (1%)
    pallas_call x11, Pallas kernels, call(): pl.pallas_call(body, name=name, grid=(1,), in_specs=specs, out_specs=[VM]...  57 us
    ppermute x25, starting transfers between devices, exchange(): return lax.ppermute(x, axes, [(a, a ^ mask) for a in range(size)])  21.8 us
    ppermute x6, waiting for transfers between devices, earlier(): return lax.ppermute(x, 'tm', [(i, i - 1) for i in range(1, plan.tm)])  12.3 us
    unnamed x80, local copies, waits for them, and re-layouts  11.4 us
    ppermute x25, waiting for transfers between devices, exchange(): return lax.ppermute(x, axes, [(a, a ^ mask) for a in range(size)])  8.19 us
    all_to_all x2, starting transfers between devices, swap_blocks(): return lax.all_to_all(x, PLANE, 0, 0, tiled=True)  8.03 us
    ppermute x6, starting transfers between devices, earlier(): return lax.ppermute(x, 'tm', [(i, i - 1) for i in range(1, plan.tm)])  7.91 us
    another operation x5, other arithmetic, second_leg(): even = jnp.stack(pieces)  4.28 us
  transfers between devices with their start and end apart: 33, of which 7 were waited for; matrix products, arithmetic and copies ran while one was open for 3% of the time, Pallas kernels for 30%

profile of v2, /device:TPU:0, one launch (start us, length us, event | category | flops | bytes accessed | tf_op | source)
XLA Modules:
  0.0 134.8 jit_solution(9053982854210935952)
XLA Ops:
  0.6 3.0 %collective-permute-start.1 = (f32[2,32,256]{2,1,0:T(8,128)}, f32[2,32,256]{2,1,0:T(8,128)S(1)}, u32[]{:S(2)}, u32[]{:S(2)}) collective-permute-start(f32[2,32,256]{2,1,0:T(8,128)} %refs_0_), channel_id=1, source_target_pairs={{0,2},{1,3},{2,0},{3,1},{4,6},{5,7},{6,4},{7,5},{8,10},{9,11},{10,... | collective-permute-start | bytes 196616 | tf_op jit(solution)/shard_map/ppermute | solution.py:150
  5.4 1.7 %slice_bitcast_fusion = (f32[128,384]{1,0:T(8,128)S(1)}, f32[128,384]{1,0:T(8,128)}) fusion(f32[2,128,384]{2,1,0:T(8,128)} %param.8), kind=kLoop, calls=%fused_computation.5 | loop fusion | bytes 786432 | tf_op jit(solution)/shard_map/squeeze | solution.py:747
  8.4 2.3 %gain.1 = (f32[136,128]{1,0:T(8,128)}, f32[2,128,256]{2,1,0:T(8,128)}) custom-call(s32[3]{0:T(128)} %pad_add_fusion.info, s32[2,128]{1,0:T(2,128)} %blocks.1, f32[2,32,256]{2,1,0:T(8,128)} %refs_0_, f32[2,32,256]{2,1,0:T(8,128)} %copy-done.37, f32[2,32,256]{2,1,0:T(8,128)} %copy-done.36, f32[2,32,256]{2,1,0:T(8,128)} %copy-done.38, f32[2,128,1024]{2,1,0:T(8,128)} %cov.3, ...), custom_call_target="tpu_custom_call" | custom-call | flops 1000000000 | bytes 1048576 | tf_op jit(solution)/shard_map/gain/pallas_call | solution.py:101
  10.6 2.9 %collective-permute-start.5 = (f32[136,128]{1,0:T(8,128)}, f32[136,128]{1,0:T(8,128)S(1)}, u32[]{:S(2)}, u32[]{:S(2)}) collective-permute-start(f32[136,128]{1,0:T(8,128)} %get-tuple-element.85), channel_id=1, source_target_pairs={{0,6},{1,7},{2,4},{3,5},{4,2},{5,3},{6,0},{7,1},{8,14},{9,15},{10,... | collective-permute-start | bytes 208904 | tf_op jit(solution)/shard_map/ppermute | solution.py:150
  15.4 4.2 %collective-permute-done.6.ints.ints_v.later_ints.later_ints_v = s32[2,152]{1,0:T(2,128)S(1)} collective-permute-done((s32[2,152]{1,0:T(2,128)S(1)}, s32[2,152]{1,0:T(2,128)S(1)}, u32[]{:S(2)}, u32[]{:S(2)}) %collective-permute-start.6) | collective-permute-done | bytes 1248 | tf_op jit(solution)/shard_map/ppermute | solution.py:185
  21.9 2.9 %collective-permute-start.10 = (f32[128,384]{1,0:T(8,128)S(1)}, f32[128,384]{1,0:T(8,128)S(1)}, u32[]{:S(2)}, u32[]{:S(2)}) collective-permute-start(f32[128,384]{1,0:T(8,128)S(1)} %get-tuple-element.94), channel_id=1, source_target_pairs={{0,6},{1,7},{2,4},{3,5},{4,2},{5,3},{6,0},{7,1},{8,14},{9,15},{10,... | collective-permute-start | bytes 589832 | tf_op jit(solution)/shard_map/ppermute | solution.py:150
  27.7 5.3 %system.1 = (f32[1024,128]{1,0:T(8,128)S(1)}, f32[704,128]{1,0:T(8,128)S(1)}) custom-call(s32[3]{0:T(128)S(1)} %copy-done.26, s32[2,152]{1,0:T(2,128)S(1)} %constant_dynamic-update-slice_fusion.ints.ints_v, f32[4,136,128]{2,1,0:T(8,128)S(1)} %pad_maximum_fusion.4.even, f32[4,136,128]{2,1,0:T(8,128)S(1)} %collective-permute-done.7.odd, ...), custom_call_target="tpu_custom_call" | custom-call | flops 20000000000 | bytes 1048576 | tf_op jit(solution)/shard_map/system/pallas_call | solution.py:101
  33.0 1.8 %collective-permute-done.9 = f32[128,384]{1,0:T(8,128)S(1)} collective-permute-done((f32[128,384]{1,0:T(8,128)S(1)}, f32[128,384]{1,0:T(8,128)S(1)}, u32[]{:S(2)}, u32[]{:S(2)}) %collective-permute-start.9) | collective-permute-done | bytes 196640 | tf_op jit(solution)/shard_map/ppermute | solution.py:150
  38.8 2.6 %collective-permute-start.15 = (f32[128,384]{1,0:T(8,128)}, f32[128,384]{1,0:T(8,128)S(1)}, u32[]{:S(2)}, u32[]{:S(2)}) collective-permute-start(f32[128,384]{1,0:T(8,128)} %get-tuple-element.102), channel_id=1, source_target_pairs={{0,6},{1,7},{2,4},{3,5},{4,2},{5,3},{6,0},{7,1},{8,14},{9,15},{10,... | collective-permute-start | bytes 589832 | tf_op jit(solution)/shard_map/ppermute | solution.py:150
  42.4 2.2 %spread.1 = (f32[1024,128]{1,0:T(8,128)S(1)}, f32[1024,384]{1,0:T(8,128)S(1)}) custom-call(s32[3]{0:T(128)S(1)} %copy-done.26, s32[2,152]{1,0:T(2,128)S(1)} %constant_dynamic-update-slice_fusion.ints.ints_v, f32[4,128,384]{2,1,0:T(8,128)} %pad_maximum_fusion.even, f32[4,128,384]{2,1,0:T(8,128)S(1)} %collective-permute-done.16.odd, f32[2,128,1024]{2,1,0:T(8,128)S(1)} %copy-done.16), custom_call_target="tpu_custom_call" | custom-call | flops 1000000000 | bytes 1048576 | tf_op jit(solution)/shard_map/spread/pallas_call | solution.py:101
  45.4 2.3 %collective-permute-done.15 = f32[128,384]{1,0:T(8,128)S(1)} collective-permute-done((f32[128,384]{1,0:T(8,128)}, f32[128,384]{1,0:T(8,128)S(1)}, u32[]{:S(2)}, u32[]{:S(2)}) %collective-permute-start.15) | collective-permute-done | bytes 196640 | tf_op jit(solution)/shard_map/ppermute | solution.py:150
  47.7 4.0 %collective-permute-done.14 = f32[128,384]{1,0:T(8,128)S(1)} collective-permute-done((f32[128,384]{1,0:T(8,128)}, f32[128,384]{1,0:T(8,128)S(1)}, u32[]{:S(2)}, u32[]{:S(2)}) %collective-permute-start.14) | collective-permute-done | bytes 196640 | tf_op jit(solution)/shard_map/ppermute | solution.py:150
  55.1 4.3 %all-to-all-start = ((f32[8,128,128]{2,1,0:T(8,128)}), f32[8,128,128]{2,1,0:T(8,128)}, u32[]{:S(2)}, u32[]{:S(2)}) async-start(f32[8,128,128]{2,1,0:T(8,128)} %bitcast.31), calls=%async_computation | async-start | bytes 1048576 | tf_op jit(solution)/shard_map/all_to_all | solution.py:181
  59.5 2.6 %collective-permute-start.21 = (f32[128,384]{1,0:T(8,128)}, f32[128,384]{1,0:T(8,128)}, u32[]{:S(2)}, u32[]{:S(2)}) collective-permute-start(f32[128,384]{1,0:T(8,128)} %collective-permute-done.11), channel_id=1, source_target_pairs={{0,6},{1,7},{2,4},{3,5},{4,2},{5,3},{6,0},{7,1},{8,14},{9,15},{10,... | collective-permute-start | bytes 589832 | tf_op jit(solution)/shard_map/ppermute | solution.py:150
  65.2 3.9 %level.1 = (f32[1024,384]{1,0:T(8,128)S(1)}, f32[1024,128]{1,0:T(8,128)S(1)}, f32[128,1024]{1,0:T(8,128)S(1)}, f32[8,128]{1,0:T(8,128)S(1)}) custom-call(s32[3]{0:T(128)S(1)} %copy-done.26, s32[2,152]{1,0:T(2,128)S(1)} %constant_dynamic-update-slice_fusion.ints.ints_v, s32[2,152]{1,0:T(2,128)S(1)} %constant_dynamic-update-slice_fusion.ints.ints_v, ...), custom_call_target="tpu_custom_call" | custom-call | flops 1000000000 | bytes 1048576 | tf_op jit(solution)/shard_map/level/pallas_call | solution.py:101
  71.4 5.2 %collective-permute-done.22.even = f32[4,128,384]{2,1,0:T(8,128)} collective-permute-done((f32[4,128,384]{2,1,0:T(8,128)}, f32[4,128,384]{2,1,0:T(8,128)}, u32[]{:S(2)}, u32[]{:S(2)}) %collective-permute-start.22) | collective-permute-done | bytes 786464 | tf_op jit(solution)/shard_map/ppermute | solution.py:185
  78.6 4.1 %covariance.1 = (f32[128,1024]{1,0:T(8,128)}, f32[8,1024]{1,0:T(8,128)}) custom-call(s32[3]{0:T(128)} %pad_add_fusion.info, s32[2,152]{1,0:T(2,128)} %copy-done.23, f32[8,128,128]{2,1,0:T(8,128)} %all-to-all-done.moved, f32[1024,384]{1,0:T(8,128)} %copy-done, f32[1024,128]{1,0:T(8,128)} %copy-done.4, f32[2,128,1024]{2,1,0:T(8,128)} %cov.3, ...), custom_call_target="tpu_custom_call" | custom-call | flops 1000000000 | bytes 1048576 | tf_op jit(solution)/shard_map/covariance/pallas_call | solution.py:101
  82.7 1.8 %later_upper.1 = (f32[1024,384]{1,0:T(8,128)S(1)}, f32[128,1024]{1,0:T(8,128)S(1)}) custom-call(s32[3]{0:T(128)S(1)} %copy-done.27, s32[2,152]{1,0:T(2,128)S(1)} %collective-permute-done.6.ints.ints_v.later_ints.later_ints_v, s32[2,152]{1,0:T(2,128)S(1)} %collective-permute-done.6.ints.ints_v.later_ints.later_ints_v, ...), custom_call_target="tpu_custom_call" | custom-call | flops 1000000000 | bytes 1048576 | tf_op jit(solution)/shard_map/later_upper/pallas_call | solution.py:101
  85.2 2.4 %collective-permute-start.28 = (f32[128,256]{1,0:T(8,128)S(1)}, f32[128,256]{1,0:T(8,128)S(1)}, u32[]{:S(2)}, u32[]{:S(2)}) collective-permute-start(f32[128,256]{1,0:T(8,128)S(1)} %later_gain.1), channel_id=1, source_target_pairs={{0,6},{1,7},{2,4},{3,5},{4,2},{5,3},{6,0},{7,1},{8,14},{9,15},{10,... | collective-permute-start | bytes 393224 | tf_op jit(solution)/shard_map/ppermute | solution.py:150
  88.8 6.5 %later_level.1 = (f32[1024,384]{1,0:T(8,128)S(1)}, f32[1024,128]{1,0:T(8,128)S(1)}, f32[8,128]{1,0:T(8,128)S(1)}, f32[1024,128]{1,0:T(8,128)}, f32[128,1024]{1,0:T(8,128)S(1)}, /*index=5*/f32[8,128]{1,0:T(8,128)S(1)}) custom-call(s32[3]{0:T(128)S(1)} %copy-done.27, s32[2,152]{1,0:T(2,128)S(1)} %collective-permute-done.6.ints.ints_v.later_ints.later_ints_v, ...), custom_call_target="tpu_custom_call" | custom-call | flops 1000000000 | bytes 1048576 | tf_op jit(solution)/shard_map/later_level/pallas_call | solution.py:101
  95.6 2.2 %ahead.1.seen = f32[256,128]{1,0:T(8,128)S(1)} custom-call(s32[3]{0:T(128)S(1)} %copy-done.27, s32[2,152]{1,0:T(2,128)S(1)} %copy-done.24, s32[2,152]{1,0:T(2,128)S(1)} %collective-permute-done.6.ints.ints_v.later_ints.later_ints_v, f32[1024,384]{1,0:T(8,128)S(1)} %get-tuple-element.108.first, f32[1024,384]{1,0:T(8,128)S(1)} %copy-done.1, ...), custom_call_target="tpu_custom_call" | custom-call | flops 1000000000 | bytes 1048576 | tf_op jit(solution)/shard_map/ahead/pallas_call | solution.py:101
  98.5 3.7 %all-to-all-start.1 = ((f32[8,128,128]{2,1,0:T(8,128)}), f32[8,128,128]{2,1,0:T(8,128)S(1)}, u32[]{:S(2)}, u32[]{:S(2)}) async-start(f32[8,128,128]{2,1,0:T(8,128)} %bitcast.22), calls=%async_computation.1 | async-start | bytes 1048576 | tf_op jit(solution)/shard_map/all_to_all | solution.py:181
  104.5 13.6 %later_system.1 = (f32[1024,256]{1,0:T(8,128)}, f32[256,256]{1,0:T(8,128)}) custom-call(s32[3]{0:T(128)} %pad_add_fusion.info, s32[2,152]{1,0:T(2,128)} %copy-done.25, s32[2,152]{1,0:T(2,128)} %copy-done.25, f32[4,128,256]{2,1,0:T(8,128)} %copy-done.34, f32[4,128,256]{2,1,0:T(8,128)} %copy-done.35, f32[128,1024]{1,0:T(8,128)} %copy-done.6, ...), custom_call_target="tpu_custom_call" | custom-call | flops 15000000512 | bytes 1048576 | tf_op jit(solution)/shard_map/later_system/pallas_call | solution.py:101
  120.1 14.4 %final.1 = (f32[1,128,1024]{2,1,0:T(8,128)}, f32[1,1,128]{2,1,0:T(1,128)}, f32[1,128,1024]{2,1,0:T(8,128)}, f32[1,128,512]{2,1,0:T(8,128)}, f32[1,1,128]{2,1,0:T(1,128)}) custom-call(s32[3]{0:T(128)} %pad_add_fusion.info, s32[2,152]{1,0:T(2,128)} %copy-done.23, s32[2,152]{1,0:T(2,128)} %copy-done.25, s32[2,152]{1,0:T(2,128)} %copy-done.23, ...), custom_call_target="tpu_custom_call" | custom-call | flops 1000000000 | bytes 1048576 | tf_op jit(solution)/shard_map/final/pallas_call | solution.py:101
  (142 shorter events, 33.3 us)
Async XLA Ops:
  10.6 9.0 %collective-permute-start.5 = (f32[136,128]{1,0:T(8,128)}, f32[136,128]{1,0:T(8,128)S(1)}, u32[]{:S(2)}, u32[]{:S(2)}) collective-permute-start(f32[136,128]{1,0:T(8,128)} %get-tuple-element.85), channel_id=1, source_target_pairs={{0,6},{1,7},{2,4},{3,5},{4,2},{5,3},{6,0},{7,1},{8,14},{9,15},{10,... | collective-permute-start | bytes 208904 | tf_op jit(solution)/shard_map/ppermute | solution.py:150
  20.6 12.4 %collective-permute-start.11 = (f32[128,384]{1,0:T(8,128)}, f32[128,384]{1,0:T(8,128)}, u32[]{:S(2)}, u32[]{:S(2)}) collective-permute-start(f32[128,384]{1,0:T(8,128)} %get-tuple-element.102), channel_id=1, source_target_pairs={{8,0},{16,8},{24,16},{9,1},{17,9},{25,17},{10,2},{18,10},{26,18},{... | collective-permute-start | bytes 589832 | tf_op jit(solution)/shard_map/ppermute | solution.py:185
  21.9 11.1 %collective-permute-start.10 = (f32[128,384]{1,0:T(8,128)S(1)}, f32[128,384]{1,0:T(8,128)S(1)}, u32[]{:S(2)}, u32[]{:S(2)}) collective-permute-start(f32[128,384]{1,0:T(8,128)S(1)} %get-tuple-element.94), channel_id=1, source_target_pairs={{0,6},{1,7},{2,4},{3,5},{4,2},{5,3},{6,0},{7,1},{8,14},{9,15},{10,... | collective-permute-start | bytes 589832 | tf_op jit(solution)/shard_map/ppermute | solution.py:150
  24.8 10.1 %collective-permute-start.9 = (f32[128,384]{1,0:T(8,128)S(1)}, f32[128,384]{1,0:T(8,128)S(1)}, u32[]{:S(2)}, u32[]{:S(2)}) collective-permute-start(f32[128,384]{1,0:T(8,128)S(1)} %get-tuple-element.94), channel_id=1, source_target_pairs={{0,4},{1,5},{2,6},{3,7},{4,0},{5,1},{6,2},{7,3},{8,12},{9,13},{10,... | collective-permute-start | bytes 589832 | tf_op jit(solution)/shard_map/ppermute | solution.py:150
  25.4 9.5 %collective-permute-start.8 = (f32[128,384]{1,0:T(8,128)S(1)}, f32[128,384]{1,0:T(8,128)S(1)}, u32[]{:S(2)}, u32[]{:S(2)}) collective-permute-start(f32[128,384]{1,0:T(8,128)S(1)} %get-tuple-element.94), channel_id=1, source_target_pairs={{0,2},{1,3},{2,0},{3,1},{4,6},{5,7},{6,4},{7,5},{8,10},{9,11},{10,... | collective-permute-start | bytes 589832 | tf_op jit(solution)/shard_map/ppermute | solution.py:150
  25.5 11.1 %collective-permute-start.12 = (f32[4,136,128]{2,1,0:T(8,128)S(1)}, f32[4,136,128]{2,1,0:T(8,128)}, u32[]{:S(2)}, u32[]{:S(2)}) collective-permute-start(f32[4,136,128]{2,1,0:T(8,128)S(1)} %pad_maximum_fusion.4.even), channel_id=1, source_target_pairs={{8,0},{16,8},{24,16},{9,1},{17,9},{25,17},{10,2},{18,10},{26,18},{... | collective-permute-start | bytes 835592 | tf_op jit(solution)/shard_map/ppermute | solution.py:185
  37.5 14.2 %collective-permute-start.17 = (f32[704,128]{1,0:T(8,128)S(1)}, f32[704,128]{1,0:T(8,128)S(1)}, u32[]{:S(2)}, u32[]{:S(2)}) collective-permute-start(f32[704,128]{1,0:T(8,128)S(1)} %get-tuple-element.100.pack), channel_id=1, source_target_pairs={{8,0},{16,8},{24,16},{9,1},{17,9},{25,17},{10,2},{18,10},{26,18},{... | collective-permute-start | bytes 1081352 | tf_op jit(solution)/shard_map/ppermute | solution.py:185
  38.8 8.9 %collective-permute-start.15 = (f32[128,384]{1,0:T(8,128)}, f32[128,384]{1,0:T(8,128)S(1)}, u32[]{:S(2)}, u32[]{:S(2)}) collective-permute-start(f32[128,384]{1,0:T(8,128)} %get-tuple-element.102), channel_id=1, source_target_pairs={{0,6},{1,7},{2,4},{3,5},{4,2},{5,3},{6,0},{7,1},{8,14},{9,15},{10,... | collective-permute-start | bytes 589832 | tf_op jit(solution)/shard_map/ppermute | solution.py:150
  41.4 10.3 %collective-permute-start.14 = (f32[128,384]{1,0:T(8,128)}, f32[128,384]{1,0:T(8,128)S(1)}, u32[]{:S(2)}, u32[]{:S(2)}) collective-permute-start(f32[128,384]{1,0:T(8,128)} %get-tuple-element.102), channel_id=1, source_target_pairs={{0,4},{1,5},{2,6},{3,7},{4,0},{5,1},{6,2},{7,3},{8,12},{9,13},{10,... | collective-permute-start | bytes 589832 | tf_op jit(solution)/shard_map/ppermute | solution.py:150
  42.0 9.8 %collective-permute-start.13 = (f32[128,384]{1,0:T(8,128)}, f32[128,384]{1,0:T(8,128)S(1)}, u32[]{:S(2)}, u32[]{:S(2)}) collective-permute-start(f32[128,384]{1,0:T(8,128)} %get-tuple-element.102), channel_id=1, source_target_pairs={{0,2},{1,3},{2,0},{3,1},{4,6},{5,7},{6,4},{7,5},{8,10},{9,11},{10,... | collective-permute-start | bytes 589832 | tf_op jit(solution)/shard_map/ppermute | solution.py:150
  52.9 10.2 %collective-permute-start.18 = (f32[4,128,384]{2,1,0:T(8,128)S(1)}, f32[4,128,384]{2,1,0:T(8,128)}, u32[]{:S(2)}, u32[]{:S(2)}) collective-permute-start(f32[4,128,384]{2,1,0:T(8,128)S(1)} %pad_maximum_fusion.1.even), channel_id=1, source_target_pairs={{0,1},{1,0},{2,3},{3,2},{4,5},{5,4},{6,7},{7,6},{8,9},{9,8},{10,11... | collective-permute-start | bytes 2359304 | tf_op jit(solution)/shard_map/ppermute | solution.py:150
  53.8 22.8 %collective-permute-start.22 = (f32[4,128,384]{2,1,0:T(8,128)}, f32[4,128,384]{2,1,0:T(8,128)}, u32[]{:S(2)}, u32[]{:S(2)}) collective-permute-start(f32[4,128,384]{2,1,0:T(8,128)} %pad_maximum_fusion.even), channel_id=1, source_target_pairs={{8,0},{16,8},{24,16},{9,1},{17,9},{25,17},{10,2},{18,10},{26,18},{... | collective-permute-start | bytes 2359304 | tf_op jit(solution)/shard_map/ppermute | solution.py:185
  55.1 21.5 %all-to-all-start = ((f32[8,128,128]{2,1,0:T(8,128)}), f32[8,128,128]{2,1,0:T(8,128)}, u32[]{:S(2)}, u32[]{:S(2)}) async-start(f32[8,128,128]{2,1,0:T(8,128)} %bitcast.31), calls=%async_computation | async-start | bytes 1048576 | tf_op jit(solution)/shard_map/all_to_all | solution.py:181
  59.5 17.1 %collective-permute-start.21 = (f32[128,384]{1,0:T(8,128)}, f32[128,384]{1,0:T(8,128)}, u32[]{:S(2)}, u32[]{:S(2)}) collective-permute-start(f32[128,384]{1,0:T(8,128)} %collective-permute-done.11), channel_id=1, source_target_pairs={{0,6},{1,7},{2,4},{3,5},{4,2},{5,3},{6,0},{7,1},{8,14},{9,15},{10,... | collective-permute-start | bytes 589832 | tf_op jit(solution)/shard_map/ppermute | solution.py:150
  62.1 14.5 %collective-permute-start.20 = (f32[128,384]{1,0:T(8,128)}, f32[128,384]{1,0:T(8,128)}, u32[]{:S(2)}, u32[]{:S(2)}) collective-permute-start(f32[128,384]{1,0:T(8,128)} %collective-permute-done.11), channel_id=1, source_target_pairs={{0,4},{1,5},{2,6},{3,7},{4,0},{5,1},{6,2},{7,3},{8,12},{9,13},{10,... | collective-permute-start | bytes 589832 | tf_op jit(solution)/shard_map/ppermute | solution.py:150
  62.7 14.0 %collective-permute-start.19 = (f32[128,384]{1,0:T(8,128)}, f32[128,384]{1,0:T(8,128)}, u32[]{:S(2)}, u32[]{:S(2)}) collective-permute-start(f32[128,384]{1,0:T(8,128)} %collective-permute-done.11), channel_id=1, source_target_pairs={{0,2},{1,3},{2,0},{3,1},{4,6},{5,7},{6,4},{7,5},{8,10},{9,11},{10,... | collective-permute-start | bytes 589832 | tf_op jit(solution)/shard_map/ppermute | solution.py:150
  78.0 10.8 %collective-permute-start.24 = (f32[4,128,384]{2,1,0:T(8,128)}, f32[4,128,384]{2,1,0:T(8,128)S(1)}, u32[]{:S(2)}, u32[]{:S(2)}) collective-permute-start(f32[4,128,384]{2,1,0:T(8,128)} %collective-permute-done.22.even), channel_id=1, source_target_pairs={{0,1},{1,0},{2,3},{3,2},{4,5},{5,4},{6,7},{7,6},{8,9},{9,8},{10,11... | collective-permute-start | bytes 2359304 | tf_op jit(solution)/shard_map/ppermute | solution.py:150
  78.5 10.3 %collective-permute-start.25 = (f32[4,136,128]{2,1,0:T(8,128)}, f32[4,136,128]{2,1,0:T(8,128)S(1)}, u32[]{:S(2)}, u32[]{:S(2)}) collective-permute-start(f32[4,136,128]{2,1,0:T(8,128)} %collective-permute-done.12.gain_even), channel_id=1, source_target_pairs={{0,1},{1,0},{2,3},{3,2},{4,5},{5,4},{6,7},{7,6},{8,9},{9,8},{10,11... | collective-permute-start | bytes 835592 | tf_op jit(solution)/shard_map/ppermute | solution.py:150
  85.2 10.1 %collective-permute-start.28 = (f32[128,256]{1,0:T(8,128)S(1)}, f32[128,256]{1,0:T(8,128)S(1)}, u32[]{:S(2)}, u32[]{:S(2)}) collective-permute-start(f32[128,256]{1,0:T(8,128)S(1)} %later_gain.1), channel_id=1, source_target_pairs={{0,6},{1,7},{2,4},{3,5},{4,2},{5,3},{6,0},{7,1},{8,14},{9,15},{10,... | collective-permute-start | bytes 393224 | tf_op jit(solution)/shard_map/ppermute | solution.py:150
  87.6 7.7 %collective-permute-start.27 = (f32[128,256]{1,0:T(8,128)S(1)}, f32[128,256]{1,0:T(8,128)S(1)}, u32[]{:S(2)}, u32[]{:S(2)}) collective-permute-start(f32[128,256]{1,0:T(8,128)S(1)} %later_gain.1), channel_id=1, source_target_pairs={{0,4},{1,5},{2,6},{3,7},{4,0},{5,1},{6,2},{7,3},{8,12},{9,13},{10,... | collective-permute-start | bytes 393224 | tf_op jit(solution)/shard_map/ppermute | solution.py:150
  88.2 7.1 %collective-permute-start.26 = (f32[128,256]{1,0:T(8,128)S(1)}, f32[128,256]{1,0:T(8,128)S(1)}, u32[]{:S(2)}, u32[]{:S(2)}) collective-permute-start(f32[128,256]{1,0:T(8,128)S(1)} %later_gain.1), channel_id=1, source_target_pairs={{0,2},{1,3},{2,0},{3,1},{4,6},{5,7},{6,4},{7,5},{8,10},{9,11},{10,... | collective-permute-start | bytes 393224 | tf_op jit(solution)/shard_map/ppermute | solution.py:150
  95.4 8.2 %collective-permute-start.30 = (f32[4,128,256]{2,1,0:T(8,128)S(1)}, f32[4,128,256]{2,1,0:T(8,128)S(1)}, u32[]{:S(2)}, u32[]{:S(2)}) collective-permute-start(f32[4,128,256]{2,1,0:T(8,128)S(1)} %pad_maximum_fusion.3.even), channel_id=1, source_target_pairs={{0,1},{1,0},{2,3},{3,2},{4,5},{5,4},{6,7},{7,6},{8,9},{9,8},{10,11... | collective-permute-start | bytes 1572872 | tf_op jit(solution)/shard_map/ppermute | solution.py:150
  98.5 19.6 %all-to-all-start.1 = ((f32[8,128,128]{2,1,0:T(8,128)}), f32[8,128,128]{2,1,0:T(8,128)S(1)}, u32[]{:S(2)}, u32[]{:S(2)}) async-start(f32[8,128,128]{2,1,0:T(8,128)} %bitcast.22), calls=%async_computation.1 | async-start | bytes 1048576 | tf_op jit(solution)/shard_map/all_to_all | solution.py:181
  102.1 17.2 %collective-permute-start.29 = (f32[128,1024]{1,0:T(8,128)S(1)}, f32[128,1024]{1,0:T(8,128)S(1)}, u32[]{:S(2)}, u32[]{:S(2)}) collective-permute-start(f32[128,1024]{1,0:T(8,128)S(1)} %copy-done.14), channel_id=1, source_target_pairs={{8,0},{16,8},{24,16},{9,1},{17,9},{25,17},{10,2},{18,10},{26,18},{... | collective-permute-start | bytes 1572872 | tf_op jit(solution)/shard_map/ppermute | solution.py:185
  (48 other events, 377.5 us)

commit v3 on v2

--- a/solution.py
+++ b/solution.py
@@ -111,6 +111,45 @@
     )(*args)
 
 
+def lazy(count, body):
+    def run(inputs, *refs):
+        sources = refs[inputs - count : inputs]
+        held = refs[len(refs) - count - 1 : len(refs) - 1]
+        sems = refs[-1]
+        copies = [pltpu.make_async_copy(a, b, sems.at[i]) for i, (a, b) in enumerate(zip(sources, held))]
+        for copy in copies:
+            copy.start()
+
+        def need(*wanted):
+            for i, ref in enumerate(held):
+                if i not in need.waited and any(ref is w for w in wanted):
+                    need.waited.add(i)
+                    copies[i].wait()
+
+        need.waited = set()
+
+        body(need, *refs[: inputs - count], *held, *refs[inputs : len(refs) - count - 1])
+
+    return run
+
+
+def lazy_call(body, name, out_shapes, args, specs, late, scratch=(), micros=1):
+    inputs = len(args) + len(late)
+    run = lazy(len(late), body)
+    return call(
+        lambda *refs: run(inputs, *refs),
+        name,
+        out_shapes,
+        (*args, *late),
+        list(specs) + [pl.BlockSpec(memory_space=pl.ANY)] * len(late),
+        scratch=list(scratch)
+        + [pltpu.VMEM(x.shape, x.dtype) for x in late]
+        + [pltpu.SemaphoreType.DMA((len(late),))],
+        micros=micros,
+        grant=56,
+    )
+
+
 VM = pl.BlockSpec(memory_space=pltpu.VMEM)
 SM = pl.BlockSpec(memory_space=pltpu.SMEM)
 
@@ -417,6 +456,7 @@
         (info, ints, ints, even, odd, values, gains, pack),
         [SM, SM, VM, VM, VM, VM, VM, VM],
         scratch=[pltpu.VMEM((items, states), F32)] + [pltpu.VMEM((states, items), BF16)] * 2,
+        grant=56,
         micros=1,
     )
 
@@ -444,7 +484,7 @@
 def later_level_step(plan, info, ints, even, odd, gain_even, gain_odd, first, upper, pack, cov):
     states, items, panel = plan.states, plan.items, plan.panel
 
-    def body(info, ints, ints_v, even, odd, gain_even, gain_odd, first, upper, pack, cov, second, weights, small, out, dyn, offset, *scratch):
+    def body(info, ints, even, odd, gain_even, gain_odd, first, upper, pack, cov, second, weights, out, *scratch):
         gains, gain_h, gain_l, cov_h, cov_l, part_h, part_l = scratch
         fill(plan, info, even, odd, second)
         fill(plan, info, gain_even, gain_odd, gains)
@@ -460,16 +500,6 @@
             at = block(plan, c)
             left = beside(split(second[at, :]), negative(split(weights[at, :])), 1)
             out[at, :] = dot3(left, beside(gathered(plan, ints, 1, c, (part_h, part_l)), rest, 0), NN)
-        panel_dynamics(plan, info, ints, first, second, weights, upper_pair, dyn)
-        factor = packed_factor(plan, ints_v, 1, pack)
-        solved = solve_vectors(plan, pack, factor, small)
-        c, mine = own_block(plan, info)
-        left = jnp.concatenate(earlier_offsets(plan, ints, c, pack) + [solved], axis=1)
-        right = jnp.concatenate([second[mine, :], weights[mine, :]], axis=1)
-        own = pack[pl.ds(pl.multiple_of(items + c * SMALL, SMALL), SMALL), :]
-        if panel % plan.width:
-            own = pltpu.roll(own, plan.width - lax.rem(info[0] * panel, plan.width), 1)[:, :panel]
-        offset[...] = mm(left, right, NT) + jnp.broadcast_to(own[1:2, :], (SMALL, panel))
 
     return call(
         body,
@@ -477,25 +507,27 @@
         [
             (states, plan.per_row * plan.width),
             (states, items),
-            (SMALL, items),
             (states, panel),
-            (panel, states),
-            (SMALL, panel),
         ],
-        (info, ints, ints, even, odd, gain_even, gain_odd, first, upper, pack, cov),
-        [SM, SM, VM, part(even.shape, 1), part(odd.shape, 1), VM, VM, VM, VM, VM, VM],
+        (info, ints, even, odd, gain_even, gain_odd, first, upper, pack, cov),
+        [SM, SM, part(even.shape, 1), part(odd.shape, 1), VM, VM, VM, VM, VM, VM],
         scratch=[pltpu.VMEM((states, items), F32)]
         + [pltpu.VMEM((states, items), BF16)] * 2
         + [pltpu.VMEM((panel, states), BF16)] * 2
         + [pltpu.VMEM((states, panel), BF16)] * 2,
+        grant=56,
         micros=1,
     )
 
 
-def ahead_step(plan, info, ints, later_ints, first, second, weights, upper, later_upper, later_pack):
+def ahead_step(plan, info, ints, later_ints, first, second, weights, upper, later_first, later_second, later_weights, later_upper, later_pack):
     states, items, panel, width = plan.states, plan.items, plan.panel, plan.width
 
-    def body(info, ints, ints_v, first, second, weights, upper, later_upper, pack, out, column, high, low):
+    def body(
+        info, ints, later_ints, ints_v, first, second, weights, upper,
+        later_first, later_second, later_weights, later_upper, pack,
+        out, dyn, small, offset, column, high, low,
+    ):
         c, _ = own_block(plan, info)
         for r in range(plan.number):
             total = jnp.zeros((width, width), F32)
@@ -519,16 +551,29 @@
             [later_upper[...], packed_factor(plan, ints_v, 0, pack)], axis=0
         )
         out[...] = mm(factor, column[...], NN)
+        panel_dynamics(plan, info, later_ints, later_first, later_second, later_weights, split(later_upper[...]), dyn)
+        solved = solve_vectors(plan, pack, packed_factor(plan, ints_v, 1, pack), small)
+        c, mine = own_block(plan, info)
+        left = jnp.concatenate(earlier_offsets(plan, later_ints, c, pack) + [solved], axis=1)
+        right = jnp.concatenate([later_second[mine, :], later_weights[mine, :]], axis=1)
+        own = pack[pl.ds(pl.multiple_of(items + c * SMALL, SMALL), SMALL), :]
+        if panel % width:
+            own = pltpu.roll(own, width - lax.rem(info[0] * panel, width), 1)[:, :panel]
+        offset[...] = mm(left, right, NT) + jnp.broadcast_to(own[1:2, :], (SMALL, panel))
 
     return call(
         body,
         "ahead",
-        [(2 * items, panel)],
-        (info, ints, later_ints, first, second, weights, upper, later_upper, later_pack),
-        [SM, SM, VM, VM, VM, VM, VM, VM, VM],
+        [(2 * items, panel), (panel, states), (SMALL, items), (SMALL, panel)],
+        (
+            info, ints, later_ints, later_ints, first, second, weights, upper,
+            later_first, later_second, later_weights, later_upper, later_pack,
+        ),
+        [SM, SM, SM] + [VM] * 10,
         scratch=[pltpu.VMEM((states, panel), F32)] + [pltpu.VMEM((states, panel), BF16)] * 2,
+        grant=56,
         micros=1,
-    )[0]
+    )
 
 
 def covariance_step(plan, info, ints, moved, values, weights, covariance, pack, small):
@@ -582,67 +627,68 @@
     )[0]
 
 
-def later_system_step(plan, info, ints, even, odd, upper, pack, first, second, weights):
-    states, items = plan.states, plan.items
+def finish_step(plan, info, ints, later_ints, own, later, covs, later_gains, moved, seen, pack, later_pack):
+    states, items, panel, number = plan.states, plan.items, plan.panel, plan.number
     rank = 2 * items
 
-    def body(info, ints, ints_v, even, odd, upper, pack, first, second, weights, carried, inverse, *scratch):
-        gain_h, gain_l, part_h, part_l = scratch
+    def body(
+        need, info, ints, later_ints, ints_v, later_ints_v, own_small, own_offset, later_small, later_offset,
+        even, odd, later_upper, later_pack, later_first, later_second, later_weights, moved, later_cov,
+        later_dyn, second, first, own_weights, own_upper, pack, seen, own_cov,
+        out_dyn, out_off, out_cov, out_fac, out_info,
+        gain_h, gain_l, part_h, part_l, held_h, held_l, side_h, side_l, carried, weights, fac, dyn, half,
+    ):
+        mine = own_block(plan, info)[1]
+
+        def own_columns(ref):
+            if panel % 128 == 0:
+                return ref[:, mine]
+            return pltpu.roll(ref[...], states - info[0] * panel, 1)[:, :panel]
+
+        need(even, odd, later_upper, later_pack, later_first, later_second, later_weights, moved, later_cov)
         for k in range(plan.n):
             at = plan.rows_of(info, k)
             gain_h[at, :], gain_l[at, :] = split((even, odd)[k % 2][k // 2])
         pair = (gain_h[...], gain_l[...])
-        above = dot3(split(upper[...]), pair, NN)
-        other = packed_factor(plan, ints_v, 0, pack)
-        below = dot3(split(other), pair, NN)
-        for c in range(plan.number):
+        factor = jnp.concatenate([later_upper[...], packed_factor(plan, later_ints_v, 0, later_pack)], axis=0)
+        factor_pair = split(factor)
+        system = dot3(factor_pair, pair, NN)
+        above, below = system[:items, :], system[items:, :]
+        top = inverse_factor(identity(items) + above[:, :items])
+        for c in range(number):
             at = block(plan, c)
-            taken = gathered(plan, ints, 0, c, (gain_h, gain_l))
-            part_h[at, :], part_l[at, :] = split(dot3(split(first[at, :]), taken, NN))
+            taken = gathered(plan, later_ints, 0, c, (gain_h, gain_l))
+            part_h[at, :], part_l[at, :] = split(dot3(split(later_first[at, :]), taken, NN))
+        for a in range(plan.n):
+            at = slice(a * panel, (a + 1) * panel)
+            held_h[:, at], held_l[:, at] = split(moved[a])
         rest = split(above)
-        for c in range(plan.number):
+        side_rest = negative(split(dot3((held_h[...], held_l[...]), split(later_upper[...]), NT)))
+        for c in range(number):
             at = block(plan, c)
-            left = beside(split(second[at, :]), negative(split(weights[at, :])), 1)
-            carried[at, :] = dot3(left, beside(gathered(plan, ints, 1, c, (part_h, part_l)), rest, 0), NN)
-        top = inverse_factor(identity(items) + above[:, :items])
+            taken = gathered_columns(plan, later_ints, 0, c, (held_h, held_l))
+            side_h[:, at], side_l[:, at] = split(dot3(taken, split(later_first[at, :]), NT))
         lower = mm(below[:, :items], top, NT)
         bottom = inverse_factor(identity(items) + below[:, items:] - mm(lower, lower, NT))
-        inverse[:items, :items] = top
-        inverse[:items, items:] = jnp.zeros((items, items), F32)
-        inverse[items:, :items] = -mm(bottom, mm(lower, top))
-        inverse[items:, items:] = bottom
-
-    return call(
-        body,
-        "later_system",
-        [(states, rank), (rank, rank)],
-        (info, ints, ints, even, odd, upper, pack, first, second, weights),
-        [SM, SM, VM, VM, VM, VM, VM, VM, VM, VM],
-        scratch=[pltpu.VMEM((states, rank), BF16)] * 4,
-        grant=56,
-        micros=15,
-    )
-
-
-def final_step(plan, info, ints, later_ints, own, later, covs, carried, inverse, moved, seen, pack, later_pack):
-    states, items, panel, width, number = plan.states, plan.items, plan.panel, plan.width, plan.number
-    rank = 2 * items
-
-    def body(
-        info, ints, later_ints, ints_v, later_ints_v,
-        first, second, own_weights, own_upper, own_small, own_offset,
-        later_first, later_second, later_weights, later_upper, later_small, later_dyn, later_offset,
-        own_cov, later_cov, carried, inverse, moved, seen, pack, later_pack,
-        out_dyn, out_off, out_cov, out_fac, out_info,
-        weights, fac, held_h, held_l, part_h, part_l, dyn, half,
-    ):
-        mine = own_block(plan, info)[1]
-
-        def own_columns(ref):
-            if panel % 128 == 0:
-                return ref[:, mine]
-            return pltpu.roll(ref[...], states - info[0] * panel, 1)[:, :panel]
-
+        for c in range(number):
+            at = block(plan, c)
+            own = split(later_second[at, :])
+            weight = split(later_weights[at, :])
+            carried[at, :] = dot3(
+                beside(own, negative(weight), 1), beside(gathered(plan, later_ints, 1, c, (part_h, part_l)), rest, 0), NN
+            )
+            taken = gathered_columns(plan, later_ints, 1, c, (side_h, side_l))
+            half[:, at] = dot3(beside(taken, side_rest, 1), beside(own, weight, 1), NT) + later_cov[:, at]
+        corner = -mm(bottom, mm(lower, top))
+        inverse = jnp.concatenate(
+            [
+                jnp.concatenate([top, jnp.zeros((items, items), F32)], axis=1),
+                jnp.concatenate([corner, bottom], axis=1),
+            ],
+            axis=0,
+        )
+        inverse_pair = split(inverse)
+        need(later_dyn, second, first, own_weights, own_upper, pack, seen, own_cov)
         fac[...] = packed_factor(plan, ints_v, 0, pack)
         last = [jnp.transpose(own_columns(own_upper)), jnp.transpose(own_columns(fac))]
 
@@ -661,39 +707,21 @@
 
         @pl.when(info[2] == 1)
         def _():
-            inverse_pair = split(inverse[...])
             weights[...] = dot3(split(carried[...]), inverse_pair, NT)
             own_weight = weights[mine, :]
             weight_pair = split(-own_weight)
-            factor = jnp.concatenate(
-                [later_upper[...], packed_factor(plan, later_ints_v, 0, later_pack)], axis=0
-            )
-            factor_pair = split(factor)
             left = later_dyn[...] + dot3(split(dot3(weight_pair, inverse_pair, NN)), factor_pair, NN)
             left_pair = split(left)
+            out_cov[0] = half[...] + dot3(weight_pair, split(weights[...]), NT)
             across(
                 plan, ints, 1, lambda i, c: columns_of(left_pair, block(plan, c)),
                 lambda c: second[block(plan, c), :], half,
             )
-            for a in range(plan.n):
-                at = slice(a * panel, (a + 1) * panel)
-                held_h[:, at], held_l[:, at] = split(moved[a])
-            rest = negative(split(dot3((held_h[...], held_l[...]), split(later_upper[...]), NT)))
-            for c in range(number):
-                at = block(plan, c)
-                taken = gathered_columns(plan, later_ints, 0, c, (held_h, held_l))
-                part_h[:, at], part_l[:, at] = split(dot3(taken, split(later_first[at, :]), NT))
-            rest = beside(rest, weight_pair, 1)
             middle = split(half[...])
             across(
                 plan, ints, 0, lambda i, c: columns_of(middle, block(plan, c)),
                 lambda c: first[block(plan, c), :], dyn,
             )
-            for c in range(number):
-                at = block(plan, c)
-                taken = beside(gathered_columns(plan, later_ints, 1, c, (part_h, part_l)), rest, 1)
-                right = jnp.concatenate([later_second[at, :], later_weights[at, :], weights[at, :]], axis=1)
-                out_cov[0, :, at] = dot3(taken, split(right), NT) + later_cov[:, at]
             through = split(dot3(left_pair, split(own_weights[...]), NN))
             out_dyn[0] = dyn[...] - dot3(through, split(own_upper[...]), NN)
             residual = jnp.concatenate([later_small[0:1, :], later_small[1:2, :]], axis=1)
@@ -709,9 +737,13 @@
             zeta = jnp.broadcast_to(zeta, (SMALL, 2 * rank))
             out_info[0] = mm(zeta, out_fac[0], NT)[0:1, :]
 
-    return call(
-        body,
-        "final",
+    even, odd = later_gains
+    first, second, own_weights, own_upper, own_small, own_offset = own
+    later_first, later_second, later_weights, later_upper, later_small, later_dyn, later_offset = later
+    own_cov, later_cov = covs
+    return lazy_call(
+        body,
+        "finish",
         [
             (1, panel, states),
             (1, 1, panel),
@@ -719,19 +751,18 @@
             (1, panel, 2 * rank),
             (1, 1, panel),
         ],
+        (info, ints, later_ints, ints, later_ints, own_small, own_offset, later_small, later_offset),
+        [SM] * 3 + [VM] * 6,
         (
-            info, ints, later_ints, ints, later_ints, *own, *later, *covs,
-            carried, inverse, moved, seen, pack, later_pack,
+            even, odd, later_upper, later_pack, later_first, later_second, later_weights, moved, later_cov,
+            later_dyn, second, first, own_weights, own_upper, pack, seen, own_cov,
         ),
-        [SM] * 3 + [VM] * 21 + [VM, VM],
-        scratch=[
-            pltpu.VMEM((states, rank), F32),
-            pltpu.VMEM((items, states), F32),
-        ]
+        scratch=[pltpu.VMEM((states, rank), BF16)] * 4
         + [pltpu.VMEM((panel, states), BF16)] * 4
+        + [pltpu.VMEM((states, rank), F32)] * 2
+        + [pltpu.VMEM((items, states), F32)]
         + [pltpu.VMEM((panel, states), F32)] * 2,
-        grant=56,
-        micros=1,
+        micros=20,
     )
 
 
@@ -771,32 +802,31 @@
     later_leg_one = first_leg(plan, later_values)
     later_gain_odd = other_core(plan, later_gain_even, gain_odd)
     first, weights, upper, small = level_step(plan, info, ints, first_even, first_odd, second, gains, pack)
-    moved, weights, later_leg_one, later_second_even = tie(moved, weights, later_leg_one, later_second_even)
+    moved, weights, later_leg_one = tie(moved, weights, later_leg_one)
     later_even, later_odd = second_leg(plan, later_leg_one)
+    cov, offset = covariance_step(plan, info, ints, moved, second, weights, covariance, pack, small)
+    later_second_even, offset = tie(later_second_even, offset)
     later_second_odd = other_core(plan, later_second_even, second_odd)
-    cov, offset = covariance_step(plan, info, ints, moved, second, weights, covariance, pack, small)
     own = (first, second, weights, upper, small, offset)
+    later_cov = earlier(plan, cov)
 
     later_first, later_upper = later_upper_step(plan, info, later_ints, later_even, later_odd, later_pack)
     gain = later_gain_step(plan, later_ints, cov, later_upper, later_pack)
     gain_leg_one = first_leg(plan, gain)
-    later_second, later_weights, later_small, spread, later_dyn, later_offset = later_level_step(
+    later_second, later_weights, spread = later_level_step(
         plan, info, later_ints, later_second_even, later_second_odd, later_gain_even, later_gain_odd,
         later_first, later_upper, later_pack, cov,
     )
-    gain_leg_one, spread, cov = tie(gain_leg_one, spread, cov)
-    later_cov = earlier(plan, cov)
+    moved = swap_blocks(plan, spread.reshape(plan.n, plan.panel, plan.panel))
+    gain_leg_one, later_weights = tie(gain_leg_one, later_weights)
+    gain_even, gain_odd = second_leg(plan, gain_leg_one)
+    seen, later_dyn, later_small, later_offset = ahead_step(
+        plan, info, ints, later_ints, first, second, weights, upper,
+        later_first, later_second, later_weights, later_upper, later_pack,
+    )
     later = (later_first, later_second, later_weights, later_upper, later_small, later_dyn, later_offset)
-    gain_even, gain_odd = second_leg(plan, gain_leg_one)
-    moved = swap_blocks(plan, spread.reshape(plan.n, plan.panel, plan.panel))
-    seen = ahead_step(plan, info, ints, later_ints, first, second, weights, upper, later_upper, later_pack)
-    carried, inverse = later_system_step(
-        plan, info, later_ints, gain_even, gain_odd, later_upper, later_pack,
-        later_first, later_second, later_weights,
-    )
-    moved, later_cov, inverse = tie(moved, later_cov, inverse)
-    dyn, off, cov, fac, information = final_step(
-        plan, info, ints, later_ints, own, later, (cov, later_cov), carried, inverse, moved, seen, pack, later_pack
+    dyn, off, cov, fac, information = finish_step(
+        plan, info, ints, later_ints, own, later, (cov, later_cov), (gain_even, gain_odd), moved, seen, pack, later_pack
     )
     return dyn, off[:, 0], cov, fac, information[:, 0]
 

time: 136 us -> 130 us (0.956)
  local copies, waits for them, and re-layouts: 13.3 us -> 8.56 us
  other arithmetic: 4.83 us -> 1.7 us
  Pallas kernels: 57 us -> 58.9 us
  waiting for transfers between devices: 20.5 us -> 21.9 us
    ppermute x6, waiting for transfers between devices: 12.3 us -> 6.44 us  [earlier(): return lax.ppermute(x, 'tm', [(i, i - 1) for i in range(1, plan.tm)])]
    ppermute x25, waiting for transfers between devices: 8.19 us -> 13.5 us  [exchange(): return lax.ppermute(x, axes, [(a, a ^ mask) for a in range(size)])]
    unnamed x80 -> x52, local copies, waits for them, and re-layouts: 11.4 us -> 7.42 us
    another operation x5, other arithmetic: 4.28 us -> 1.14 us  [second_leg(): even = jnp.stack(pieces)]
    all_to_all x2, waiting for transfers between devices: 0.01 us -> 1.95 us  [swap_blocks(): return lax.all_to_all(x, PLANE, 0, 0, tiled=True)]
    pallas_call x11 -> x10, Pallas kernels: 57 us -> 58.9 us  [call(): pl.pallas_call(body, name=name, grid=(1,), in_specs=specs, out_specs=[VM]...]
  transfers between devices with their start and end apart: 33 -> 33, of which waited for: 7 -> 10; matrix products, arithmetic and copies ran while one was open for 3% -> 3% of each run, Pallas kernels for 30% -> 26%
where the time goes in v3:
time: 130 us
  Pallas kernels  58.9 us (45%)
  starting transfers between devices  37.3 us (29%)
  waiting for transfers between devices  21.9 us (17%)
  local copies, waits for them, and re-layouts  8.56 us (7%)
  other arithmetic  1.7 us (1%)
    pallas_call x10, Pallas kernels, call(): pl.pallas_call(body, name=name, grid=(1,), in_specs=specs, out_specs=[VM]...  58.9 us
    ppermute x25, starting transfers between devices, exchange(): return lax.ppermute(x, axes, [(a, a ^ mask) for a in range(size)])  21.8 us
    ppermute x25, waiting for transfers between devices, exchange(): return lax.ppermute(x, axes, [(a, a ^ mask) for a in range(size)])  13.5 us
    ppermute x6, starting transfers between devices, earlier(): return lax.ppermute(x, 'tm', [(i, i - 1) for i in range(1, plan.tm)])  7.89 us
    all_to_all x2, starting transfers between devices, swap_blocks(): return lax.all_to_all(x, PLANE, 0, 0, tiled=True)  7.63 us
    unnamed x52, local copies, waits for them, and re-layouts  7.42 us
    ppermute x6, waiting for transfers between devices, earlier(): return lax.ppermute(x, 'tm', [(i, i - 1) for i in range(1, plan.tm)])  6.44 us
  transfers between devices with their start and end apart: 33, of which 10 were waited for; matrix products, arithmetic and copies ran while one was open for 3% of the time, Pallas kernels for 26%

profile of v3, /device:TPU:0, one launch (start us, length us, event | category | flops | bytes accessed | tf_op | source)
XLA Modules:
  0.0 129.6 jit_solution(18055310904239669583)
XLA Ops:
  0.6 3.0 %collective-permute-start.1 = (f32[2,32,256]{2,1,0:T(8,128)}, f32[2,32,256]{2,1,0:T(8,128)S(1)}, u32[]{:S(2)}, u32[]{:S(2)}) collective-permute-start(f32[2,32,256]{2,1,0:T(8,128)} %refs_0_), channel_id=1, source_target_pairs={{0,2},{1,3},{2,0},{3,1},{4,6},{5,7},{6,4},{7,5},{8,10},{9,11},{10,... | collective-permute-start | bytes 196616 | tf_op jit(solution)/shard_map/ppermute | solution.py:189
  8.2 2.2 %gain.1 = (f32[136,128]{1,0:T(8,128)}, f32[2,128,256]{2,1,0:T(8,128)}) custom-call(s32[3]{0:T(128)} %pad_add_fusion.info.refs_0_, s32[2,128]{1,0:T(2,128)} %blocks.1, f32[2,32,256]{2,1,0:T(8,128)} %refs_0_, f32[2,32,256]{2,1,0:T(8,128)} %copy-done.23, f32[2,32,256]{2,1,0:T(8,128)} %copy-done.22, f32[2,32,256]{2,1,0:T(8,128)} %copy-done.24, ...), custom_call_target="tpu_custom_call" | custom-call | flops 1000000000 | bytes 1048576 | tf_op jit(solution)/shard_map/gain/pallas_call | solution.py:101
  10.5 2.3 %collective-permute-start.5 = (f32[136,128]{1,0:T(8,128)}, f32[136,128]{1,0:T(8,128)S(1)}, u32[]{:S(2)}, u32[]{:S(2)}) collective-permute-start(f32[136,128]{1,0:T(8,128)} %get-tuple-element.81), channel_id=1, source_target_pairs={{0,6},{1,7},{2,4},{3,5},{4,2},{5,3},{6,0},{7,1},{8,14},{9,15},{10,... | collective-permute-start | bytes 208904 | tf_op jit(solution)/shard_map/ppermute | solution.py:189
  15.3 4.2 %collective-permute-done.6.ints.ints_v.later_ints.refs_2_.refs_4_ = s32[2,152]{1,0:T(2,128)S(1)} collective-permute-done((s32[2,152]{1,0:T(2,128)S(1)}, s32[2,152]{1,0:T(2,128)S(1)}, u32[]{:S(2)}, u32[]{:S(2)}) %collective-permute-start.6) | collective-permute-done | bytes 1248 | tf_op jit(solution)/shard_map/ppermute | solution.py:224
  21.8 2.4 %collective-permute-start.10 = (f32[128,384]{1,0:T(8,128)S(1)}, f32[128,384]{1,0:T(8,128)S(1)}, u32[]{:S(2)}, u32[]{:S(2)}) collective-permute-start(f32[128,384]{1,0:T(8,128)S(1)} %get-tuple-element.90), channel_id=1, source_target_pairs={{0,6},{1,7},{2,4},{3,5},{4,2},{5,3},{6,0},{7,1},{8,14},{9,15},{10,... | collective-permute-start | bytes 589832 | tf_op jit(solution)/shard_map/ppermute | solution.py:189
  27.6 5.3 %system.1 = (f32[1024,128]{1,0:T(8,128)S(1)}, f32[704,128]{1,0:T(8,128)S(1)}) custom-call(s32[3]{0:T(128)S(1)} %copy-done.10, s32[2,152]{1,0:T(2,128)S(1)} %constant_dynamic-update-slice_fusion.ints.ints_v.refs_1_.refs_3_, f32[4,136,128]{2,1,0:T(8,128)S(1)} %pad_maximum_fusion.4.even, f32[4,136,128]{2,1,0:T(8,128)S(1)} %collective-permute-done.7.odd, ...), custom_call_target="tpu_custom_call" | custom-call | flops 20000000000 | bytes 1048576 | tf_op jit(solution)/shard_map/system/pallas_call | solution.py:101
  34.2 1.8 %collective-permute-done.12.gain_even = f32[4,136,128]{2,1,0:T(8,128)S(1)} collective-permute-done((f32[4,136,128]{2,1,0:T(8,128)S(1)}, f32[4,136,128]{2,1,0:T(8,128)S(1)}, u32[]{:S(2)}, u32[]{:S(2)}) %collective-permute-start.12) | collective-permute-done | bytes 278560 | tf_op jit(solution)/shard_map/ppermute | solution.py:224
  37.5 2.4 %collective-permute-start.15 = (f32[128,384]{1,0:T(8,128)S(1)}, f32[128,384]{1,0:T(8,128)S(1)}, u32[]{:S(2)}, u32[]{:S(2)}) collective-permute-start(f32[128,384]{1,0:T(8,128)S(1)} %get-tuple-element.98), channel_id=1, source_target_pairs={{0,6},{1,7},{2,4},{3,5},{4,2},{5,3},{6,0},{7,1},{8,14},{9,15},{10,... | collective-permute-start | bytes 589832 | tf_op jit(solution)/shard_map/ppermute | solution.py:189
  41.1 2.5 %spread.1 = (f32[1024,128]{1,0:T(8,128)}, f32[1024,384]{1,0:T(8,128)S(1)}) custom-call(s32[3]{0:T(128)S(1)} %copy-done.10, s32[2,152]{1,0:T(2,128)S(1)} %constant_dynamic-update-slice_fusion.ints.ints_v.refs_1_.refs_3_, f32[4,128,384]{2,1,0:T(8,128)S(1)} %pad_maximum_fusion.even, f32[4,128,384]{2,1,0:T(8,128)S(1)} %collective-permute-done.16.odd, ...), custom_call_target="tpu_custom_call" | custom-call | flops 1000000000 | bytes 1048576 | tf_op jit(solution)/shard_map/spread/pallas_call | solution.py:101
  46.2 3.7 %collective-permute-done.14 = f32[128,384]{1,0:T(8,128)S(1)} collective-permute-done((f32[128,384]{1,0:T(8,128)S(1)}, f32[128,384]{1,0:T(8,128)S(1)}, u32[]{:S(2)}, u32[]{:S(2)}) %collective-permute-start.14) | collective-permute-done | bytes 196640 | tf_op jit(solution)/shard_map/ppermute | solution.py:189
  50.1 3.7 %all-to-all-start = ((f32[8,128,128]{2,1,0:T(8,128)}), f32[8,128,128]{2,1,0:T(8,128)S(1)}, u32[]{:S(2)}, u32[]{:S(2)}) async-start(f32[8,128,128]{2,1,0:T(8,128)} %bitcast.17), calls=%async_computation | async-start | bytes 1048576 | tf_op jit(solution)/shard_map/all_to_all | solution.py:220
  53.8 1.5 %collective-permute-start.19 = (f32[4,128,384]{2,1,0:T(8,128)S(1)}, f32[4,128,384]{2,1,0:T(8,128)}, u32[]{:S(2)}, u32[]{:S(2)}) collective-permute-start(f32[4,128,384]{2,1,0:T(8,128)S(1)} %pad_maximum_fusion.even), channel_id=1, source_target_pairs={{8,0},{16,8},{24,16},{9,1},{17,9},{25,17},{10,2},{18,10},{26,18},{... | collective-permute-start | bytes 2359304 | tf_op jit(solution)/shard_map/ppermute | solution.py:224
  55.3 3.0 %collective-permute-start.22 = (f32[128,384]{1,0:T(8,128)S(1)}, f32[128,384]{1,0:T(8,128)S(1)}, u32[]{:S(2)}, u32[]{:S(2)}) collective-permute-start(f32[128,384]{1,0:T(8,128)S(1)} %collective-permute-done.11), channel_id=1, source_target_pairs={{0,6},{1,7},{2,4},{3,5},{4,2},{5,3},{6,0},{7,1},{8,14},{9,15},{10,... | collective-permute-start | bytes 589832 | tf_op jit(solution)/shard_map/ppermute | solution.py:189
  58.9 5.8 %level.1 = (f32[1024,384]{1,0:T(8,128)}, f32[1024,128]{1,0:T(8,128)}, f32[128,1024]{1,0:T(8,128)}, f32[8,128]{1,0:T(8,128)}) custom-call(s32[3]{0:T(128)} %pad_add_fusion.info.refs_0_, s32[2,152]{1,0:T(2,128)} %copy-done.8, s32[2,152]{1,0:T(2,128)} %copy-done.8, f32[4,128,384]{2,1,0:T(8,128)} %copy-done.13, f32[4,128,384]{2,1,0:T(8,128)} %collective-permute-done.18.odd, ...), custom_call_target="tpu_custom_call" | custom-call | flops 1000000000 | bytes 1048576 | tf_op jit(solution)/shard_map/level/pallas_call | solution.py:101
  64.8 3.5 %collective-permute-done.22 = f32[128,384]{1,0:T(8,128)S(1)} collective-permute-done((f32[128,384]{1,0:T(8,128)S(1)}, f32[128,384]{1,0:T(8,128)S(1)}, u32[]{:S(2)}, u32[]{:S(2)}) %collective-permute-start.22) | collective-permute-done | bytes 196640 | tf_op jit(solution)/shard_map/ppermute | solution.py:189
  68.3 2.8 %collective-permute-done.21 = f32[128,384]{1,0:T(8,128)S(1)} collective-permute-done((f32[128,384]{1,0:T(8,128)S(1)}, f32[128,384]{1,0:T(8,128)S(1)}, u32[]{:S(2)}, u32[]{:S(2)}) %collective-permute-start.21) | collective-permute-done | bytes 196640 | tf_op jit(solution)/shard_map/ppermute | solution.py:189
  71.9 4.0 %covariance.1 = (f32[128,1024]{1,0:T(8,128)}, f32[8,1024]{1,0:T(8,128)}) custom-call(s32[3]{0:T(128)} %pad_add_fusion.info.refs_0_, s32[2,152]{1,0:T(2,128)} %copy-done.8, f32[8,128,128]{2,1,0:T(8,128)} %copy-done.14, f32[1024,384]{1,0:T(8,128)} %copy-done, f32[1024,128]{1,0:T(8,128)} %get-tuple-element.109.weights.refs_21_, f32[2,128,1024]{2,1,0:T(8,128)} %cov.3, ...), custom_call_target="tpu_custom_call" | custom-call | flops 1000000000 | bytes 1048576 | tf_op jit(solution)/shard_map/covariance/pallas_call | solution.py:101
  76.9 1.8 %later_upper.1 = (f32[1024,384]{1,0:T(8,128)S(1)}, f32[128,1024]{1,0:T(8,128)S(1)}) custom-call(s32[3]{0:T(128)S(1)} %copy-done.11, s32[2,152]{1,0:T(2,128)S(1)} %collective-permute-done.6.ints.ints_v.later_ints.refs_2_.refs_4_, s32[2,152]{1,0:T(2,128)S(1)} %collective-permute-done.6.ints.ints_v.later_ints.refs_2_.refs_4_, ...), custom_call_target="tpu_custom_call" | custom-call | flops 1000000000 | bytes 1048576 | tf_op jit(solution)/shard_map/later_upper/pallas_call | solution.py:101
  80.1 2.6 %collective-permute-start.28 = (f32[128,256]{1,0:T(8,128)S(1)}, f32[128,256]{1,0:T(8,128)S(1)}, u32[]{:S(2)}, u32[]{:S(2)}) collective-permute-start(f32[128,256]{1,0:T(8,128)S(1)} %later_gain.1), channel_id=1, source_target_pairs={{0,6},{1,7},{2,4},{3,5},{4,2},{5,3},{6,0},{7,1},{8,14},{9,15},{10,... | collective-permute-start | bytes 393224 | tf_op jit(solution)/shard_map/ppermute | solution.py:189
  85.8 6.8 %later_level.1 = (f32[1024,384]{1,0:T(8,128)}, f32[1024,128]{1,0:T(8,128)}, f32[1024,128]{1,0:T(8,128)}) custom-call(s32[3]{0:T(128)} %pad_add_fusion.info.refs_0_, s32[2,152]{1,0:T(2,128)} %copy-done.9, f32[4,128,384]{2,1,0:T(8,128)} %collective-permute-done.19.even, f32[4,128,384]{2,1,0:T(8,128)} %copy-done.15, f32[4,136,128]{2,1,0:T(8,128)} %copy-done.18, ...), custom_call_target="tpu_custom_call" | custom-call | flops 1000000000 | bytes 1048576 | tf_op jit(solution)/shard_map/later_level/pallas_call | solution.py:101
  92.8 3.9 %all-to-all-start.1 = ((f32[8,128,128]{2,1,0:T(8,128)}), f32[8,128,128]{2,1,0:T(8,128)S(1)}, u32[]{:S(2)}, u32[]{:S(2)}) async-start(f32[8,128,128]{2,1,0:T(8,128)} %bitcast.34), calls=%async_computation.1 | async-start | bytes 1048576 | tf_op jit(solution)/shard_map/all_to_all | solution.py:220
  96.7 6.9 %ahead.1 = (f32[256,128]{1,0:T(8,128)}, f32[128,1024]{1,0:T(8,128)}, f32[8,128]{1,0:T(8,128)}, f32[8,128]{1,0:T(8,128)}) custom-call(s32[3]{0:T(128)} %pad_add_fusion.info.refs_0_, s32[2,152]{1,0:T(2,128)} %copy-done.8, s32[2,152]{1,0:T(2,128)} %copy-done.9, s32[2,152]{1,0:T(2,128)} %copy-done.9, f32[1024,384]{1,0:T(8,128)} %get-tuple-element.112.first.refs_20_, ...), custom_call_target="tpu_custom_call" | custom-call | flops 1000000000 | bytes 1048576 | tf_op jit(solution)/shard_map/ahead/pallas_call | solution.py:101
  103.6 2.0 %all-to-all-done.1.refs_16_ = f32[8,128,128]{2,1,0:T(8,128)S(1)} async-done(((f32[8,128,128]{2,1,0:T(8,128)}), f32[8,128,128]{2,1,0:T(8,128)S(1)}, u32[]{:S(2)}, u32[]{:S(2)}) %all-to-all-start.1) | async-done | bytes 524320 | tf_op jit(solution)/shard_map/all_to_all | solution.py:220
  106.6 22.8 %finish.1 = (f32[1,128,1024]{2,1,0:T(8,128)}, f32[1,1,128]{2,1,0:T(1,128)}, f32[1,128,1024]{2,1,0:T(8,128)}, f32[1,128,512]{2,1,0:T(8,128)}, f32[1,1,128]{2,1,0:T(1,128)}) custom-call(s32[3]{0:T(128)} %pad_add_fusion.info.refs_0_, s32[2,152]{1,0:T(2,128)} %copy-done.8, s32[2,152]{1,0:T(2,128)} %copy-done.9, s32[2,152]{1,0:T(2,128)} %copy-done.8, ...), custom_call_target="tpu_custom_call" | custom-call | flops 20000000000 | bytes 1048576 | tf_op jit(solution)/shard_map/finish/pallas_call | solution.py:101
  (113 shorter events, 27.4 us)
Async XLA Ops:
  10.5 9.0 %collective-permute-start.5 = (f32[136,128]{1,0:T(8,128)}, f32[136,128]{1,0:T(8,128)S(1)}, u32[]{:S(2)}, u32[]{:S(2)}) collective-permute-start(f32[136,128]{1,0:T(8,128)} %get-tuple-element.81), channel_id=1, source_target_pairs={{0,6},{1,7},{2,4},{3,5},{4,2},{5,3},{6,0},{7,1},{8,14},{9,15},{10,... | collective-permute-start | bytes 208904 | tf_op jit(solution)/shard_map/ppermute | solution.py:189
  20.5 12.4 %collective-permute-start.11 = (f32[128,384]{1,0:T(8,128)S(1)}, f32[128,384]{1,0:T(8,128)S(1)}, u32[]{:S(2)}, u32[]{:S(2)}) collective-permute-start(f32[128,384]{1,0:T(8,128)S(1)} %get-tuple-element.98), channel_id=1, source_target_pairs={{8,0},{16,8},{24,16},{9,1},{17,9},{25,17},{10,2},{18,10},{26,18},{... | collective-permute-start | bytes 589832 | tf_op jit(solution)/shard_map/ppermute | solution.py:224
  21.8 11.1 %collective-permute-start.10 = (f32[128,384]{1,0:T(8,128)S(1)}, f32[128,384]{1,0:T(8,128)S(1)}, u32[]{:S(2)}, u32[]{:S(2)}) collective-permute-start(f32[128,384]{1,0:T(8,128)S(1)} %get-tuple-element.90), channel_id=1, source_target_pairs={{0,6},{1,7},{2,4},{3,5},{4,2},{5,3},{6,0},{7,1},{8,14},{9,15},{10,... | collective-permute-start | bytes 589832 | tf_op jit(solution)/shard_map/ppermute | solution.py:189
  24.1 10.1 %collective-permute-start.9 = (f32[128,384]{1,0:T(8,128)S(1)}, f32[128,384]{1,0:T(8,128)S(1)}, u32[]{:S(2)}, u32[]{:S(2)}) collective-permute-start(f32[128,384]{1,0:T(8,128)S(1)} %get-tuple-element.90), channel_id=1, source_target_pairs={{0,4},{1,5},{2,6},{3,7},{4,0},{5,1},{6,2},{7,3},{8,12},{9,13},{10,... | collective-permute-start | bytes 589832 | tf_op jit(solution)/shard_map/ppermute | solution.py:189
  24.7 9.6 %collective-permute-start.8 = (f32[128,384]{1,0:T(8,128)S(1)}, f32[128,384]{1,0:T(8,128)S(1)}, u32[]{:S(2)}, u32[]{:S(2)}) collective-permute-start(f32[128,384]{1,0:T(8,128)S(1)} %get-tuple-element.90), channel_id=1, source_target_pairs={{0,2},{1,3},{2,0},{3,1},{4,6},{5,7},{6,4},{7,5},{8,10},{9,11},{10,... | collective-permute-start | bytes 589832 | tf_op jit(solution)/shard_map/ppermute | solution.py:189
  25.3 10.7 %collective-permute-start.12 = (f32[4,136,128]{2,1,0:T(8,128)S(1)}, f32[4,136,128]{2,1,0:T(8,128)S(1)}, u32[]{:S(2)}, u32[]{:S(2)}) collective-permute-start(f32[4,136,128]{2,1,0:T(8,128)S(1)} %pad_maximum_fusion.4.even), channel_id=1, source_target_pairs={{8,0},{16,8},{24,16},{9,1},{17,9},{25,17},{10,2},{18,10},{26,18},{... | collective-permute-start | bytes 835592 | tf_op jit(solution)/shard_map/ppermute | solution.py:224
  36.2 13.8 %collective-permute-start.17 = (f32[704,128]{1,0:T(8,128)S(1)}, f32[704,128]{1,0:T(8,128)S(1)}, u32[]{:S(2)}, u32[]{:S(2)}) collective-permute-start(f32[704,128]{1,0:T(8,128)S(1)} %get-tuple-element.96.pack.refs_23_), channel_id=1, source_target_pairs={{8,0},{16,8},{24,16},{9,1},{17,9},{25,17},{10,2},{18,10},{26,18},{... | collective-permute-start | bytes 1081352 | tf_op jit(solution)/shard_map/ppermute | solution.py:224
  37.5 8.7 %collective-permute-start.15 = (f32[128,384]{1,0:T(8,128)S(1)}, f32[128,384]{1,0:T(8,128)S(1)}, u32[]{:S(2)}, u32[]{:S(2)}) collective-permute-start(f32[128,384]{1,0:T(8,128)S(1)} %get-tuple-element.98), channel_id=1, source_target_pairs={{0,6},{1,7},{2,4},{3,5},{4,2},{5,3},{6,0},{7,1},{8,14},{9,15},{10,... | collective-permute-start | bytes 589832 | tf_op jit(solution)/shard_map/ppermute | solution.py:189
  39.9 10.1 %collective-permute-start.14 = (f32[128,384]{1,0:T(8,128)S(1)}, f32[128,384]{1,0:T(8,128)S(1)}, u32[]{:S(2)}, u32[]{:S(2)}) collective-permute-start(f32[128,384]{1,0:T(8,128)S(1)} %get-tuple-element.98), channel_id=1, source_target_pairs={{0,4},{1,5},{2,6},{3,7},{4,0},{5,1},{6,2},{7,3},{8,12},{9,13},{10,... | collective-permute-start | bytes 589832 | tf_op jit(solution)/shard_map/ppermute | solution.py:189
  40.4 9.6 %collective-permute-start.13 = (f32[128,384]{1,0:T(8,128)S(1)}, f32[128,384]{1,0:T(8,128)S(1)}, u32[]{:S(2)}, u32[]{:S(2)}) collective-permute-start(f32[128,384]{1,0:T(8,128)S(1)} %get-tuple-element.98), channel_id=1, source_target_pairs={{0,2},{1,3},{2,0},{3,1},{4,6},{5,7},{6,4},{7,5},{8,10},{9,11},{10,... | collective-permute-start | bytes 589832 | tf_op jit(solution)/shard_map/ppermute | solution.py:189
  50.0 8.9 %collective-permute-start.18 = (f32[4,128,384]{2,1,0:T(8,128)S(1)}, f32[4,128,384]{2,1,0:T(8,128)}, u32[]{:S(2)}, u32[]{:S(2)}) collective-permute-start(f32[4,128,384]{2,1,0:T(8,128)S(1)} %pad_maximum_fusion.1.even), channel_id=1, source_target_pairs={{0,1},{1,0},{2,3},{3,2},{4,5},{5,4},{6,7},{7,6},{8,9},{9,8},{10,11... | collective-permute-start | bytes 2359304 | tf_op jit(solution)/shard_map/ppermute | solution.py:189
  50.1 21.0 %all-to-all-start = ((f32[8,128,128]{2,1,0:T(8,128)}), f32[8,128,128]{2,1,0:T(8,128)S(1)}, u32[]{:S(2)}, u32[]{:S(2)}) async-start(f32[8,128,128]{2,1,0:T(8,128)} %bitcast.17), calls=%async_computation | async-start | bytes 1048576 | tf_op jit(solution)/shard_map/all_to_all | solution.py:220
  53.8 22.6 %collective-permute-start.19 = (f32[4,128,384]{2,1,0:T(8,128)S(1)}, f32[4,128,384]{2,1,0:T(8,128)}, u32[]{:S(2)}, u32[]{:S(2)}) collective-permute-start(f32[4,128,384]{2,1,0:T(8,128)S(1)} %pad_maximum_fusion.even), channel_id=1, source_target_pairs={{8,0},{16,8},{24,16},{9,1},{17,9},{25,17},{10,2},{18,10},{26,18},{... | collective-permute-start | bytes 2359304 | tf_op jit(solution)/shard_map/ppermute | solution.py:224
  55.3 13.0 %collective-permute-start.22 = (f32[128,384]{1,0:T(8,128)S(1)}, f32[128,384]{1,0:T(8,128)S(1)}, u32[]{:S(2)}, u32[]{:S(2)}) collective-permute-start(f32[128,384]{1,0:T(8,128)S(1)} %collective-permute-done.11), channel_id=1, source_target_pairs={{0,6},{1,7},{2,4},{3,5},{4,2},{5,3},{6,0},{7,1},{8,14},{9,15},{10,... | collective-permute-start | bytes 589832 | tf_op jit(solution)/shard_map/ppermute | solution.py:189
  58.3 12.9 %collective-permute-start.21 = (f32[128,384]{1,0:T(8,128)S(1)}, f32[128,384]{1,0:T(8,128)S(1)}, u32[]{:S(2)}, u32[]{:S(2)}) collective-permute-start(f32[128,384]{1,0:T(8,128)S(1)} %collective-permute-done.11), channel_id=1, source_target_pairs={{0,4},{1,5},{2,6},{3,7},{4,0},{5,1},{6,2},{7,3},{8,12},{9,13},{10,... | collective-permute-start | bytes 589832 | tf_op jit(solution)/shard_map/ppermute | solution.py:189
  58.8 12.3 %collective-permute-start.20 = (f32[128,384]{1,0:T(8,128)S(1)}, f32[128,384]{1,0:T(8,128)S(1)}, u32[]{:S(2)}, u32[]{:S(2)}) collective-permute-start(f32[128,384]{1,0:T(8,128)S(1)} %collective-permute-done.11), channel_id=1, source_target_pairs={{0,2},{1,3},{2,0},{3,1},{4,6},{5,7},{6,4},{7,5},{8,10},{9,11},{10,... | collective-permute-start | bytes 589832 | tf_op jit(solution)/shard_map/ppermute | solution.py:189
  76.4 8.5 %collective-permute-start.24 = (f32[4,128,384]{2,1,0:T(8,128)}, f32[4,128,384]{2,1,0:T(8,128)S(1)}, u32[]{:S(2)}, u32[]{:S(2)}) collective-permute-start(f32[4,128,384]{2,1,0:T(8,128)} %collective-permute-done.19.even), channel_id=1, source_target_pairs={{0,1},{1,0},{2,3},{3,2},{4,5},{5,4},{6,7},{7,6},{8,9},{9,8},{10,11... | collective-permute-start | bytes 2359304 | tf_op jit(solution)/shard_map/ppermute | solution.py:189
  76.4 7.2 %collective-permute-start.25 = (f32[4,136,128]{2,1,0:T(8,128)S(1)}, f32[4,136,128]{2,1,0:T(8,128)S(1)}, u32[]{:S(2)}, u32[]{:S(2)}) collective-permute-start(f32[4,136,128]{2,1,0:T(8,128)S(1)} %collective-permute-done.12.gain_even), channel_id=1, source_target_pairs={{0,1},{1,0},{2,3},{3,2},{4,5},{5,4},{6,7},{7,6},{8,9},{9,8},{10,11... | collective-permute-start | bytes 835592 | tf_op jit(solution)/shard_map/ppermute | solution.py:189
  80.1 12.5 %collective-permute-start.28 = (f32[128,256]{1,0:T(8,128)S(1)}, f32[128,256]{1,0:T(8,128)S(1)}, u32[]{:S(2)}, u32[]{:S(2)}) collective-permute-start(f32[128,256]{1,0:T(8,128)S(1)} %later_gain.1), channel_id=1, source_target_pairs={{0,6},{1,7},{2,4},{3,5},{4,2},{5,3},{6,0},{7,1},{8,14},{9,15},{10,... | collective-permute-start | bytes 393224 | tf_op jit(solution)/shard_map/ppermute | solution.py:189
  82.7 10.0 %collective-permute-start.27 = (f32[128,256]{1,0:T(8,128)S(1)}, f32[128,256]{1,0:T(8,128)S(1)}, u32[]{:S(2)}, u32[]{:S(2)}) collective-permute-start(f32[128,256]{1,0:T(8,128)S(1)} %later_gain.1), channel_id=1, source_target_pairs={{0,4},{1,5},{2,6},{3,7},{4,0},{5,1},{6,2},{7,3},{8,12},{9,13},{10,... | collective-permute-start | bytes 393224 | tf_op jit(solution)/shard_map/ppermute | solution.py:189
  83.2 9.4 %collective-permute-start.26 = (f32[128,256]{1,0:T(8,128)S(1)}, f32[128,256]{1,0:T(8,128)S(1)}, u32[]{:S(2)}, u32[]{:S(2)}) collective-permute-start(f32[128,256]{1,0:T(8,128)S(1)} %later_gain.1), channel_id=1, source_target_pairs={{0,2},{1,3},{2,0},{3,1},{4,6},{5,7},{6,4},{7,5},{8,10},{9,11},{10,... | collective-permute-start | bytes 393224 | tf_op jit(solution)/shard_map/ppermute | solution.py:189
  83.6 20.0 %collective-permute-start.30 = (f32[128,1024]{1,0:T(8,128)S(1)}, f32[128,1024]{1,0:T(8,128)S(1)}, u32[]{:S(2)}, u32[]{:S(2)}) collective-permute-start(f32[128,1024]{1,0:T(8,128)S(1)} %copy-done.6), channel_id=1, source_target_pairs={{8,0},{16,8},{24,16},{9,1},{17,9},{25,17},{10,2},{18,10},{26,18},{... | collective-permute-start | bytes 1572872 | tf_op jit(solution)/shard_map/ppermute | solution.py:224
  92.7 12.9 %collective-permute-start.29 = (f32[4,128,256]{2,1,0:T(8,128)S(1)}, f32[4,128,256]{2,1,0:T(8,128)S(1)}, u32[]{:S(2)}, u32[]{:S(2)}) collective-permute-start(f32[4,128,256]{2,1,0:T(8,128)S(1)} %pad_maximum_fusion.3.refs_9_), channel_id=1, source_target_pairs={{0,1},{1,0},{2,3},{3,2},{4,5},{5,4},{6,7},{7,6},{8,9},{9,8},{10,11... | collective-permute-start | bytes 1572872 | tf_op jit(solution)/shard_map/ppermute | solution.py:189
  92.8 12.8 %all-to-all-start.1 = ((f32[8,128,128]{2,1,0:T(8,128)}), f32[8,128,128]{2,1,0:T(8,128)S(1)}, u32[]{:S(2)}, u32[]{:S(2)}) async-start(f32[8,128,128]{2,1,0:T(8,128)} %bitcast.34), calls=%async_computation.1 | async-start | bytes 1048576 | tf_op jit(solution)/shard_map/all_to_all | solution.py:220
  (34 other events, 289.0 us)

commit v4 on v3

--- a/solution.py
+++ b/solution.py
@@ -645,7 +645,7 @@
                 return ref[:, mine]
             return pltpu.roll(ref[...], states - info[0] * panel, 1)[:, :panel]
 
-        need(even, odd, later_upper, later_pack, later_first, later_second, later_weights, moved, later_cov)
+        need(even, odd, later_upper, later_pack)
         for k in range(plan.n):
             at = plan.rows_of(info, k)
             gain_h[at, :], gain_l[at, :] = split((even, odd)[k % 2][k // 2])
@@ -654,6 +654,7 @@
         factor_pair = split(factor)
         system = dot3(factor_pair, pair, NN)
         above, below = system[:items, :], system[items:, :]
+        need(later_first, later_second, later_weights, moved, later_cov)
         top = inverse_factor(identity(items) + above[:, :items])
         for c in range(number):
             at = block(plan, c)

time: 130 us -> 129 us (level)
  no operation moved by 1% of the time
where the time goes in v4:
time: 129 us
  Pallas kernels  57.9 us (45%)
  starting transfers between devices  37.3 us (29%)
  waiting for transfers between devices  21.9 us (17%)
  local copies, waits for them, and re-layouts  8.56 us (7%)
  other arithmetic  1.7 us (1%)
    pallas_call x10, Pallas kernels, call(): pl.pallas_call(body, name=name, grid=(1,), in_specs=specs, out_specs=[VM]...  57.9 us
    ppermute x25, starting transfers between devices, exchange(): return lax.ppermute(x, axes, [(a, a ^ mask) for a in range(size)])  21.8 us
    ppermute x25, waiting for transfers between devices, exchange(): return lax.ppermute(x, axes, [(a, a ^ mask) for a in range(size)])  13.5 us
    ppermute x6, starting transfers between devices, earlier(): return lax.ppermute(x, 'tm', [(i, i - 1) for i in range(1, plan.tm)])  7.89 us
    all_to_all x2, starting transfers between devices, swap_blocks(): return lax.all_to_all(x, PLANE, 0, 0, tiled=True)  7.62 us
    unnamed x52, local copies, waits for them, and re-layouts  7.42 us
    ppermute x6, waiting for transfers between devices, earlier(): return lax.ppermute(x, 'tm', [(i, i - 1) for i in range(1, plan.tm)])  6.45 us
  transfers between devices with their start and end apart: 33, of which 10 were waited for; matrix products, arithmetic and copies ran while one was open for 3% of the time, Pallas kernels for 26%

profile of v4, /device:TPU:0, one launch (start us, length us, event | category | flops | bytes accessed | tf_op | source)
XLA Modules:
  0.0 128.7 jit_solution(15136811761067209528)
XLA Ops:
  0.6 3.0 %collective-permute-start.1 = (f32[2,32,256]{2,1,0:T(8,128)}, f32[2,32,256]{2,1,0:T(8,128)S(1)}, u32[]{:S(2)}, u32[]{:S(2)}) collective-permute-start(f32[2,32,256]{2,1,0:T(8,128)} %refs_0_), channel_id=1, source_target_pairs={{0,2},{1,3},{2,0},{3,1},{4,6},{5,7},{6,4},{7,5},{8,10},{9,11},{10,... | collective-permute-start | bytes 196616 | tf_op jit(solution)/shard_map/ppermute | solution.py:189
  8.2 2.2 %gain.1 = (f32[136,128]{1,0:T(8,128)}, f32[2,128,256]{2,1,0:T(8,128)}) custom-call(s32[3]{0:T(128)} %pad_add_fusion.info.refs_0_, s32[2,128]{1,0:T(2,128)} %blocks.1, f32[2,32,256]{2,1,0:T(8,128)} %refs_0_, f32[2,32,256]{2,1,0:T(8,128)} %copy-done.23, f32[2,32,256]{2,1,0:T(8,128)} %copy-done.22, f32[2,32,256]{2,1,0:T(8,128)} %copy-done.24, ...), custom_call_target="tpu_custom_call" | custom-call | flops 1000000000 | bytes 1048576 | tf_op jit(solution)/shard_map/gain/pallas_call | solution.py:101
  10.5 2.3 %collective-permute-start.5 = (f32[136,128]{1,0:T(8,128)}, f32[136,128]{1,0:T(8,128)S(1)}, u32[]{:S(2)}, u32[]{:S(2)}) collective-permute-start(f32[136,128]{1,0:T(8,128)} %get-tuple-element.81), channel_id=1, source_target_pairs={{0,6},{1,7},{2,4},{3,5},{4,2},{5,3},{6,0},{7,1},{8,14},{9,15},{10,... | collective-permute-start | bytes 208904 | tf_op jit(solution)/shard_map/ppermute | solution.py:189
  15.3 4.2 %collective-permute-done.6.ints.ints_v.later_ints.refs_2_.refs_4_ = s32[2,152]{1,0:T(2,128)S(1)} collective-permute-done((s32[2,152]{1,0:T(2,128)S(1)}, s32[2,152]{1,0:T(2,128)S(1)}, u32[]{:S(2)}, u32[]{:S(2)}) %collective-permute-start.6) | collective-permute-done | bytes 1248 | tf_op jit(solution)/shard_map/ppermute | solution.py:224
  21.8 2.4 %collective-permute-start.10 = (f32[128,384]{1,0:T(8,128)S(1)}, f32[128,384]{1,0:T(8,128)S(1)}, u32[]{:S(2)}, u32[]{:S(2)}) collective-permute-start(f32[128,384]{1,0:T(8,128)S(1)} %get-tuple-element.90), channel_id=1, source_target_pairs={{0,6},{1,7},{2,4},{3,5},{4,2},{5,3},{6,0},{7,1},{8,14},{9,15},{10,... | collective-permute-start | bytes 589832 | tf_op jit(solution)/shard_map/ppermute | solution.py:189
  27.6 5.3 %system.1 = (f32[1024,128]{1,0:T(8,128)S(1)}, f32[704,128]{1,0:T(8,128)S(1)}) custom-call(s32[3]{0:T(128)S(1)} %copy-done.10, s32[2,152]{1,0:T(2,128)S(1)} %constant_dynamic-update-slice_fusion.ints.ints_v.refs_1_.refs_3_, f32[4,136,128]{2,1,0:T(8,128)S(1)} %pad_maximum_fusion.4.even, f32[4,136,128]{2,1,0:T(8,128)S(1)} %collective-permute-done.7.odd, ...), custom_call_target="tpu_custom_call" | custom-call | flops 20000000000 | bytes 1048576 | tf_op jit(solution)/shard_map/system/pallas_call | solution.py:101
  34.2 1.8 %collective-permute-done.12.gain_even = f32[4,136,128]{2,1,0:T(8,128)S(1)} collective-permute-done((f32[4,136,128]{2,1,0:T(8,128)S(1)}, f32[4,136,128]{2,1,0:T(8,128)S(1)}, u32[]{:S(2)}, u32[]{:S(2)}) %collective-permute-start.12) | collective-permute-done | bytes 278560 | tf_op jit(solution)/shard_map/ppermute | solution.py:224
  37.5 2.4 %collective-permute-start.15 = (f32[128,384]{1,0:T(8,128)S(1)}, f32[128,384]{1,0:T(8,128)S(1)}, u32[]{:S(2)}, u32[]{:S(2)}) collective-permute-start(f32[128,384]{1,0:T(8,128)S(1)} %get-tuple-element.98), channel_id=1, source_target_pairs={{0,6},{1,7},{2,4},{3,5},{4,2},{5,3},{6,0},{7,1},{8,14},{9,15},{10,... | collective-permute-start | bytes 589832 | tf_op jit(solution)/shard_map/ppermute | solution.py:189
  41.1 2.5 %spread.1 = (f32[1024,128]{1,0:T(8,128)}, f32[1024,384]{1,0:T(8,128)S(1)}) custom-call(s32[3]{0:T(128)S(1)} %copy-done.10, s32[2,152]{1,0:T(2,128)S(1)} %constant_dynamic-update-slice_fusion.ints.ints_v.refs_1_.refs_3_, f32[4,128,384]{2,1,0:T(8,128)S(1)} %pad_maximum_fusion.even, f32[4,128,384]{2,1,0:T(8,128)S(1)} %collective-permute-done.16.odd, ...), custom_call_target="tpu_custom_call" | custom-call | flops 1000000000 | bytes 1048576 | tf_op jit(solution)/shard_map/spread/pallas_call | solution.py:101
  46.2 3.7 %collective-permute-done.14 = f32[128,384]{1,0:T(8,128)S(1)} collective-permute-done((f32[128,384]{1,0:T(8,128)S(1)}, f32[128,384]{1,0:T(8,128)S(1)}, u32[]{:S(2)}, u32[]{:S(2)}) %collective-permute-start.14) | collective-permute-done | bytes 196640 | tf_op jit(solution)/shard_map/ppermute | solution.py:189
  50.1 3.7 %all-to-all-start = ((f32[8,128,128]{2,1,0:T(8,128)}), f32[8,128,128]{2,1,0:T(8,128)S(1)}, u32[]{:S(2)}, u32[]{:S(2)}) async-start(f32[8,128,128]{2,1,0:T(8,128)} %bitcast.17), calls=%async_computation | async-start | bytes 1048576 | tf_op jit(solution)/shard_map/all_to_all | solution.py:220
  53.8 1.5 %collective-permute-start.19 = (f32[4,128,384]{2,1,0:T(8,128)S(1)}, f32[4,128,384]{2,1,0:T(8,128)}, u32[]{:S(2)}, u32[]{:S(2)}) collective-permute-start(f32[4,128,384]{2,1,0:T(8,128)S(1)} %pad_maximum_fusion.even), channel_id=1, source_target_pairs={{8,0},{16,8},{24,16},{9,1},{17,9},{25,17},{10,2},{18,10},{26,18},{... | collective-permute-start | bytes 2359304 | tf_op jit(solution)/shard_map/ppermute | solution.py:224
  55.3 3.0 %collective-permute-start.22 = (f32[128,384]{1,0:T(8,128)S(1)}, f32[128,384]{1,0:T(8,128)S(1)}, u32[]{:S(2)}, u32[]{:S(2)}) collective-permute-start(f32[128,384]{1,0:T(8,128)S(1)} %collective-permute-done.11), channel_id=1, source_target_pairs={{0,6},{1,7},{2,4},{3,5},{4,2},{5,3},{6,0},{7,1},{8,14},{9,15},{10,... | collective-permute-start | bytes 589832 | tf_op jit(solution)/shard_map/ppermute | solution.py:189
  58.9 5.8 %level.1 = (f32[1024,384]{1,0:T(8,128)}, f32[1024,128]{1,0:T(8,128)}, f32[128,1024]{1,0:T(8,128)}, f32[8,128]{1,0:T(8,128)}) custom-call(s32[3]{0:T(128)} %pad_add_fusion.info.refs_0_, s32[2,152]{1,0:T(2,128)} %copy-done.8, s32[2,152]{1,0:T(2,128)} %copy-done.8, f32[4,128,384]{2,1,0:T(8,128)} %copy-done.13, f32[4,128,384]{2,1,0:T(8,128)} %collective-permute-done.18.odd, ...), custom_call_target="tpu_custom_call" | custom-call | flops 1000000000 | bytes 1048576 | tf_op jit(solution)/shard_map/level/pallas_call | solution.py:101
  64.7 3.5 %collective-permute-done.22 = f32[128,384]{1,0:T(8,128)S(1)} collective-permute-done((f32[128,384]{1,0:T(8,128)S(1)}, f32[128,384]{1,0:T(8,128)S(1)}, u32[]{:S(2)}, u32[]{:S(2)}) %collective-permute-start.22) | collective-permute-done | bytes 196640 | tf_op jit(solution)/shard_map/ppermute | solution.py:189
  68.3 2.8 %collective-permute-done.21 = f32[128,384]{1,0:T(8,128)S(1)} collective-permute-done((f32[128,384]{1,0:T(8,128)S(1)}, f32[128,384]{1,0:T(8,128)S(1)}, u32[]{:S(2)}, u32[]{:S(2)}) %collective-permute-start.21) | collective-permute-done | bytes 196640 | tf_op jit(solution)/shard_map/ppermute | solution.py:189
  71.9 4.0 %covariance.1 = (f32[128,1024]{1,0:T(8,128)}, f32[8,1024]{1,0:T(8,128)}) custom-call(s32[3]{0:T(128)} %pad_add_fusion.info.refs_0_, s32[2,152]{1,0:T(2,128)} %copy-done.8, f32[8,128,128]{2,1,0:T(8,128)} %copy-done.14, f32[1024,384]{1,0:T(8,128)} %copy-done, f32[1024,128]{1,0:T(8,128)} %get-tuple-element.109.weights.refs_21_, f32[2,128,1024]{2,1,0:T(8,128)} %cov.3, ...), custom_call_target="tpu_custom_call" | custom-call | flops 1000000000 | bytes 1048576 | tf_op jit(solution)/shard_map/covariance/pallas_call | solution.py:101
  76.9 1.8 %later_upper.1 = (f32[1024,384]{1,0:T(8,128)S(1)}, f32[128,1024]{1,0:T(8,128)S(1)}) custom-call(s32[3]{0:T(128)S(1)} %copy-done.11, s32[2,152]{1,0:T(2,128)S(1)} %collective-permute-done.6.ints.ints_v.later_ints.refs_2_.refs_4_, s32[2,152]{1,0:T(2,128)S(1)} %collective-permute-done.6.ints.ints_v.later_ints.refs_2_.refs_4_, ...), custom_call_target="tpu_custom_call" | custom-call | flops 1000000000 | bytes 1048576 | tf_op jit(solution)/shard_map/later_upper/pallas_call | solution.py:101
  80.1 2.6 %collective-permute-start.28 = (f32[128,256]{1,0:T(8,128)S(1)}, f32[128,256]{1,0:T(8,128)S(1)}, u32[]{:S(2)}, u32[]{:S(2)}) collective-permute-start(f32[128,256]{1,0:T(8,128)S(1)} %later_gain.1), channel_id=1, source_target_pairs={{0,6},{1,7},{2,4},{3,5},{4,2},{5,3},{6,0},{7,1},{8,14},{9,15},{10,... | collective-permute-start | bytes 393224 | tf_op jit(solution)/shard_map/ppermute | solution.py:189
  85.8 6.8 %later_level.1 = (f32[1024,384]{1,0:T(8,128)}, f32[1024,128]{1,0:T(8,128)}, f32[1024,128]{1,0:T(8,128)}) custom-call(s32[3]{0:T(128)} %pad_add_fusion.info.refs_0_, s32[2,152]{1,0:T(2,128)} %copy-done.9, f32[4,128,384]{2,1,0:T(8,128)} %collective-permute-done.19.even, f32[4,128,384]{2,1,0:T(8,128)} %copy-done.15, f32[4,136,128]{2,1,0:T(8,128)} %copy-done.18, ...), custom_call_target="tpu_custom_call" | custom-call | flops 1000000000 | bytes 1048576 | tf_op jit(solution)/shard_map/later_level/pallas_call | solution.py:101
  92.8 3.9 %all-to-all-start.1 = ((f32[8,128,128]{2,1,0:T(8,128)}), f32[8,128,128]{2,1,0:T(8,128)S(1)}, u32[]{:S(2)}, u32[]{:S(2)}) async-start(f32[8,128,128]{2,1,0:T(8,128)} %bitcast.34), calls=%async_computation.1 | async-start | bytes 1048576 | tf_op jit(solution)/shard_map/all_to_all | solution.py:220
  96.7 6.9 %ahead.1 = (f32[256,128]{1,0:T(8,128)}, f32[128,1024]{1,0:T(8,128)}, f32[8,128]{1,0:T(8,128)}, f32[8,128]{1,0:T(8,128)}) custom-call(s32[3]{0:T(128)} %pad_add_fusion.info.refs_0_, s32[2,152]{1,0:T(2,128)} %copy-done.8, s32[2,152]{1,0:T(2,128)} %copy-done.9, s32[2,152]{1,0:T(2,128)} %copy-done.9, f32[1024,384]{1,0:T(8,128)} %get-tuple-element.112.first.refs_20_, ...), custom_call_target="tpu_custom_call" | custom-call | flops 1000000000 | bytes 1048576 | tf_op jit(solution)/shard_map/ahead/pallas_call | solution.py:101
  103.6 1.9 %all-to-all-done.1.refs_16_ = f32[8,128,128]{2,1,0:T(8,128)S(1)} async-done(((f32[8,128,128]{2,1,0:T(8,128)}), f32[8,128,128]{2,1,0:T(8,128)S(1)}, u32[]{:S(2)}, u32[]{:S(2)}) %all-to-all-start.1) | async-done | bytes 524320 | tf_op jit(solution)/shard_map/all_to_all | solution.py:220
  106.6 21.9 %finish.1 = (f32[1,128,1024]{2,1,0:T(8,128)}, f32[1,1,128]{2,1,0:T(1,128)}, f32[1,128,1024]{2,1,0:T(8,128)}, f32[1,128,512]{2,1,0:T(8,128)}, f32[1,1,128]{2,1,0:T(1,128)}) custom-call(s32[3]{0:T(128)} %pad_add_fusion.info.refs_0_, s32[2,152]{1,0:T(2,128)} %copy-done.8, s32[2,152]{1,0:T(2,128)} %copy-done.9, s32[2,152]{1,0:T(2,128)} %copy-done.8, ...), custom_call_target="tpu_custom_call" | custom-call | flops 20000000000 | bytes 1048576 | tf_op jit(solution)/shard_map/finish/pallas_call | solution.py:101
  (113 shorter events, 27.5 us)
Async XLA Ops:
  10.5 9.0 %collective-permute-start.5 = (f32[136,128]{1,0:T(8,128)}, f32[136,128]{1,0:T(8,128)S(1)}, u32[]{:S(2)}, u32[]{:S(2)}) collective-permute-start(f32[136,128]{1,0:T(8,128)} %get-tuple-element.81), channel_id=1, source_target_pairs={{0,6},{1,7},{2,4},{3,5},{4,2},{5,3},{6,0},{7,1},{8,14},{9,15},{10,... | collective-permute-start | bytes 208904 | tf_op jit(solution)/shard_map/ppermute | solution.py:189
  20.5 12.4 %collective-permute-start.11 = (f32[128,384]{1,0:T(8,128)S(1)}, f32[128,384]{1,0:T(8,128)S(1)}, u32[]{:S(2)}, u32[]{:S(2)}) collective-permute-start(f32[128,384]{1,0:T(8,128)S(1)} %get-tuple-element.98), channel_id=1, source_target_pairs={{8,0},{16,8},{24,16},{9,1},{17,9},{25,17},{10,2},{18,10},{26,18},{... | collective-permute-start | bytes 589832 | tf_op jit(solution)/shard_map/ppermute | solution.py:224
  21.8 11.1 %collective-permute-start.10 = (f32[128,384]{1,0:T(8,128)S(1)}, f32[128,384]{1,0:T(8,128)S(1)}, u32[]{:S(2)}, u32[]{:S(2)}) collective-permute-start(f32[128,384]{1,0:T(8,128)S(1)} %get-tuple-element.90), channel_id=1, source_target_pairs={{0,6},{1,7},{2,4},{3,5},{4,2},{5,3},{6,0},{7,1},{8,14},{9,15},{10,... | collective-permute-start | bytes 589832 | tf_op jit(solution)/shard_map/ppermute | solution.py:189
  24.1 10.1 %collective-permute-start.9 = (f32[128,384]{1,0:T(8,128)S(1)}, f32[128,384]{1,0:T(8,128)S(1)}, u32[]{:S(2)}, u32[]{:S(2)}) collective-permute-start(f32[128,384]{1,0:T(8,128)S(1)} %get-tuple-element.90), channel_id=1, source_target_pairs={{0,4},{1,5},{2,6},{3,7},{4,0},{5,1},{6,2},{7,3},{8,12},{9,13},{10,... | collective-permute-start | bytes 589832 | tf_op jit(solution)/shard_map/ppermute | solution.py:189
  24.7 9.6 %collective-permute-start.8 = (f32[128,384]{1,0:T(8,128)S(1)}, f32[128,384]{1,0:T(8,128)S(1)}, u32[]{:S(2)}, u32[]{:S(2)}) collective-permute-start(f32[128,384]{1,0:T(8,128)S(1)} %get-tuple-element.90), channel_id=1, source_target_pairs={{0,2},{1,3},{2,0},{3,1},{4,6},{5,7},{6,4},{7,5},{8,10},{9,11},{10,... | collective-permute-start | bytes 589832 | tf_op jit(solution)/shard_map/ppermute | solution.py:189
  25.3 10.7 %collective-permute-start.12 = (f32[4,136,128]{2,1,0:T(8,128)S(1)}, f32[4,136,128]{2,1,0:T(8,128)S(1)}, u32[]{:S(2)}, u32[]{:S(2)}) collective-permute-start(f32[4,136,128]{2,1,0:T(8,128)S(1)} %pad_maximum_fusion.4.even), channel_id=1, source_target_pairs={{8,0},{16,8},{24,16},{9,1},{17,9},{25,17},{10,2},{18,10},{26,18},{... | collective-permute-start | bytes 835592 | tf_op jit(solution)/shard_map/ppermute | solution.py:224
  36.2 13.8 %collective-permute-start.17 = (f32[704,128]{1,0:T(8,128)S(1)}, f32[704,128]{1,0:T(8,128)S(1)}, u32[]{:S(2)}, u32[]{:S(2)}) collective-permute-start(f32[704,128]{1,0:T(8,128)S(1)} %get-tuple-element.96.pack.refs_23_), channel_id=1, source_target_pairs={{8,0},{16,8},{24,16},{9,1},{17,9},{25,17},{10,2},{18,10},{26,18},{... | collective-permute-start | bytes 1081352 | tf_op jit(solution)/shard_map/ppermute | solution.py:224
  37.5 8.7 %collective-permute-start.15 = (f32[128,384]{1,0:T(8,128)S(1)}, f32[128,384]{1,0:T(8,128)S(1)}, u32[]{:S(2)}, u32[]{:S(2)}) collective-permute-start(f32[128,384]{1,0:T(8,128)S(1)} %get-tuple-element.98), channel_id=1, source_target_pairs={{0,6},{1,7},{2,4},{3,5},{4,2},{5,3},{6,0},{7,1},{8,14},{9,15},{10,... | collective-permute-start | bytes 589832 | tf_op jit(solution)/shard_map/ppermute | solution.py:189
  39.9 10.1 %collective-permute-start.14 = (f32[128,384]{1,0:T(8,128)S(1)}, f32[128,384]{1,0:T(8,128)S(1)}, u32[]{:S(2)}, u32[]{:S(2)}) collective-permute-start(f32[128,384]{1,0:T(8,128)S(1)} %get-tuple-element.98), channel_id=1, source_target_pairs={{0,4},{1,5},{2,6},{3,7},{4,0},{5,1},{6,2},{7,3},{8,12},{9,13},{10,... | collective-permute-start | bytes 589832 | tf_op jit(solution)/shard_map/ppermute | solution.py:189
  40.4 9.6 %collective-permute-start.13 = (f32[128,384]{1,0:T(8,128)S(1)}, f32[128,384]{1,0:T(8,128)S(1)}, u32[]{:S(2)}, u32[]{:S(2)}) collective-permute-start(f32[128,384]{1,0:T(8,128)S(1)} %get-tuple-element.98), channel_id=1, source_target_pairs={{0,2},{1,3},{2,0},{3,1},{4,6},{5,7},{6,4},{7,5},{8,10},{9,11},{10,... | collective-permute-start | bytes 589832 | tf_op jit(solution)/shard_map/ppermute | solution.py:189
  50.0 8.9 %collective-permute-start.18 = (f32[4,128,384]{2,1,0:T(8,128)S(1)}, f32[4,128,384]{2,1,0:T(8,128)}, u32[]{:S(2)}, u32[]{:S(2)}) collective-permute-start(f32[4,128,384]{2,1,0:T(8,128)S(1)} %pad_maximum_fusion.1.even), channel_id=1, source_target_pairs={{0,1},{1,0},{2,3},{3,2},{4,5},{5,4},{6,7},{7,6},{8,9},{9,8},{10,11... | collective-permute-start | bytes 2359304 | tf_op jit(solution)/shard_map/ppermute | solution.py:189
  50.1 21.0 %all-to-all-start = ((f32[8,128,128]{2,1,0:T(8,128)}), f32[8,128,128]{2,1,0:T(8,128)S(1)}, u32[]{:S(2)}, u32[]{:S(2)}) async-start(f32[8,128,128]{2,1,0:T(8,128)} %bitcast.17), calls=%async_computation | async-start | bytes 1048576 | tf_op jit(solution)/shard_map/all_to_all | solution.py:220
  53.8 22.6 %collective-permute-start.19 = (f32[4,128,384]{2,1,0:T(8,128)S(1)}, f32[4,128,384]{2,1,0:T(8,128)}, u32[]{:S(2)}, u32[]{:S(2)}) collective-permute-start(f32[4,128,384]{2,1,0:T(8,128)S(1)} %pad_maximum_fusion.even), channel_id=1, source_target_pairs={{8,0},{16,8},{24,16},{9,1},{17,9},{25,17},{10,2},{18,10},{26,18},{... | collective-permute-start | bytes 2359304 | tf_op jit(solution)/shard_map/ppermute | solution.py:224
  55.3 13.0 %collective-permute-start.22 = (f32[128,384]{1,0:T(8,128)S(1)}, f32[128,384]{1,0:T(8,128)S(1)}, u32[]{:S(2)}, u32[]{:S(2)}) collective-permute-start(f32[128,384]{1,0:T(8,128)S(1)} %collective-permute-done.11), channel_id=1, source_target_pairs={{0,6},{1,7},{2,4},{3,5},{4,2},{5,3},{6,0},{7,1},{8,14},{9,15},{10,... | collective-permute-start | bytes 589832 | tf_op jit(solution)/shard_map/ppermute | solution.py:189
  58.3 12.9 %collective-permute-start.21 = (f32[128,384]{1,0:T(8,128)S(1)}, f32[128,384]{1,0:T(8,128)S(1)}, u32[]{:S(2)}, u32[]{:S(2)}) collective-permute-start(f32[128,384]{1,0:T(8,128)S(1)} %collective-permute-done.11), channel_id=1, source_target_pairs={{0,4},{1,5},{2,6},{3,7},{4,0},{5,1},{6,2},{7,3},{8,12},{9,13},{10,... | collective-permute-start | bytes 589832 | tf_op jit(solution)/shard_map/ppermute | solution.py:189
  58.8 12.3 %collective-permute-start.20 = (f32[128,384]{1,0:T(8,128)S(1)}, f32[128,384]{1,0:T(8,128)S(1)}, u32[]{:S(2)}, u32[]{:S(2)}) collective-permute-start(f32[128,384]{1,0:T(8,128)S(1)} %collective-permute-done.11), channel_id=1, source_target_pairs={{0,2},{1,3},{2,0},{3,1},{4,6},{5,7},{6,4},{7,5},{8,10},{9,11},{10,... | collective-permute-start | bytes 589832 | tf_op jit(solution)/shard_map/ppermute | solution.py:189
  76.4 8.5 %collective-permute-start.24 = (f32[4,128,384]{2,1,0:T(8,128)}, f32[4,128,384]{2,1,0:T(8,128)S(1)}, u32[]{:S(2)}, u32[]{:S(2)}) collective-permute-start(f32[4,128,384]{2,1,0:T(8,128)} %collective-permute-done.19.even), channel_id=1, source_target_pairs={{0,1},{1,0},{2,3},{3,2},{4,5},{5,4},{6,7},{7,6},{8,9},{9,8},{10,11... | collective-permute-start | bytes 2359304 | tf_op jit(solution)/shard_map/ppermute | solution.py:189
  76.4 7.2 %collective-permute-start.25 = (f32[4,136,128]{2,1,0:T(8,128)S(1)}, f32[4,136,128]{2,1,0:T(8,128)S(1)}, u32[]{:S(2)}, u32[]{:S(2)}) collective-permute-start(f32[4,136,128]{2,1,0:T(8,128)S(1)} %collective-permute-done.12.gain_even), channel_id=1, source_target_pairs={{0,1},{1,0},{2,3},{3,2},{4,5},{5,4},{6,7},{7,6},{8,9},{9,8},{10,11... | collective-permute-start | bytes 835592 | tf_op jit(solution)/shard_map/ppermute | solution.py:189
  80.1 12.5 %collective-permute-start.28 = (f32[128,256]{1,0:T(8,128)S(1)}, f32[128,256]{1,0:T(8,128)S(1)}, u32[]{:S(2)}, u32[]{:S(2)}) collective-permute-start(f32[128,256]{1,0:T(8,128)S(1)} %later_gain.1), channel_id=1, source_target_pairs={{0,6},{1,7},{2,4},{3,5},{4,2},{5,3},{6,0},{7,1},{8,14},{9,15},{10,... | collective-permute-start | bytes 393224 | tf_op jit(solution)/shard_map/ppermute | solution.py:189
  82.7 10.0 %collective-permute-start.27 = (f32[128,256]{1,0:T(8,128)S(1)}, f32[128,256]{1,0:T(8,128)S(1)}, u32[]{:S(2)}, u32[]{:S(2)}) collective-permute-start(f32[128,256]{1,0:T(8,128)S(1)} %later_gain.1), channel_id=1, source_target_pairs={{0,4},{1,5},{2,6},{3,7},{4,0},{5,1},{6,2},{7,3},{8,12},{9,13},{10,... | collective-permute-start | bytes 393224 | tf_op jit(solution)/shard_map/ppermute | solution.py:189
  83.2 9.4 %collective-permute-start.26 = (f32[128,256]{1,0:T(8,128)S(1)}, f32[128,256]{1,0:T(8,128)S(1)}, u32[]{:S(2)}, u32[]{:S(2)}) collective-permute-start(f32[128,256]{1,0:T(8,128)S(1)} %later_gain.1), channel_id=1, source_target_pairs={{0,2},{1,3},{2,0},{3,1},{4,6},{5,7},{6,4},{7,5},{8,10},{9,11},{10,... | collective-permute-start | bytes 393224 | tf_op jit(solution)/shard_map/ppermute | solution.py:189
  83.6 20.0 %collective-permute-start.30 = (f32[128,1024]{1,0:T(8,128)S(1)}, f32[128,1024]{1,0:T(8,128)S(1)}, u32[]{:S(2)}, u32[]{:S(2)}) collective-permute-start(f32[128,1024]{1,0:T(8,128)S(1)} %copy-done.6), channel_id=1, source_target_pairs={{8,0},{16,8},{24,16},{9,1},{17,9},{25,17},{10,2},{18,10},{26,18},{... | collective-permute-start | bytes 1572872 | tf_op jit(solution)/shard_map/ppermute | solution.py:224
  92.7 12.9 %collective-permute-start.29 = (f32[4,128,256]{2,1,0:T(8,128)S(1)}, f32[4,128,256]{2,1,0:T(8,128)S(1)}, u32[]{:S(2)}, u32[]{:S(2)}) collective-permute-start(f32[4,128,256]{2,1,0:T(8,128)S(1)} %pad_maximum_fusion.3.refs_9_), channel_id=1, source_target_pairs={{0,1},{1,0},{2,3},{3,2},{4,5},{5,4},{6,7},{7,6},{8,9},{9,8},{10,11... | collective-permute-start | bytes 1572872 | tf_op jit(solution)/shard_map/ppermute | solution.py:189
  92.8 12.8 %all-to-all-start.1 = ((f32[8,128,128]{2,1,0:T(8,128)}), f32[8,128,128]{2,1,0:T(8,128)S(1)}, u32[]{:S(2)}, u32[]{:S(2)}) async-start(f32[8,128,128]{2,1,0:T(8,128)} %bitcast.34), calls=%async_computation.1 | async-start | bytes 1048576 | tf_op jit(solution)/shard_map/all_to_all | solution.py:220
  (34 other events, 289.0 us)
